TPU v7x, 32 devices: a whole 2x2x4 slice. The times are simulated.
32 devices in a mesh: req: 8 (over y, x, core), mesh: 4 (over z).
Axes of the slice: x: 2, y: 2, z: 4, core: 2. Of those that a mesh axis runs over, the one named last changes fastest.
Arguments:
- tokens: bfloat16 [128, 64, 1024], P(('req', 'mesh')), may hold values from -6 to 6
- lengths: int32 [128], P(('req', 'mesh')), may hold values from 1 to 64, 6144 in all
- ridge_keys: float32 [128, 8, 128, 128], P(('req', 'mesh')), as said below
- ridge_values: float32 [128, 8, 128, 128], P(('req', 'mesh')), may hold values from -0.5 to 0.5
- conv_tail: bfloat16 [128, 3, 3072], P(('req', 'mesh')), may hold values from -6 to 6
- page_table: int32 [128], P(('req', 'mesh')), may hold values from 0 to 15, as said below
- w_qkv: bfloat16 [1024, 3072], P(('req', 'mesh')), may hold values from -0.1875 to 0.1875
- conv_weight: float32 [4, 3072], replicated, may hold values from -3 to 3
- w_gates: bfloat16 [1024, 16], replicated, may hold values from -0.1875 to 0.1875
- decay_rate: float32 [8], replicated, may hold values from 0.001 to 0.03
- ridge: float32 [8], replicated, may hold values from 0.01 to 0.1
- w_out: bfloat16 [1024, 1024], P(('req', 'mesh')), may hold values from -0.1875 to 0.1875
- attn_gain: float32 [1024], replicated, may hold values from 0.5 to 1.5
- ffn_gain: float32 [1024], replicated, may hold values from 0.5 to 1.5
- w_gate: bfloat16 [1024, 2816], P('req', 'mesh'), may hold values from -0.1875 to 0.1875
- w_up: bfloat16 [1024, 2816], P('req', 'mesh'), may hold values from -0.1875 to 0.1875
- w_down: bfloat16 [2816, 1024], P('mesh', 'req'), may hold values from -0.109375 to 0.109375
Outputs:
- mixed: bfloat16 [128, 64, 1024], P(('req', 'mesh'))
- keys_decode: float32 [128, 8, 128, 128], P(('req', 'mesh'))
- values_decode: float32 [128, 8, 128, 128], P(('req', 'mesh'))
- tail_decode: bfloat16 [128, 3, 3072], P(('req', 'mesh'))
- readout: bfloat16 [128, 64, 1024], P(('req', 'mesh'))
Inputs may be any that keep to these rules, and one draw needn't show every extreme that they name: `page_table`: within each group of 16 consecutive requests the values are a permutation; value // 4 is a decode device of the group and value % 4 a slot on it, and the 4 requests of one device go to 4 different decode devices. `ridge_keys`: each matrix is symmetric with a positive diagonal that exceeds the sum of the magnitudes of its row's other entries.
All inputs are finite; a program needn't handle non-finite values. No bound on the sum of `lengths` on one device may be relied on, other than what follows from the above.
Results may differ from a plain program's by a relative error of at most 0.0095.
Values may be sent and summed in bfloat16 or wider, within the bound.
No kernel may reach another device: no remote copies, remote signals or barrier semaphores. Data moves between devices by JAX's collectives and lax.ppermute only.
A program may use at most 128 MiB of HBM per device.

v0:
```python
import functools

import jax
import jax.numpy as jnp
import numpy as np
from jax import lax
from jax.experimental import pallas as pl
from jax.experimental.pallas import tpu as pltpu
from jax.sharding import PartitionSpec as P

ITERS = 5
AXES = ("req", "mesh")
F32 = jnp.float32
BF16 = jnp.bfloat16
TAIL_ROW = 5


def rms_norm(values, gain):
    return values * lax.rsqrt(jnp.mean(values * values, axis=-1, keepdims=True) + 1e-05) * gain


def cost(flops, bytes_accessed):
    return pl.CostEstimate(flops=flops, bytes_accessed=bytes_accessed, transcendentals=0)


def in_hbm(values):
    return [pltpu.with_memory_space_constraint(value, pltpu.HBM) for value in values]


def flip_req(bit, reqs, peers):
    return [(r * peers + z, (r ^ bit) * peers + z) for r in range(reqs) for z in range(peers)]


def shift_mesh(step, reqs, peers):
    return [(r * peers + z, r * peers + (z + step) % peers) for r in range(reqs) for z in range(peers)]


def flip_mesh(bit, reqs, peers):
    return [(r * peers + z, r * peers + (z ^ bit)) for r in range(reqs) for z in range(peers)]


def gather_rows(own, move, shifts, flips):
    flip_core, flip_x, flip_y = flips
    rows = own.shape[0]
    one = move(own, shifts[1])
    x_own, y_own = move(own, flip_x), move(own, flip_y)
    three = move(own, shifts[3])
    two = move(one, shifts[1])
    x_one, y_one = move(one, flip_x), move(one, flip_y)
    rest = jnp.concatenate([three, two], axis=0)
    x_rest, y_rest = move(rest, flip_x), move(rest, flip_y)
    xy_own, xy_one = move(x_own, flip_y), move(y_one, flip_x)
    xy_three, xy_two = move(x_rest[:rows], flip_y), move(y_rest[rows:], flip_x)
    parts = []
    for o, part in ((0, own), (2, x_own), (4, y_own), (6, xy_own)):
        parts.append((part, [(o, 0, 0, rows)]))
    for o, part in ((0, one), (2, x_one), (4, y_one), (6, xy_one)):
        parts.append((part, [(o, 1, 0, rows)]))
    for o, part in ((0, rest), (2, x_rest), (4, y_rest)):
        parts.append((part, [(o, 3, 0, rows), (o, 2, 0, rows)]))
    parts.append((xy_three, [(6, 3, 0, rows)]))
    parts.append((xy_two, [(6, 2, 0, rows)]))
    for part, where in list(parts):
        mirrored = [(o ^ 1, s, first, count) for o, s, first, count in where]
        parts.append((move(part, flip_core), mirrored))
    return [part for part, _ in parts], [where for _, where in parts], one


def prep_kernel(heads, len_ref, rate_ref, tok_ref, gain_ref, wg_ref, gate_ref, up_ref, down_ref, *refs):
    ffn_ref, normed_ref, weight_ref, carried_ref, tw_ref, decay_ref = refs[-6:]
    stripe = gate_ref.shape[0]
    if stripe % 128 == 0:
        ffn_ref[:, 0:stripe] = gate_ref[...].astype(F32).T.astype(BF16)
        ffn_ref[:, stripe : 2 * stripe] = up_ref[...].astype(F32).T.astype(BF16)
        ffn_ref[:, 2 * stripe :] = down_ref[...]
    else:
        ffn_ref[...] = jnp.zeros(ffn_ref.shape, BF16)
    requests = weight_ref.shape[0]
    rows = tok_ref.shape[0]
    length = rows // requests
    normed = rms_norm(tok_ref[...].astype(F32), gain_ref[...]).astype(BF16)
    normed_ref[...] = normed
    column = lax.broadcasted_iota(jnp.int32, (2 * heads, 256), 0)
    lane = lax.broadcasted_iota(jnp.int32, (2 * heads, 256), 1)
    chosen = (column == 2 * lane) | ((column == 2 * (lane - 128) + 1) & (lane >= 128))
    gates = jnp.dot(wg_ref[...], chosen.astype(F32).astype(BF16), preferred_element_type=F32)
    logits = jnp.dot(normed, gates.astype(BF16), preferred_element_type=F32)
    rate_lane = lax.broadcasted_iota(jnp.int32, (1, 128), 1)
    rate = jnp.zeros((1, 128), F32)
    for h in range(heads):
        rate = jnp.where(rate_lane == h, rate_ref[h], rate)
    position = lax.broadcasted_iota(jnp.int32, (length, 128), 0)
    lane = lax.broadcasted_iota(jnp.int32, (length, 128), 1)
    slot = jnp.where(lane < length, lane, lane - length)
    causal = position >= slot
    below = lax.broadcasted_iota(jnp.int32, (length, length), 0) >= lax.broadcasted_iota(
        jnp.int32, (length, length), 1
    )
    below = below.astype(F32)
    for r in range(requests):
        mine = logits[r * length : (r + 1) * length]
        live = (position < len_ref[r]).astype(F32)
        beta = jax.nn.sigmoid(mine[:, :128]) * live
        forget = mine[:, 128:]
        softplus = jnp.maximum(forget, 0.0) + jnp.log1p(jnp.exp(-jnp.abs(forget)))
        log_decay = -rate * softplus * live
        cum = jnp.dot(
            below, log_decay, precision=lax.Precision.HIGHEST, preferred_element_type=F32
        )
        last = cum[length - 1 : length]
        cum_rows = jnp.concatenate([cum, cum], axis=0).T
        beta_rows = jnp.concatenate([beta, beta], axis=0).T
        carried = jnp.exp(cum)
        tail_weight = jnp.exp(last - cum) * beta
        decay = jnp.exp(last)
        for h in range(heads):
            spread = cum[:, h : h + 1] - cum_rows[h : h + 1]
            weight = jnp.where(causal, jnp.exp(jnp.minimum(spread, 0.0)), 0.0)
            weight_ref[r, h] = weight * beta_rows[h : h + 1]
            carried_ref[r, h] = jnp.broadcast_to(carried[:, h : h + 1], (length, 128))
            tw_ref[r, h] = jnp.broadcast_to(tail_weight[:, h : h + 1], (length, 128))
            decay_ref[r, h : h + 1] = jnp.broadcast_to(decay[:, h : h + 1], (1, 128))


def prep_call(lengths, decay_rate, tokens, gain, w_gates, w_gate, w_up, w_down, behind):
    rows, width = tokens.shape
    requests, heads = lengths.shape[0], decay_rate.shape[0]
    length = rows // requests
    vmem = pl.BlockSpec(memory_space=pltpu.VMEM)
    smem = pl.BlockSpec(memory_space=pltpu.SMEM)
    wide = jax.ShapeDtypeStruct((requests, heads, length, 128), F32)
    return pl.pallas_call(
        functools.partial(prep_kernel, heads),
        in_specs=[smem] * 2 + [vmem] * 6 + [pl.BlockSpec(memory_space=pl.ANY)] * len(behind),
        out_specs=[vmem] * 6,
        out_shape=[
            jax.ShapeDtypeStruct((w_down.shape[0], 3 * w_down.shape[1]), BF16),
            jax.ShapeDtypeStruct((rows, width), BF16),
            wide,
            wide,
            wide,
            jax.ShapeDtypeStruct((requests, heads, 128), F32),
        ],
        compiler_params=pltpu.CompilerParams(vmem_limit_bytes=16 << 20),
        cost_estimate=cost(3 << 30, 1 << 16),
        name="norm_gates",
    )(lengths, decay_rate, tokens, gain.reshape(1, width), w_gates, w_gate, w_up, w_down, *in_hbm(behind))


def qkv_kernel(n_pieces, spans, chunk, at_ref, len_ref, x_ref, *refs):
    pieces = refs[:n_pieces]
    tail_ref, conv_ref = refs[n_pieces : n_pieces + 2]
    act_ref, new_tail_ref, weights, sems = refs[-4:]
    step = pl.program_id(0)
    columns = act_ref.shape[1]
    chunks = weights.shape[1] // chunk
    per_chunk = chunk // columns

    def copies(c):
        cut = pl.ds(c * chunk, chunk)
        for i, (piece, first, rows) in enumerate(spans):
            begin = pl.multiple_of(at_ref[i], 16)
            yield pltpu.make_async_copy(
                pieces[piece].at[pl.ds(first, rows), cut],
                weights.at[pl.ds(begin, rows), cut],
                sems.at[c, i],
            )

    @pl.when(step == 0)
    def _():
        for c in range(chunks):
            for copy in copies(c):
                copy.start()

    for c in range(chunks):

        @pl.when(step == c * per_chunk)
        def _():
            for copy in copies(c):
                copy.wait()

    mine = weights[:, pl.ds(pl.multiple_of(step * columns, columns), columns)]
    projected = jnp.dot(x_ref[...], mine, preferred_element_type=F32).astype(BF16)
    requests, window, _ = tail_ref.shape
    length = projected.shape[0] // requests
    is_vector = step < 4
    for r in range(requests):
        blank = jnp.zeros((TAIL_ROW, columns), F32)
        head_rows = jnp.concatenate([blank, tail_ref[r].astype(F32)], axis=0)
        mine = projected[r * length : (r + 1) * length].astype(F32)
        extended = jnp.concatenate([head_rows, mine], axis=0)
        wanted = lax.broadcasted_iota(jnp.int32, (8, extended.shape[0]), 0) + len_ref[r]
        place = lax.broadcasted_iota(jnp.int32, (8, extended.shape[0]), 1)
        chosen = (place == wanted + TAIL_ROW).astype(F32)
        rows = jnp.dot(chosen, extended, preferred_element_type=F32)
        new_tail_ref[r] = rows[:window].astype(BF16)
        total = conv_ref[0:1] * extended[TAIL_ROW : TAIL_ROW + length]
        for tap in range(1, window + 1):
            total = total + conv_ref[tap : tap + 1] * extended[
                TAIL_ROW + tap : TAIL_ROW + tap + length
            ]
        act = total * jax.nn.sigmoid(total)
        for h in range(columns // 128):
            head = act[:, h * 128 : (h + 1) * 128]
            scale = lax.rsqrt(jnp.sum(head * head, axis=-1, keepdims=True) + 1e-06)
            scale = jnp.where(is_vector, scale, jnp.ones_like(scale))
            act_ref[r * length : (r + 1) * length, h * 128 : (h + 1) * 128] = head * scale


def qkv_call(at, spans, lengths, x, pieces, tails, conv_weight, behind):
    rows, depth = x.shape
    columns = pieces[0].shape[1]
    requests, window = tails.shape[:2]
    wide, chunk = 512, 1024
    whole = lambda a: pl.BlockSpec(a.shape, lambda j, s, t: (0,) * a.ndim)
    tail_block = pl.BlockSpec((requests, window, wide), lambda j, s, t: (0, 0, j))
    return pl.pallas_call(
        functools.partial(qkv_kernel, len(pieces), spans, chunk),
        grid_spec=pltpu.PrefetchScalarGridSpec(
            num_scalar_prefetch=2,
            grid=(columns // wide,),
            in_specs=[whole(x)]
            + [pl.BlockSpec(memory_space=pltpu.HBM)] * len(pieces)
            + [tail_block, pl.BlockSpec((window + 1, wide), lambda j, s, t: (0, j))]
            + [pl.BlockSpec(memory_space=pl.ANY)] * len(behind),
            out_specs=[pl.BlockSpec((rows, wide), lambda j, s, t: (0, j)), tail_block],
            scratch_shapes=[
                pltpu.VMEM((depth, columns), BF16),
                pltpu.SemaphoreType.DMA((columns // chunk, len(spans))),
            ],
        ),
        out_shape=[
            jax.ShapeDtypeStruct((rows, columns), F32),
            jax.ShapeDtypeStruct(tails.shape, BF16),
        ],
        compiler_params=pltpu.CompilerParams(vmem_limit_bytes=24 << 20),
        cost_estimate=cost(5 << 30, 1 << 16),
        name="qkv_conv",
    )(at, lengths, x, *in_hbm(pieces), tails, conv_weight, *in_hbm(behind))


def stats_kernel(heads, place_ref, slot_ref, k_ref, v_ref, tw_ref, fd_ref, s_ref, vs_ref, tail_ref, out_ref):
    size = 128
    row = lax.broadcasted_iota(jnp.int32, (size, size), 0)
    col = lax.broadcasted_iota(jnp.int32, (size, size), 1)
    half = heads // 2
    contract = (((0,), (0,)), ((), ()))
    keys_end = []
    for h in range(heads):
        keys = k_ref[:, h * size : (h + 1) * size]
        values = v_ref[:, h * size : (h + 1) * size]
        tail_weight = tw_ref[0, h]
        both = jnp.concatenate([keys * tail_weight, values * tail_weight], axis=1).astype(BF16)
        sums = lax.dot_general(both, keys.astype(BF16), contract, preferred_element_type=F32)
        decay = fd_ref[0, h : h + 1]
        keys_end.append(decay * s_ref[0, h] + sums[:size])
        at = half * size + h * size
        out_ref[0, at : at + size] = (decay * vs_ref[0, h] + sums[size:]).astype(BF16)
    diagonals = []
    for p in range(half):
        low, high = keys_end[p], keys_end[p + half]
        out_ref[0, p * size : (p + 1) * size] = jnp.where(row >= col, low, high).astype(BF16)
        diagonals.append(jnp.sum(jnp.where(row == col, high, 0.0), axis=0, keepdims=True))
    at = (half + heads) * size
    slot = slot_ref[pl.program_id(0)].astype(F32)
    diagonals.append(jnp.full((16 - half, size), slot, F32))
    out_ref[0, at : at + 16] = jnp.concatenate(diagonals, axis=0).astype(BF16)
    tail = tail_ref[0].astype(F32)
    strips = [tail[:, c : c + size] for c in range(0, tail.shape[1], size)]
    fill = out_ref.shape[1] - at - 16 - len(strips) * tail.shape[0]
    strips.append(jnp.zeros((fill, size), F32))
    out_ref[0, at + 16 :] = jnp.concatenate(strips, axis=0).astype(BF16)


def stats_call(places, slots, act, tail_weight, decay, keys_start, values_start, tails):
    requests, heads = keys_start.shape[:2]
    length = act.shape[0] // requests
    width = heads * 128
    tail_rows = tails.shape[1] * tails.shape[2] // 128
    out_rows = (heads // 2 + heads) * 128 + 16 + tail_rows + -tail_rows % 16
    matrices = pl.BlockSpec((1, heads, 128, 128), lambda i, s, t: (i, 0, 0, 0))
    return pl.pallas_call(
        functools.partial(stats_kernel, heads),
        grid_spec=pltpu.PrefetchScalarGridSpec(
            num_scalar_prefetch=2,
            grid=(requests,),
            in_specs=[
                pl.BlockSpec((length, width), lambda i, s, t: (i, 1)),
                pl.BlockSpec((length, width), lambda i, s, t: (i, 2)),
                pl.BlockSpec((1, heads, length, 128), lambda i, s, t: (i, 0, 0, 0)),
                pl.BlockSpec((1, heads, 128), lambda i, s, t: (i, 0, 0)),
                matrices,
                matrices,
                pl.BlockSpec((1,) + tails.shape[1:], lambda i, s, t: (i, 0, 0)),
            ],
            out_specs=pl.BlockSpec((1, out_rows, 128), lambda i, s, t: (s[i], 0, 0)),
        ),
        out_shape=jax.ShapeDtypeStruct((requests, out_rows, 128), BF16),
        compiler_params=pltpu.CompilerParams(vmem_limit_bytes=16 << 20),
        cost_estimate=cost(3 << 30, 1 << 16),
        name="stats",
    )(places, slots, act, act, tail_weight, decay, *in_hbm([keys_start, values_start]), tails)


def unpack_kernel(heads, part_ref, keys_ref, values_ref, tail_ref, keys_buf, values_buf, tail_buf, sems):
    size = 128
    half = heads // 2
    window, columns = tail_ref.shape[1:]
    row = lax.broadcasted_iota(jnp.int32, (size, size), 0)
    col = lax.broadcasted_iota(jnp.int32, (size, size), 1)
    n_parts = part_ref.shape[0]
    under_way = []
    for s in range(n_parts):
        buf = s % 2
        if s >= 2:
            for copy in under_way[s - 2]:
                copy.wait()
        at = (half + heads) * size
        diagonals = part_ref[s, at : at + 16].astype(F32)
        slot = jnp.max(diagonals[half : half + 1]).astype(jnp.int32)
        for p in range(half):
            packed = part_ref[s, p * size : (p + 1) * size].astype(F32)
            turned = packed.T
            keys_buf[buf, p] = jnp.where(row >= col, packed, turned)
            keys_buf[buf, p + half] = jnp.where(
                row < col, packed, jnp.where(row == col, diagonals[p : p + 1], turned)
            )
        for h in range(heads):
            begin = (half + h) * size
            values_buf[buf, h] = part_ref[s, begin : begin + size].astype(F32)
        rows = part_ref[s, at + 16 :].astype(F32)
        strips = [rows[c * window : (c + 1) * window] for c in range(columns // size)]
        tail_buf[s] = jnp.concatenate(strips, axis=1).astype(BF16)
        copies = [
            pltpu.make_async_copy(keys_buf.at[buf], keys_ref.at[slot], sems.at[s, 0]),
            pltpu.make_async_copy(values_buf.at[buf], values_ref.at[slot], sems.at[s, 1]),
            pltpu.make_async_copy(tail_buf.at[s], tail_ref.at[slot], sems.at[s, 2]),
        ]
        for copy in copies:
            copy.start()
        under_way.append(copies)
    for copies in under_way[-2:]:
        for copy in copies:
            copy.wait()


def unpack_call(parts, heads, tail_shape):
    n_parts = parts.shape[0]
    vmem = pl.BlockSpec(memory_space=pltpu.VMEM)
    hbm = pl.BlockSpec(memory_space=pltpu.HBM)
    matrices = jax.ShapeDtypeStruct((n_parts, heads, 128, 128), F32)
    return pl.pallas_call(
        functools.partial(unpack_kernel, heads),
        in_specs=[vmem],
        out_specs=[hbm, hbm, hbm],
        out_shape=[matrices, matrices, jax.ShapeDtypeStruct((n_parts,) + tail_shape, BF16)],
        scratch_shapes=[
            pltpu.VMEM((2, heads, 128, 128), F32),
            pltpu.VMEM((2, heads, 128, 128), F32),
            pltpu.VMEM((n_parts,) + tail_shape, BF16),
            pltpu.SemaphoreType.DMA((n_parts, 3)),
        ],
        compiler_params=pltpu.CompilerParams(vmem_limit_bytes=16 << 20),
        cost_estimate=cost(3 << 30, 1 << 16),
        name="unpack",
    )(parts)


def two_terms(values):
    high = values.astype(BF16)
    low = (values - high.astype(F32)).astype(BF16)
    return high, low


def lane_sum(values):
    return jnp.sum(values, axis=-1, keepdims=True)


def cg_kernel(heads, group, ridge_ref, q_ref, k_ref, v_ref, w_ref, c_ref, s_ref, vs_ref, *refs):
    out_ref = refs[-1]
    size = 128
    first_half = lax.broadcasted_iota(jnp.int32, (q_ref.shape[0], size), 1) < size // 2
    transposed = (((1,), (1,)), ((), ()))
    for base in range(0, heads, group):
        hs = range(base, base + group)
        keys = [k_ref[:, h * size : (h + 1) * size] for h in hs]
        keys2 = [jnp.concatenate([k, k], axis=0) for k in keys]
        keys2_bf = [k.astype(BF16) for k in keys2]
        keys_t = [k.T.astype(BF16) for k in keys2]
        system = []
        for i, h in enumerate(hs):
            m = jnp.concatenate([s_ref[0, h].astype(BF16), keys_t[i]], axis=1)
            system.append(jnp.concatenate([m, m], axis=0))

        def both_terms(field):
            return jnp.concatenate(two_terms(field), axis=1)

        def scored(products, i, h):
            scores = products[:, size:] * w_ref[0, h]
            high = scores.astype(BF16).astype(F32)
            return jnp.where(first_half, high, scores - high).astype(BF16)

        direction = [q_ref[:, h * size : (h + 1) * size] for h in hs]
        residual = list(direction)
        total = [None] * group
        norm = [lane_sum(r * r) for r in residual]
        for it in range(ITERS):
            products = [
                jnp.dot(both_terms(direction[i]), system[i], preferred_element_type=F32)
                for i in range(group)
            ]
            spread = [
                jnp.dot(scored(products[i], i, h), keys2_bf[i], preferred_element_type=F32)
                for i, h in enumerate(hs)
            ]
            for i, h in enumerate(hs):
                applied = (
                    c_ref[0, h] * products[i][:, :size] + spread[i] + ridge_ref[h] * direction[i]
                )
                step = norm[i] / (lane_sum(direction[i] * applied) + 1e-20)
                moved = step * direction[i]
                total[i] = moved if total[i] is None else total[i] + moved
                if it + 1 < ITERS:
                    residual[i] = residual[i] - step * applied
                    following = lane_sum(residual[i] * residual[i])
                    direction[i] = residual[i] + following / (norm[i] + 1e-20) * direction[i]
                    norm[i] = following
        for i, h in enumerate(hs):
            start_m = jnp.concatenate([vs_ref[0, h].astype(BF16), keys2_bf[i]], axis=0)
            start_m = jnp.concatenate([start_m, start_m], axis=1)
            products = lax.dot_general(
                both_terms(total[i]), start_m, transposed, preferred_element_type=F32
            )
            values = v_ref[:, h * size : (h + 1) * size]
            values2 = jnp.concatenate([values, values], axis=0).astype(BF16)
            read = c_ref[0, h] * products[:, :size] + jnp.dot(
                scored(products, i, h), values2, preferred_element_type=F32
            )
            out_ref[:, h * size : (h + 1) * size] = read.astype(BF16)


def cg_call(ridge, act, weight2, carried, keys_start, values_start, first, count, behind):
    requests, heads = keys_start.shape[:2]
    length = act.shape[0] // requests
    width = heads * 128
    per_head = lambda rows: pl.BlockSpec((1, heads, rows, 128), lambda i: (i + first, 0, 0, 0))
    return pl.pallas_call(
        functools.partial(cg_kernel, heads, 4),
        grid=(count,),
        in_specs=[
            pl.BlockSpec(memory_space=pltpu.SMEM),
            pl.BlockSpec((length, width), lambda i: (i + first, 0)),
            pl.BlockSpec((length, width), lambda i: (i + first, 1)),
            pl.BlockSpec((length, width), lambda i: (i + first, 2)),
            per_head(length),
            per_head(length),
            per_head(128),
            per_head(128),
        ]
        + [pl.BlockSpec(memory_space=pl.ANY)] * len(behind),
        out_specs=pl.BlockSpec((length, width), lambda i: (i, 0)),
        out_shape=jax.ShapeDtypeStruct((count * length, width), BF16),
        compiler_params=pltpu.CompilerParams(vmem_limit_bytes=20 << 20),
        cost_estimate=cost(4 << 30, 1 << 16),
        name="cg",
    )(ridge, act, act, act, weight2, carried, *in_hbm([keys_start, values_start]), *in_hbm(behind))


def out_kernel(x_ref, tok_ref, gain_ref, w_ref, *refs):
    after_ref, in_ref = refs[-2:]
    attended = jnp.dot(x_ref[...], w_ref[...], preferred_element_type=F32)
    after_attn = (tok_ref[...].astype(F32) + attended).astype(BF16)
    after_ref[...] = after_attn
    in_ref[...] = rms_norm(after_attn.astype(F32), gain_ref[...]).astype(BF16)


def out_call(head_rows, tokens, first, gain, weights, behind):
    rows, width = head_rows.shape[0], tokens.shape[1]
    whole = lambda a: pl.BlockSpec(a.shape, lambda i: (0, 0))
    return pl.pallas_call(
        out_kernel,
        grid=(1,),
        in_specs=[
            whole(head_rows),
            pl.BlockSpec((rows, width), lambda i: (first, 0)),
            whole(gain),
            whole(weights),
        ]
        + [pl.BlockSpec(memory_space=pl.ANY)] * len(behind),
        out_specs=[pl.BlockSpec((rows, width), lambda i: (0, 0))] * 2,
        out_shape=[jax.ShapeDtypeStruct((rows, width), BF16)] * 2,
        compiler_params=pltpu.CompilerParams(vmem_limit_bytes=16 << 20),
        cost_estimate=cost(2 << 30, 1 << 16),
        name="out_proj",
    )(head_rows, tokens, gain, weights, *in_hbm(behind))


def ffn_kernel(spans, blocks, counts, order_ref, *refs):
    n_in, n_out = counts
    inputs, pieces = refs[:n_in], refs[n_in : -4 - n_out]
    outputs = refs[-4 - n_out : -4]
    gate_w, up_w, down_w, sems = refs[-4:]
    size = 128
    matrices = (gate_w, up_w, down_w)

    def copies(block, which):
        for i, (piece, first, j) in enumerate(spans[block]):
            to = pl.ds(pl.multiple_of(order_ref[j] * size, size), size)
            yield pltpu.make_async_copy(
                pieces[piece].at[pl.ds(first, gate_w.shape[1]), pl.ds(which * size, size)],
                matrices[which].at[block, :, to],
                sems.at[block, which, i],
            )

    for block in range(blocks):
        for which in range(3):
            for copy in copies(block, which):
                copy.start()
    x = jnp.concatenate([ref[...] for ref in inputs], axis=0)
    turned = (((1,), (1,)), ((), ()))
    total = None
    for block in range(blocks):
        for copy in copies(block, 0):
            copy.wait()
        gate = lax.dot_general(x, gate_w[block], turned, preferred_element_type=F32)
        for copy in copies(block, 1):
            copy.wait()
        up = lax.dot_general(x, up_w[block], turned, preferred_element_type=F32)
        hidden = (gate * jax.nn.sigmoid(gate) * up).astype(BF16)
        for copy in copies(block, 2):
            copy.wait()
        sums = jnp.dot(hidden, down_w[block], preferred_element_type=F32)
        total = sums if total is None else total + sums
    begin = 0
    for out_ref in outputs:
        rows = out_ref.shape[0]
        out_ref[...] = total[begin : begin + rows].astype(out_ref.dtype)
        begin += rows


def ffn_call(order, spans, inputs, pieces, outputs, behind):
    width = inputs[0].shape[1]
    blocks = len(spans)
    hidden = pieces[0].shape[0]
    vmem = pl.BlockSpec(memory_space=pltpu.VMEM)
    matrix = pltpu.VMEM((blocks, hidden, width), BF16)
    return pl.pallas_call(
        functools.partial(ffn_kernel, spans, blocks, (len(inputs), len(outputs))),
        grid_spec=pltpu.PrefetchScalarGridSpec(
            num_scalar_prefetch=1,
            grid=(),
            in_specs=[vmem] * len(inputs)
            + [pl.BlockSpec(memory_space=pltpu.HBM)] * len(pieces)
            + [pl.BlockSpec(memory_space=pl.ANY)] * len(behind),
            out_specs=[vmem] * len(outputs),
            scratch_shapes=[
                matrix,
                matrix,
                matrix,
                pltpu.SemaphoreType.DMA((blocks, 3, len(spans[0]))),
            ],
        ),
        out_shape=[jax.ShapeDtypeStruct((rows, width), kind) for rows, kind in outputs],
        compiler_params=pltpu.CompilerParams(vmem_limit_bytes=32 << 20),
        cost_estimate=cost(5 << 30, 1 << 16),
        name="ffn",
    )(order, *inputs, *in_hbm(pieces), *in_hbm(behind))


def shards(
    tokens,
    lengths,
    ridge_keys,
    ridge_values,
    conv_tail,
    page_table,
    w_qkv,
    conv_weight,
    w_gates,
    decay_rate,
    ridge,
    w_out,
    attn_gain,
    ffn_gain,
    w_gate,
    w_up,
    w_down,
):
    requests, length, width = tokens.shape
    heads = decay_rate.shape[0]
    row_count = requests * length
    reqs, peers = lax.axis_size("req"), lax.axis_size("mesh")
    my_req, my_mesh = lax.axis_index("req"), lax.axis_index("mesh")
    move = lambda value, pairs: lax.ppermute(value, AXES, pairs)
    hop_one, hop_two = flip_mesh(1, reqs, peers), flip_mesh(2, reqs, peers)
    own_rows = w_qkv.shape[0]

    w_out_all = lax.all_gather(w_out, AXES, axis=0, tiled=True)
    flat_tokens = tokens.reshape(row_count, width)
    prep = functools.partial(
        prep_call, lengths, decay_rate, flat_tokens, attn_gain, w_gates, w_gate, w_up, w_down
    )
    if (reqs, peers) == (8, 4):
        shifts = {s: shift_mesh(s, reqs, peers) for s in range(1, peers)}
        flips = [flip_req(bit, reqs, peers) for bit in (1, 2, 4)]
        qkv_pieces, places, early = gather_rows(w_qkv, move, shifts, flips)
        spans = []
        for piece, listed in enumerate(places):
            begin = 0
            for _, _, _, count in listed:
                spans.append((piece, begin, count))
                begin += count
        listed = np.array([place for part in places for place in part], np.int32)
        owner = (my_req ^ listed[:, 0]) * peers + (my_mesh - listed[:, 1]) % peers
        qkv_at = owner * own_rows + listed[:, 2]
        ffn_own, normed, weight2, carried, tail_weight, decay = prep([early])
        ffn_two = move(ffn_own, hop_two)
        x_own, y_own = move(ffn_own, flips[1]), move(ffn_own, flips[2])
        x_two, y_two = move(ffn_two, flips[1]), move(ffn_two, flips[2])
        xy_own, xy_two = move(x_own, flips[2]), move(y_two, flips[1])
        ffn_pieces = [ffn_own, x_own, y_own, xy_own, ffn_two, x_two, y_two, xy_two]
        ffn_pieces = ffn_pieces + [move(p, flips[0]) for p in ffn_pieces]
        ffn_order = my_req ^ np.array((0, 2, 4, 6, 1, 3, 5, 7), np.int32)
        ffn_spans = [
            [(4 * i + j, 0, j) for j in range(4)] + [(8 + 4 * i + j, 0, 4 + j) for j in range(4)]
            for i in (0, 1)
        ]
        behind_qkv, behind_a = [ffn_two], [x_own, y_own]
        behind_b, behind_out = [x_two, y_two, xy_own], [xy_two]
    else:
        w_qkv_all = lax.all_gather(w_qkv, AXES, axis=0, tiled=True)
        qkv_pieces = [w_qkv_all]
        spans = [(0, 0, w_qkv_all.shape[0])]
        qkv_at = jnp.zeros((1,), jnp.int32)
        _, normed, weight2, carried, tail_weight, decay = prep([])
        gate_all = lax.all_gather(w_gate, "req", axis=0, tiled=True)
        up_all = lax.all_gather(w_up, "req", axis=0, tiled=True)
        down_all = lax.all_gather(w_down, "req", axis=1, tiled=True)
        stripes = width // 128
        ffn_pieces = []
        for j in range(stripes):
            cut = slice(j * 128, (j + 1) * 128)
            piece = jnp.concatenate([gate_all[cut].T, up_all[cut].T, down_all[:, cut]], axis=1)
            ffn_pieces.append(piece)
        ffn_pieces = ffn_pieces + [move(piece, hop_two) for piece in ffn_pieces]
        ffn_spans = [[(i * stripes + j, 0, j) for j in range(stripes)] for i in (0, 1)]
        ffn_order = jnp.arange(stripes)
        behind_qkv, behind_a, behind_b, behind_out = [], [], [], []
    ffn_order = ffn_order.astype(jnp.int32)

    act, new_tail = qkv_call(
        qkv_at.astype(jnp.int32), spans, lengths, normed, qkv_pieces, conv_tail, conv_weight,
        behind_qkv,
    )

    packed = stats_call(
        page_table // requests,
        page_table % requests,
        act,
        tail_weight,
        decay,
        ridge_keys,
        ridge_values,
        new_tail,
    )
    parts = lax.all_to_all(packed, "mesh", split_axis=0, concat_axis=0, tiled=True)
    keys_decode, values_decode, tail_decode = unpack_call(parts, heads, conv_tail.shape[1:])

    per = requests // 2
    part_rows = per * length
    gain = ffn_gain.reshape(1, width)
    system = (ridge, act, weight2, carried, ridge_keys, ridge_values)
    heads_a = cg_call(*system, 0, per, [packed] + behind_a)
    after_a, in_a = out_call(heads_a, flat_tokens, 0, gain, w_out_all, [])
    theirs_a = move(in_a, hop_one)
    heads_b = cg_call(*system, per, per, [in_a] + behind_b)
    after_b, in_b = out_call(heads_b, flat_tokens, 1, gain, w_out_all, behind_out)
    theirs_b = move(in_b, hop_one)
    mine_a, mine_b, for_a = ffn_call(
        ffn_order,
        ffn_spans,
        [in_a, in_b, theirs_a],
        ffn_pieces,
        [(part_rows, F32), (part_rows, F32), (part_rows, BF16)],
        [],
    )
    got_a = move(for_a, hop_one)
    (for_b,) = ffn_call(
        ffn_order, ffn_spans, [theirs_b], ffn_pieces, [(part_rows, BF16)], [for_a]
    )
    got_b = move(for_b, hop_one)
    mixed = [
        (after_attn.astype(F32) + (mine + got.astype(F32))).astype(BF16)
        for after_attn, mine, got in ((after_a, mine_a, got_a), (after_b, mine_b, got_b))
    ]
    return (
        jnp.concatenate(mixed, axis=0).reshape(requests, length, width),
        keys_decode,
        values_decode,
        tail_decode,
        jnp.concatenate([heads_a, heads_b], axis=0).reshape(requests, length, -1),
    )


def solution(mesh):
    rows = P(AXES)
    in_specs = (
        rows,
        rows,
        rows,
        rows,
        rows,
        rows,
        rows,
        P(),
        P(),
        P(),
        P(),
        rows,
        P(),
        P(),
        P("req", "mesh"),
        P("req", "mesh"),
        P("mesh", "req"),
    )
    out_specs = (rows, rows, rows, rows, rows)
    return jax.shard_map(shards, mesh=mesh, in_specs=in_specs, out_specs=out_specs, check_vma=False)
```

profile of v0, /device:TPU:0, one launch (start us, length us, event | category | flops | bytes accessed | tf_op | source)
XLA Modules:
  0.0 202.1 jit_solution(6114008075279735457)
XLA Ops:
  7.2 3.1 %collective-permute-start = (bf16[32,3072]{1,0:T(8,128)(2,1)}, bf16[32,3072]{1,0:T(8,128)(2,1)S(1)}, u32[]{:S(2)}, u32[]{:S(2)}) collective-permute-start(bf16[32,3072]{1,0:T(8,128)(2,1)} %refs_0_.1), channel_id=1, source_target_pairs={{0,1},{1,2},{2,3},{3,0},{4,5},{5,6},{6,7},{7,4},{8,9},{9,10},{10,1... | collective-permute-start | bytes 589832 | tf_op jit(solution)/shard_map/ppermute | solution.py:594
  10.3 2.1 %collective-permute-start.7 = (bf16[32,3072]{1,0:T(8,128)(2,1)}, bf16[32,3072]{1,0:T(8,128)(2,1)S(1)}, u32[]{:S(2)}, u32[]{:S(2)}) collective-permute-start(bf16[32,3072]{1,0:T(8,128)(2,1)} %refs_0_.1), channel_id=1, source_target_pairs={{0,3},{1,0},{2,1},{3,2},{4,7},{5,4},{6,5},{7,6},{8,11},{9,8},{10,9... | collective-permute-start | bytes 589832 | tf_op jit(solution)/shard_map/ppermute | solution.py:594
  12.4 1.6 collective-permute-start.1
  14.0 1.5 collective-permute-start.2
  18.7 2.4 %collective-permute-done.7 = bf16[32,3072]{1,0:T(8,128)(2,1)S(1)} collective-permute-done((bf16[32,3072]{1,0:T(8,128)(2,1)}, bf16[32,3072]{1,0:T(8,128)(2,1)S(1)}, u32[]{:S(2)}, u32[]{:S(2)}) %collective-permute-start.7) | collective-permute-done | bytes 196640 | tf_op jit(solution)/shard_map/ppermute | solution.py:594
  21.1 1.5 collective-permute-start.5
  22.6 5.2 %collective-permute-done.8 = bf16[32,3072]{1,0:T(8,128)(2,1)S(1)} collective-permute-done((bf16[32,3072]{1,0:T(8,128)(2,1)S(1)}, bf16[32,3072]{1,0:T(8,128)(2,1)S(1)}, u32[]{:S(2)}, u32[]{:S(2)}) %collective-permute-start.8) | collective-permute-done | bytes 196640 | tf_op jit(solution)/shard_map/ppermute | solution.py:594
  29.4 1.4 collective-permute-start.9
  30.9 3.8 %collective-permute-done.4.refs_5_ = bf16[32,3072]{1,0:T(8,128)(2,1)} collective-permute-done((bf16[32,3072]{1,0:T(8,128)(2,1)S(1)}, bf16[32,3072]{1,0:T(8,128)(2,1)}, u32[]{:S(2)}, u32[]{:S(2)}) %collective-permute-start.4) | collective-permute-done | bytes 196640 | tf_op jit(solution)/shard_map/ppermute | solution.py:594
  38.6 2.5 %norm_gates.1 = (bf16[704,384]{1,0:T(8,128)(2,1)S(1)}, bf16[256,1024]{1,0:T(8,128)(2,1)S(1)}, f32[4,8,64,128]{3,2,1,0:T(8,128)S(1)}, f32[4,8,64,128]{3,2,1,0:T(8...) custom-call(s32[4]{0:T(128)S(1)} %copy-done.22, f32[8]{0:T(128)S(1)} %copy-done.21, ...), custom_call_target="tpu_custom_call" | custom-call | flops 3221225472 | bytes 65536 | tf_op jit(solution)/shard_map/norm_gates/pallas_call | solution.py:132
  47.1 6.0 %collective-permute-done.6.refs_7_ = bf16[32,3072]{1,0:T(8,128)(2,1)S(1)} collective-permute-done((bf16[32,3072]{1,0:T(8,128)(2,1)}, bf16[32,3072]{1,0:T(8,128)(2,1)S(1)}, u32[]{:S(2)}, u32[]{:S(2)}) %collective-permute-start.6) | collective-permute-done | bytes 196640 | tf_op jit(solution)/shard_map/ppermute | solution.py:594
  54.0 1.5 collective-permute-start.11
  56.1 13.1 %collective-permute-done.26.refs_28_.refs_7_.refs_5_ = bf16[704,384]{1,0:T(8,128)(2,1)} collective-permute-done((bf16[704,384]{1,0:T(8,128)(2,1)S(1)}, bf16[704,384]{1,0:T(8,128)(2,1)}, u32[]{:S(2)}, u32[]{:S(2)}) %collective-permute-start.26) | collective-permute-done | bytes 540704 | tf_op jit(solution)/shard_map/ppermute | solution.py:594
  73.8 9.4 %qkv_conv.1 = (f32[256,3072]{1,0:T(8,128)S(1)}, bf16[4,3,3072]{2,1,0:T(4,128)(2,1)S(1)}) custom-call(s32[32]{0:T(128)S(1)} %fusion.2.at_ref, s32[4]{0:T(128)S(1)} %copy-done.23, bf16[256,1024]{1,0:T(8,128)(2,1)S(1)} %copy-done.25, bf16[32,3072]{1,0:T(8,128)(2,1)} %refs_0_.1, bf16[32,3072]{1,0:T(8,128)(2,1)} %copy-done.43, bf16[32,3072]{1,0:T(8,128)(2,1)} %copy-done.44, ...), custom_call_target="tpu_custom_call" | custom-call | flops 5368709120 | bytes 65536 | tf_op jit(solution)/shard_map/qkv_conv/pallas_call | solution.py:217
  83.3 4.3 %stats.1.refs_0_ = bf16[4,1632,128]{2,1,0:T(8,128)(2,1)S(1)} custom-call(s32[4]{0:T(128)S(1)} %get-tuple-element.47.place_ref, s32[4]{0:T(128)S(1)} %get-tuple-element.46.slot_ref, f32[256,3072]{1,0:T(8,128)S(1)} %get-tuple-element.25.k_ref.v_ref.q_ref, f32[256,3072]{1,0:T(8,128)S(1)} %get-tuple-element.25.k_ref.v_ref.q_ref, ...), custom_call_target="tpu_custom_call" | custom-call | flops 3221225472 | bytes 65536 | tf_op jit(solution)/shard_map/stats/pallas_call | solution.py:282
  88.7 4.7 %all-to-all-start = ((bf16[4,1632,128]{2,1,0:T(8,128)(2,1)}), bf16[4,1632,128]{2,1,0:T(8,128)(2,1)}, u32[]{:S(2)}, u32[]{:S(2)}) async-start(bf16[4,1632,128]{2,1,0:T(8,128)(2,1)} %copy-done), calls=%async_computation | async-start | bytes 3342336 | tf_op jit(solution)/shard_map/all_to_all | solution.py:666
  95.9 1.7 collective-permute-start.29
  97.5 15.1 %collective-permute-done.27.refs_1_.refs_4_.refs_2_ = bf16[704,384]{1,0:T(8,128)(2,1)} collective-permute-done((bf16[704,384]{1,0:T(8,128)(2,1)}, bf16[704,384]{1,0:T(8,128)(2,1)}, u32[]{:S(2)}, u32[]{:S(2)}) %collective-permute-start.27) | collective-permute-done | bytes 540704 | tf_op jit(solution)/shard_map/ppermute | solution.py:594
  114.1 10.5 %collective-permute-done.30.refs_2_.refs_9_.refs_7_ = bf16[704,384]{1,0:T(8,128)(2,1)} collective-permute-done((bf16[704,384]{1,0:T(8,128)(2,1)}, bf16[704,384]{1,0:T(8,128)(2,1)}, u32[]{:S(2)}, u32[]{:S(2)}) %collective-permute-start.30) | collective-permute-done | bytes 540704 | tf_op jit(solution)/shard_map/ppermute | solution.py:594
  124.6 1.7 collective-permute-start.32
  126.3 1.2 copy-done.2
  127.5 1.2 copy-done.5
  128.8 13.8 %cg.2.x_ref = bf16[128,1024]{1,0:T(8,128)(2,1)S(1)} custom-call(f32[8]{0:T(128)S(1)} %copy-done.9, f32[256,3072]{1,0:T(8,128)S(1)} %get-tuple-element.25.k_ref.v_ref.q_ref, f32[256,3072]{1,0:T(8,128)S(1)} %get-tuple-element.25.k_ref.v_ref.q_ref, f32[256,3072]{1,0:T(8,128)S(1)} %get-tuple-element.25.k_ref.v_ref.q_ref, f32[4,8,64,128]{3,2,1,0:T(8,128)S(1)} %copy-done.2, ...), custom_call_target="tpu_custom_call" | custom-call | flops 4294967296 | bytes 65536 | tf_op jit(solution)/shard_map/cg/pallas_call | solution.py:447
  142.6 4.1 %unpack.1 = (f32[4,8,128,128]{3,2,1,0:T(8,128)}, f32[4,8,128,128]{3,2,1,0:T(8,128)}, bf16[4,3,3072]{2,1,0:T(4,128)(2,1)S(1)}) custom-call(bf16[4,1632,128]{2,1,0:T(8,128)(2,1)} %all-to-all-done.part_ref), custom_call_target="tpu_custom_call" | custom-call | flops 3221225472 | bytes 65536 | tf_op jit(solution)/shard_map/unpack/pallas_call | solution.py:352
  147.4 1.6 copy-done.10
  150.1 1.3 out_proj.2
  152.4 1.5 collective-permute-start.33
  153.9 14.0 %cg.3.x_ref = bf16[128,1024]{1,0:T(8,128)(2,1)S(1)} custom-call(f32[8]{0:T(128)S(1)} %copy-done.9, f32[256,3072]{1,0:T(8,128)S(1)} %get-tuple-element.25.k_ref.v_ref.q_ref, f32[256,3072]{1,0:T(8,128)S(1)} %get-tuple-element.25.k_ref.v_ref.q_ref, f32[256,3072]{1,0:T(8,128)S(1)} %get-tuple-element.25.k_ref.v_ref.q_ref, f32[4,8,64,128]{3,2,1,0:T(8,128)S(1)} %copy-done.3, ...), custom_call_target="tpu_custom_call" | custom-call | flops 4294967296 | bytes 65536 | tf_op jit(solution)/shard_map/cg/pallas_call | solution.py:447
  170.5 8.9 %ffn.2 = (f32[128,1024]{1,0:T(8,128)S(1)}, f32[128,1024]{1,0:T(8,128)S(1)}, bf16[128,1024]{1,0:T(8,128)(2,1)S(1)}) custom-call(s32[8]{0:T(128)S(1)} %broadcast_xor_fusion.order_ref, bf16[128,1024]{1,0:T(8,128)(2,1)} %get-tuple-element.32.refs_0_, bf16[128,1024]{1,0:T(8,128)(2,1)S(1)} %get-tuple-element.33.refs_1_, ...), custom_call_target="tpu_custom_call" | custom-call | flops 5368709120 | bytes 65536 | tf_op jit(solution)/shard_map/ffn/pallas_call | solution.py:547
  179.4 1.4 collective-permute-start.42
  180.8 5.9 %ffn.3 = bf16[128,1024]{1,0:T(8,128)(2,1)S(1)} custom-call(s32[8]{0:T(128)S(1)} %broadcast_xor_fusion.order_ref, bf16[128,1024]{1,0:T(8,128)(2,1)S(1)} %collective-permute-done.43.refs_0_, bf16[704,384]{1,0:T(8,128)(2,1)} %copy-done.12, bf16[704,384]{1,0:T(8,128)(2,1)} %collective-permute-done.27.refs_1_.refs_4_.refs_2_, ...), custom_call_target="tpu_custom_call" | custom-call | flops 5368709120 | bytes 65536 | tf_op jit(solution)/shard_map/ffn/pallas_call | solution.py:547
  188.5 5.9 %collective-permute-done.44 = bf16[128,1024]{1,0:T(8,128)(2,1)S(1)} collective-permute-done((bf16[128,1024]{1,0:T(8,128)(2,1)S(1)}, bf16[128,1024]{1,0:T(8,128)(2,1)S(1)}, u32[]{:S(2)}, u32[]{:S(2)}) %collective-permute-start.44) | collective-permute-done | bytes 262176 | tf_op jit(solution)/shard_map/ppermute | solution.py:594
  (205 shorter events, 33.7 us)
Async XLA Ops:
  7.2 140.3 %all-gather.2.cloned.1.call-start = ((), (), s32[]{:S(2)}) async-start(), calls=%async_computation.1 | async-start | bytes 2162688 | tf_op jit(solution)/shard_map/all_gather | solution.py:598
  7.2 11.4 %collective-permute-start = (bf16[32,3072]{1,0:T(8,128)(2,1)}, bf16[32,3072]{1,0:T(8,128)(2,1)S(1)}, u32[]{:S(2)}, u32[]{:S(2)}) collective-permute-start(bf16[32,3072]{1,0:T(8,128)(2,1)} %refs_0_.1), channel_id=1, source_target_pairs={{0,1},{1,2},{2,3},{3,0},{4,5},{5,6},{6,7},{7,4},{8,9},{9,10},{10,1... | collective-permute-start | bytes 589832 | tf_op jit(solution)/shard_map/ppermute | solution.py:594
  12.4 16.1 %collective-permute-start.1 = (bf16[32,3072]{1,0:T(8,128)(2,1)}, bf16[32,3072]{1,0:T(8,128)(2,1)S(1)}, u32[]{:S(2)}, u32[]{:S(2)}) collective-permute-start(bf16[32,3072]{1,0:T(8,128)(2,1)} %refs_0_.1), channel_id=1, source_target_pairs={{0,8},{1,9},{2,10},{3,11},{4,12},{5,13},{6,14},{7,15},{8,0},{9,1},... | collective-permute-start | bytes 589832 | tf_op jit(solution)/shard_map/ppermute | solution.py:594
  14.0 14.6 %collective-permute-start.2 = (bf16[32,3072]{1,0:T(8,128)(2,1)}, bf16[32,3072]{1,0:T(8,128)(2,1)S(1)}, u32[]{:S(2)}, u32[]{:S(2)}) collective-permute-start(bf16[32,3072]{1,0:T(8,128)(2,1)} %refs_0_.1), channel_id=1, source_target_pairs={{0,16},{1,17},{2,18},{3,19},{4,20},{5,21},{6,22},{7,23},{8,24},{9,... | collective-permute-start | bytes 589832 | tf_op jit(solution)/shard_map/ppermute | solution.py:594
  15.5 13.7 %collective-permute-start.13 = (bf16[32,3072]{1,0:T(8,128)(2,1)}, bf16[32,3072]{1,0:T(8,128)(2,1)S(1)}, u32[]{:S(2)}, u32[]{:S(2)}) collective-permute-start(bf16[32,3072]{1,0:T(8,128)(2,1)} %refs_0_.1), channel_id=1, source_target_pairs={{0,4},{1,5},{2,6},{3,7},{4,0},{5,1},{6,2},{7,3},{8,12},{9,13},{10,... | collective-permute-start | bytes 589832 | tf_op jit(solution)/shard_map/ppermute | solution.py:594
  28.5 16.3 %collective-permute-start.17 = (bf16[32,3072]{1,0:T(8,128)(2,1)S(1)}, bf16[32,3072]{1,0:T(8,128)(2,1)S(1)}, u32[]{:S(2)}, u32[]{:S(2)}) collective-permute-start(bf16[32,3072]{1,0:T(8,128)(2,1)S(1)} %collective-permute-done.refs_0_.refs_4_), channel_id=1, source_target_pairs={{0,4},{1,5},{2,6},{3,7},{4,0},{5,1},{6,2},{7,3},{8,12},{9,13},{10,... | collective-permute-start | bytes 589832 | tf_op jit(solution)/shard_map/ppermute | solution.py:594
  28.6 16.9 %collective-permute-start.3 = (bf16[32,3072]{1,0:T(8,128)(2,1)S(1)}, bf16[32,3072]{1,0:T(8,128)(2,1)}, u32[]{:S(2)}, u32[]{:S(2)}) collective-permute-start(bf16[32,3072]{1,0:T(8,128)(2,1)S(1)} %collective-permute-done.1.refs_1_), channel_id=1, source_target_pairs={{0,16},{1,17},{2,18},{3,19},{4,20},{5,21},{6,22},{7,23},{8,24},{9,... | collective-permute-start | bytes 589832 | tf_op jit(solution)/shard_map/ppermute | solution.py:594
  29.3 16.3 %collective-permute-start.14 = (bf16[32,3072]{1,0:T(8,128)(2,1)S(1)}, bf16[32,3072]{1,0:T(8,128)(2,1)S(1)}, u32[]{:S(2)}, u32[]{:S(2)}) collective-permute-start(bf16[32,3072]{1,0:T(8,128)(2,1)S(1)} %collective-permute-done.1.refs_1_), channel_id=1, source_target_pairs={{0,4},{1,5},{2,6},{3,7},{4,0},{5,1},{6,2},{7,3},{8,12},{9,13},{10,... | collective-permute-start | bytes 589832 | tf_op jit(solution)/shard_map/ppermute | solution.py:594
  29.4 23.7 %collective-permute-start.9 = (bf16[64,3072]{1,0:T(8,128)(2,1)S(1)}, bf16[64,3072]{1,0:T(8,128)(2,1)S(1)}, u32[]{:S(2)}, u32[]{:S(2)}) collective-permute-start(bf16[64,3072]{1,0:T(8,128)(2,1)S(1)} %constant_dynamic-update-slice_fusion.refs_8_), channel_id=1, source_target_pairs={{0,8},{1,9},{2,10},{3,11},{4,12},{5,13},{6,14},{7,15},{8,0},{9,1},... | collective-permute-start | bytes 1179656 | tf_op jit(solution)/shard_map/ppermute | solution.py:594
  34.6 19.0 %collective-permute-start.10 = (bf16[64,3072]{1,0:T(8,128)(2,1)S(1)}, bf16[64,3072]{1,0:T(8,128)(2,1)S(1)}, u32[]{:S(2)}, u32[]{:S(2)}) collective-permute-start(bf16[64,3072]{1,0:T(8,128)(2,1)S(1)} %constant_dynamic-update-slice_fusion.refs_8_), channel_id=1, source_target_pairs={{0,16},{1,17},{2,18},{3,19},{4,20},{5,21},{6,22},{7,23},{8,24},{9,... | collective-permute-start | bytes 1179656 | tf_op jit(solution)/shard_map/ppermute | solution.py:594
  44.8 24.4 %collective-permute-start.26 = (bf16[704,384]{1,0:T(8,128)(2,1)S(1)}, bf16[704,384]{1,0:T(8,128)(2,1)}, u32[]{:S(2)}, u32[]{:S(2)}) collective-permute-start(bf16[704,384]{1,0:T(8,128)(2,1)S(1)} %get-tuple-element.24.refs_3_.refs_1_), channel_id=1, source_target_pairs={{0,2},{1,3},{2,0},{3,1},{4,6},{5,7},{6,4},{7,5},{8,10},{9,11},{10,... | collective-permute-start | bytes 1622024 | tf_op jit(solution)/shard_map/ppermute | solution.py:594
  53.7 15.6 %collective-permute-start.21 = (bf16[64,3072]{1,0:T(8,128)(2,1)S(1)}, bf16[64,3072]{1,0:T(8,128)(2,1)S(1)}, u32[]{:S(2)}, u32[]{:S(2)}) collective-permute-start(bf16[64,3072]{1,0:T(8,128)(2,1)S(1)} %constant_dynamic-update-slice_fusion.refs_8_), channel_id=1, source_target_pairs={{0,4},{1,5},{2,6},{3,7},{4,0},{5,1},{6,2},{7,3},{8,12},{9,13},{10,... | collective-permute-start | bytes 1179656 | tf_op jit(solution)/shard_map/ppermute | solution.py:594
  54.0 15.9 %collective-permute-start.11 = (bf16[32,3072]{1,0:T(8,128)(2,1)S(1)}, bf16[32,3072]{1,0:T(8,128)(2,1)S(1)}, u32[]{:S(2)}, u32[]{:S(2)}) collective-permute-start(bf16[32,3072]{1,0:T(8,128)(2,1)S(1)} %slice.8), channel_id=1, source_target_pairs={{0,16},{1,17},{2,18},{3,19},{4,20},{5,21},{6,22},{7,23},{8,24},{9,... | collective-permute-start | bytes 589832 | tf_op jit(solution)/shard_map/ppermute | solution.py:594
  55.4 14.5 %collective-permute-start.12 = (bf16[32,3072]{1,0:T(8,128)(2,1)S(1)}, bf16[32,3072]{1,0:T(8,128)(2,1)S(1)}, u32[]{:S(2)}, u32[]{:S(2)}) collective-permute-start(bf16[32,3072]{1,0:T(8,128)(2,1)S(1)} %slice.9), channel_id=1, source_target_pairs={{0,8},{1,9},{2,10},{3,11},{4,12},{5,13},{6,14},{7,15},{8,0},{9,1},... | collective-permute-start | bytes 589832 | tf_op jit(solution)/shard_map/ppermute | solution.py:594
  56.1 15.7 %collective-permute-start.22 = (bf16[64,3072]{1,0:T(8,128)(2,1)S(1)}, bf16[64,3072]{1,0:T(8,128)(2,1)S(1)}, u32[]{:S(2)}, u32[]{:S(2)}) collective-permute-start(bf16[64,3072]{1,0:T(8,128)(2,1)S(1)} %collective-permute-done.9.refs_9_), channel_id=1, source_target_pairs={{0,4},{1,5},{2,6},{3,7},{4,0},{5,1},{6,2},{7,3},{8,12},{9,13},{10,... | collective-permute-start | bytes 1179656 | tf_op jit(solution)/shard_map/ppermute | solution.py:594
  88.7 53.9 %all-to-all-start = ((bf16[4,1632,128]{2,1,0:T(8,128)(2,1)}), bf16[4,1632,128]{2,1,0:T(8,128)(2,1)}, u32[]{:S(2)}, u32[]{:S(2)}) async-start(bf16[4,1632,128]{2,1,0:T(8,128)(2,1)} %copy-done), calls=%async_computation | async-start | bytes 3342336 | tf_op jit(solution)/shard_map/all_to_all | solution.py:666
  93.4 19.2 %collective-permute-start.27 = (bf16[704,384]{1,0:T(8,128)(2,1)}, bf16[704,384]{1,0:T(8,128)(2,1)}, u32[]{:S(2)}, u32[]{:S(2)}) collective-permute-start(bf16[704,384]{1,0:T(8,128)(2,1)} %copy-done.12), channel_id=1, source_target_pairs={{0,8},{1,9},{2,10},{3,11},{4,12},{5,13},{6,14},{7,15},{8,0},{9,1},... | collective-permute-start | bytes 1622024 | tf_op jit(solution)/shard_map/ppermute | solution.py:594
  93.8 19.2 %collective-permute-start.28 = (bf16[704,384]{1,0:T(8,128)(2,1)}, bf16[704,384]{1,0:T(8,128)(2,1)}, u32[]{:S(2)}, u32[]{:S(2)}) collective-permute-start(bf16[704,384]{1,0:T(8,128)(2,1)} %copy-done.12), channel_id=1, source_target_pairs={{0,16},{1,17},{2,18},{3,19},{4,20},{5,21},{6,22},{7,23},{8,24},{9,... | collective-permute-start | bytes 1622024 | tf_op jit(solution)/shard_map/ppermute | solution.py:594
  94.8 19.1 %collective-permute-start.34 = (bf16[704,384]{1,0:T(8,128)(2,1)}, bf16[704,384]{1,0:T(8,128)(2,1)S(1)}, u32[]{:S(2)}, u32[]{:S(2)}) collective-permute-start(bf16[704,384]{1,0:T(8,128)(2,1)} %copy-done.12), channel_id=1, source_target_pairs={{0,4},{1,5},{2,6},{3,7},{4,0},{5,1},{6,2},{7,3},{8,12},{9,13},{10,... | collective-permute-start | bytes 1622024 | tf_op jit(solution)/shard_map/ppermute | solution.py:594
  94.8 29.8 %collective-permute-start.30 = (bf16[704,384]{1,0:T(8,128)(2,1)}, bf16[704,384]{1,0:T(8,128)(2,1)}, u32[]{:S(2)}, u32[]{:S(2)}) collective-permute-start(bf16[704,384]{1,0:T(8,128)(2,1)} %collective-permute-done.26.refs_28_.refs_7_.refs_5_), channel_id=1, source_target_pairs={{0,16},{1,17},{2,18},{3,19},{4,20},{5,21},{6,22},{7,23},{8,24},{9,... | collective-permute-start | bytes 1622024 | tf_op jit(solution)/shard_map/ppermute | solution.py:594
  95.9 28.7 %collective-permute-start.29 = (bf16[704,384]{1,0:T(8,128)(2,1)}, bf16[704,384]{1,0:T(8,128)(2,1)S(1)}, u32[]{:S(2)}, u32[]{:S(2)}) collective-permute-start(bf16[704,384]{1,0:T(8,128)(2,1)} %collective-permute-done.26.refs_28_.refs_7_.refs_5_), channel_id=1, source_target_pairs={{0,8},{1,9},{2,10},{3,11},{4,12},{5,13},{6,14},{7,15},{8,0},{9,1},... | collective-permute-start | bytes 1622024 | tf_op jit(solution)/shard_map/ppermute | solution.py:594
  112.6 38.9 %collective-permute-start.38 = (bf16[704,384]{1,0:T(8,128)(2,1)}, bf16[704,384]{1,0:T(8,128)(2,1)}, u32[]{:S(2)}, u32[]{:S(2)}) collective-permute-start(bf16[704,384]{1,0:T(8,128)(2,1)} %collective-permute-done.26.refs_28_.refs_7_.refs_5_), channel_id=1, source_target_pairs={{0,4},{1,5},{2,6},{3,7},{4,0},{5,1},{6,2},{7,3},{8,12},{9,13},{10,... | collective-permute-start | bytes 1622024 | tf_op jit(solution)/shard_map/ppermute | solution.py:594
  113.0 38.4 %collective-permute-start.31 = (bf16[704,384]{1,0:T(8,128)(2,1)}, bf16[704,384]{1,0:T(8,128)(2,1)}, u32[]{:S(2)}, u32[]{:S(2)}) collective-permute-start(bf16[704,384]{1,0:T(8,128)(2,1)} %collective-permute-done.27.refs_1_.refs_4_.refs_2_), channel_id=1, source_target_pairs={{0,16},{1,17},{2,18},{3,19},{4,20},{5,21},{6,22},{7,23},{8,24},{9,... | collective-permute-start | bytes 1622024 | tf_op jit(solution)/shard_map/ppermute | solution.py:594
  113.8 38.1 %collective-permute-start.35 = (bf16[704,384]{1,0:T(8,128)(2,1)}, bf16[704,384]{1,0:T(8,128)(2,1)}, u32[]{:S(2)}, u32[]{:S(2)}) collective-permute-start(bf16[704,384]{1,0:T(8,128)(2,1)} %collective-permute-done.27.refs_1_.refs_4_.refs_2_), channel_id=1, source_target_pairs={{0,4},{1,5},{2,6},{3,7},{4,0},{5,1},{6,2},{7,3},{8,12},{9,13},{10,... | collective-permute-start | bytes 1622024 | tf_op jit(solution)/shard_map/ppermute | solution.py:594
  124.6 27.8 %collective-permute-start.36 = (bf16[704,384]{1,0:T(8,128)(2,1)}, bf16[704,384]{1,0:T(8,128)(2,1)}, u32[]{:S(2)}, u32[]{:S(2)}) collective-permute-start(bf16[704,384]{1,0:T(8,128)(2,1)} %collective-permute-done.28.refs_2_.refs_5_.refs_3_), channel_id=1, source_target_pairs={{0,4},{1,5},{2,6},{3,7},{4,0},{5,1},{6,2},{7,3},{8,12},{9,13},{10,... | collective-permute-start | bytes 1622024 | tf_op jit(solution)/shard_map/ppermute | solution.py:594
  124.6 27.5 %collective-permute-start.32 = (bf16[704,384]{1,0:T(8,128)(2,1)}, bf16[704,384]{1,0:T(8,128)(2,1)}, u32[]{:S(2)}, u32[]{:S(2)}) collective-permute-start(bf16[704,384]{1,0:T(8,128)(2,1)} %collective-permute-done.30.refs_2_.refs_9_.refs_7_), channel_id=1, source_target_pairs={{0,8},{1,9},{2,10},{3,11},{4,12},{5,13},{6,14},{7,15},{8,0},{9,1},... | collective-permute-start | bytes 1622024 | tf_op jit(solution)/shard_map/ppermute | solution.py:594
  151.4 17.2 %collective-permute-start.40 = (bf16[704,384]{1,0:T(8,128)(2,1)}, bf16[704,384]{1,0:T(8,128)(2,1)S(1)}, u32[]{:S(2)}, u32[]{:S(2)}) collective-permute-start(bf16[704,384]{1,0:T(8,128)(2,1)} %collective-permute-done.30.refs_2_.refs_9_.refs_7_), channel_id=1, source_target_pairs={{0,4},{1,5},{2,6},{3,7},{4,0},{5,1},{6,2},{7,3},{8,12},{9,13},{10,... | collective-permute-start | bytes 1622024 | tf_op jit(solution)/shard_map/ppermute | solution.py:594
  151.6 17.8 %collective-permute-start.39 = (bf16[704,384]{1,0:T(8,128)(2,1)S(1)}, bf16[704,384]{1,0:T(8,128)(2,1)S(1)}, u32[]{:S(2)}, u32[]{:S(2)}) collective-permute-start(bf16[704,384]{1,0:T(8,128)(2,1)S(1)} %copy-done.27), channel_id=1, source_target_pairs={{0,4},{1,5},{2,6},{3,7},{4,0},{5,1},{6,2},{7,3},{8,12},{9,13},{10,... | collective-permute-start | bytes 1622024 | tf_op jit(solution)/shard_map/ppermute | solution.py:594
  151.9 17.5 %collective-permute-start.37 = (bf16[704,384]{1,0:T(8,128)(2,1)}, bf16[704,384]{1,0:T(8,128)(2,1)S(1)}, u32[]{:S(2)}, u32[]{:S(2)}) collective-permute-start(bf16[704,384]{1,0:T(8,128)(2,1)} %collective-permute-done.31.refs_3_.refs_6_.refs_4_), channel_id=1, source_target_pairs={{0,4},{1,5},{2,6},{3,7},{4,0},{5,1},{6,2},{7,3},{8,12},{9,13},{10,... | collective-permute-start | bytes 1622024 | tf_op jit(solution)/shard_map/ppermute | solution.py:594
  152.1 17.3 %collective-permute-start.41 = (bf16[704,384]{1,0:T(8,128)(2,1)}, bf16[704,384]{1,0:T(8,128)(2,1)S(1)}, u32[]{:S(2)}, u32[]{:S(2)}) collective-permute-start(bf16[704,384]{1,0:T(8,128)(2,1)} %collective-permute-done.32.refs_0_.refs_10_.refs_8_), channel_id=1, source_target_pairs={{0,4},{1,5},{2,6},{3,7},{4,0},{5,1},{6,2},{7,3},{8,12},{9,13},{10,... | collective-permute-start | bytes 1622024 | tf_op jit(solution)/shard_map/ppermute | solution.py:594
  152.4 17.0 %collective-permute-start.33 = (bf16[128,1024]{1,0:T(8,128)(2,1)}, bf16[128,1024]{1,0:T(8,128)(2,1)S(1)}, u32[]{:S(2)}, u32[]{:S(2)}) collective-permute-start(bf16[128,1024]{1,0:T(8,128)(2,1)} %get-tuple-element.32.refs_0_), channel_id=1, source_target_pairs={{0,1},{1,0},{2,3},{3,2},{4,5},{5,4},{6,7},{7,6},{8,9},{9,8},{10,11... | collective-permute-start | bytes 786440 | tf_op jit(solution)/shard_map/ppermute | solution.py:594
  168.6 12.2 %collective-permute-start.43 = (bf16[128,1024]{1,0:T(8,128)(2,1)S(1)}, bf16[128,1024]{1,0:T(8,128)(2,1)S(1)}, u32[]{:S(2)}, u32[]{:S(2)}) collective-permute-start(bf16[128,1024]{1,0:T(8,128)(2,1)S(1)} %get-tuple-element.33.refs_1_), channel_id=1, source_target_pairs={{0,1},{1,0},{2,3},{3,2},{4,5},{5,4},{6,7},{7,6},{8,9},{9,8},{10,11... | collective-permute-start | bytes 786440 | tf_op jit(solution)/shard_map/ppermute | solution.py:594
  (73 other events, 629.3 us)
Sparse Core Ops, SparseCore 0:
  53.9 63.4 all-gather.1
where the time goes:
time: 203 us; the launch traced here: 202 us
  Pallas kernels  64.8 us (32%)
  waiting for transfers between devices  64.5 us (32%)
  starting transfers between devices  35.3 us (17%)
  local copies, waits for them, and re-layouts  20.9 us (10%)
  between operations  14.7 us (7%)
    ppermute x45, waiting for transfers between devices, shards(): move = lambda value, pairs: lax.ppermute(value, AXES, pairs)  64.5 us
    ppermute x45, starting transfers between devices, shards(): move = lambda value, pairs: lax.ppermute(value, AXES, pairs)  30.6 us
    pallas_call x2, Pallas kernels, cg_call(): pl.pallas_call(functools.partial(cg_kernel, heads, 4), grid=(count,), in_...  27.9 us
    unnamed x122, local copies, waits for them, and re-layouts  20.9 us
    pallas_call x2, Pallas kernels, ffn_call(): pl.pallas_call(functools.partial(ffn_kernel, spans, blocks, (len(inputs),...  14.8 us
    pallas_call x1, Pallas kernels, qkv_call(): pl.pallas_call(functools.partial(qkv_kernel, len(pieces), spans, chunk),...  9.41 us
    all_to_all x1, starting transfers between devices, shards(): lax.all_to_all(packed, 'mesh', split_axis=0, concat_axis=0, tiled=True)  4.68 us
    pallas_call x1, Pallas kernels, stats_call(): pl.pallas_call(functools.partial(stats_kernel, heads), grid_spec=pltpu.Pr...  4.27 us
  transfers between devices with their start and end apart: 47, of which 13 were waited for; matrix products, arithmetic and copies ran while one was open for 2% of the time, Pallas kernels for 32%

commit v1 on v0

v1 whole, which is shorter than its diff:
```python
import functools

import jax
import jax.numpy as jnp
import numpy as np
from jax import lax
from jax.experimental import pallas as pl
from jax.experimental.pallas import tpu as pltpu
from jax.sharding import PartitionSpec as P

ITERS = 5
AXES = ("req", "mesh")
TAIL_ROW = 5
F32 = jnp.float32
BF16 = jnp.bfloat16


def rms_norm(values, gain):
    return values * lax.rsqrt(jnp.mean(values * values, axis=-1, keepdims=True) + 1e-05) * gain


def cost(flops, bytes_accessed):
    return pl.CostEstimate(flops=flops, bytes_accessed=bytes_accessed, transcendentals=0)


def in_hbm(values):
    return [pltpu.with_memory_space_constraint(value, pltpu.HBM) for value in values]


def in_vmem(values):
    return [pltpu.with_memory_space_constraint(value, pltpu.VMEM) for value in values]


def flip_req(bit, reqs, peers):
    return [(r * peers + z, (r ^ bit) * peers + z) for r in range(reqs) for z in range(peers)]


def shift_mesh(step, reqs, peers):
    return [(r * peers + z, r * peers + (z + step) % peers) for r in range(reqs) for z in range(peers)]


def flip_mesh(bit, reqs, peers):
    return [(r * peers + z, r * peers + (z ^ bit)) for r in range(reqs) for z in range(peers)]


def gather_rows(own, move, shifts, flips, beside):
    flip_x, flip_y = flips
    rows = own.shape[0]
    one = move(own, shifts[1])
    x_own, y_own = move(own, flip_x), move(own, flip_y)
    three = move(own, shifts[3])
    two = move(one, shifts[1])
    x_one, y_one = move(one, flip_x), move(one, flip_y)
    *results, three = beside(three, [x_own, y_own])
    (two,) = release_call([two], [x_one, y_one])
    rest = jnp.concatenate([three, two], axis=0)
    x_rest, y_rest = move(rest, flip_x), move(rest, flip_y)
    xy_own, xy_one = move(x_own, flip_y), move(y_one, flip_x)
    xy_three, xy_two = move(x_rest[:rows], flip_y), move(y_rest[rows:], flip_x)
    parts = []
    for o, part in ((0, own), (2, x_own), (4, y_own), (6, xy_own)):
        parts.append((part, [(o, 0)]))
    for o, part in ((0, one), (2, x_one), (4, y_one), (6, xy_one)):
        parts.append((part, [(o, 1)]))
    for o, part in ((0, rest), (2, x_rest), (4, y_rest)):
        parts.append((part, [(o, 3), (o, 2)]))
    parts.append((xy_three, [(6, 3)]))
    parts.append((xy_two, [(6, 2)]))
    return [part for part, _ in parts], [where for _, where in parts], results, two, [xy_three, xy_two]


def prep_kernel(heads, len_ref, rate_ref, tok_ref, gain_ref, wg_ref, *refs):
    gate_ref, up_ref, down_ref = refs[:3]
    ffn_ref, normed_ref, weight_ref, carried_ref, tw_ref, decay_ref = refs[-7:-1]
    stripe = down_ref.shape[1]
    if stripe % 128 == 0:
        ffn_ref[:, 0:stripe] = gate_ref[...]
        ffn_ref[:, stripe : 2 * stripe] = up_ref[...]
        ffn_ref[:, 2 * stripe :] = down_ref[...]
    else:
        ffn_ref[...] = jnp.zeros(ffn_ref.shape, BF16)
    requests = weight_ref.shape[0]
    rows = tok_ref.shape[0]
    length = rows // requests
    normed = rms_norm(tok_ref[...].astype(F32), gain_ref[...]).astype(BF16)
    normed_ref[...] = normed
    lane = lax.broadcasted_iota(jnp.int32, (256, 2 * heads), 0)
    column = lax.broadcasted_iota(jnp.int32, (256, 2 * heads), 1)
    chosen = (column == 2 * lane) | ((column == 2 * (lane - 128) + 1) & (lane >= 128))
    gates = jnp.dot(chosen.astype(F32).astype(BF16), wg_ref[...], preferred_element_type=F32)
    logits = lax.dot_general(
        normed, gates.astype(BF16), (((1,), (1,)), ((), ())), preferred_element_type=F32
    )
    rate_lane = lax.broadcasted_iota(jnp.int32, (1, 128), 1)
    rate = jnp.zeros((1, 128), F32)
    for h in range(heads):
        rate = jnp.where(rate_lane == h, rate_ref[h], rate)
    position = lax.broadcasted_iota(jnp.int32, (length, 128), 0)
    lane = lax.broadcasted_iota(jnp.int32, (length, 128), 1)
    slot = jnp.where(lane < length, lane, lane - length)
    causal = position >= slot
    below = lax.broadcasted_iota(jnp.int32, (length, length), 0) >= lax.broadcasted_iota(
        jnp.int32, (length, length), 1
    )
    below = below.astype(F32)
    for r in range(requests):
        mine = logits[r * length : (r + 1) * length]
        live = (position < len_ref[r]).astype(F32)
        beta = jax.nn.sigmoid(mine[:, :128]) * live
        forget = mine[:, 128:]
        softplus = jnp.maximum(forget, 0.0) + jnp.log1p(jnp.exp(-jnp.abs(forget)))
        log_decay = -rate * softplus * live
        cum = jnp.dot(
            below, log_decay, precision=lax.Precision.HIGHEST, preferred_element_type=F32
        )
        last = cum[length - 1 : length]
        cum_rows = jnp.concatenate([cum, cum], axis=0).T
        beta_rows = jnp.concatenate([beta, beta], axis=0).T
        carried = jnp.exp(cum)
        tail_weight = jnp.exp(last - cum) * beta
        decay = jnp.exp(last)
        for h in range(heads):
            spread = cum[:, h : h + 1] - cum_rows[h : h + 1]
            weight = jnp.where(causal, jnp.exp(jnp.minimum(spread, 0.0)), 0.0)
            weight_ref[r, h] = weight * beta_rows[h : h + 1]
            carried_ref[r, h] = jnp.broadcast_to(carried[:, h : h + 1], (length, 128))
            tw_ref[r, h] = jnp.broadcast_to(tail_weight[:, h : h + 1], (length, 128))
            decay_ref[r, h : h + 1] = jnp.broadcast_to(decay[:, h : h + 1], (1, 128))


def prep_call(lengths, decay_rate, tokens, gain, w_gates, ffn_weights, through, behind):
    rows, width = tokens.shape
    requests, heads = lengths.shape[0], decay_rate.shape[0]
    length = rows // requests
    smem = pl.BlockSpec(memory_space=pltpu.SMEM)
    hbm = pl.BlockSpec(memory_space=pltpu.HBM)
    whole = lambda shape: pl.BlockSpec(shape, lambda i: (0,) * len(shape))
    inputs = [tokens, gain.reshape(1, width), w_gates.T, *ffn_weights]
    hidden, stripe = ffn_weights[0].shape
    wide = (requests, heads, length, 128)
    shapes = [(hidden, 3 * stripe), (rows, width), wide, wide, wide, (requests, heads, 128)]
    return pl.pallas_call(
        functools.partial(prep_kernel, heads),
        grid=(1,),
        in_specs=[smem] * 2 + [whole(value.shape) for value in inputs] + [hbm] * (1 + len(behind)),
        out_specs=[whole(shape) for shape in shapes] + [hbm],
        out_shape=[pltpu.HBM(shape, F32 if i > 1 else BF16) for i, shape in enumerate(shapes)]
        + [pltpu.HBM(through.shape, through.dtype)],
        input_output_aliases={2 + len(inputs): len(shapes)},
        compiler_params=pltpu.CompilerParams(vmem_limit_bytes=20 << 20),
        cost_estimate=cost(3 << 30, 1 << 16),
        name="norm_gates",
    )(lengths, decay_rate, *in_hbm(inputs + [through] + behind))


def split_kernel(core_ref, w_ref, keep_ref, send_ref):
    wide = keep_ref.shape[1] // 3
    for which in range(3):
        to = slice(which * wide, (which + 1) * wide)
        for out_ref, half in ((keep_ref, core_ref[0]), (send_ref, 1 - core_ref[0])):
            begin = pl.multiple_of((2 * which + half) * wide, wide)
            out_ref[:, to] = w_ref[:, pl.ds(begin, wide)]


def split_call(core, weights):
    rows, columns = weights.shape
    vmem = pl.BlockSpec(memory_space=pltpu.VMEM)
    return pl.pallas_call(
        split_kernel,
        in_specs=[pl.BlockSpec(memory_space=pltpu.SMEM), vmem],
        out_specs=[vmem] * 2,
        out_shape=[jax.ShapeDtypeStruct((rows, columns // 2), BF16)] * 2,
        cost_estimate=cost(1 << 28, 1 << 16),
        name="split_heads",
    )(core, weights)


def project_kernel(n_pieces, spans, at_ref, x_ref, other_ref, *refs):
    pieces = refs[:n_pieces]
    mine_ref, theirs_ref, weights, sems = refs[-4:]
    step = pl.program_id(0)
    columns = mine_ref.shape[1]
    chunks = weights.shape[1] // columns

    def copies(c):
        cut = pl.ds(c * columns, columns)
        for i, (piece, first, rows) in enumerate(spans):
            begin = pl.multiple_of(at_ref[i], 16)
            yield pltpu.make_async_copy(
                pieces[piece].at[pl.ds(first, rows), cut],
                weights.at[pl.ds(begin, rows), cut],
                sems.at[c, i],
            )

    @pl.when(step == 0)
    def _():
        for c in range(chunks):
            for copy in copies(c):
                copy.start()

    for c in range(chunks):

        @pl.when(step == c)
        def _():
            for copy in copies(c):
                copy.wait()

    now = weights[:, pl.ds(pl.multiple_of(step * columns, columns), columns)]
    theirs = jnp.dot(other_ref[...], now, preferred_element_type=F32)
    theirs_ref[...] = theirs.astype(BF16)
    mine_ref[...] = jnp.dot(x_ref[...], now, preferred_element_type=F32).astype(BF16)


def project_call(at, spans, x, other, pieces, behind):
    rows, depth = x.shape
    columns = pieces[0].shape[1]
    wide = 512
    whole = pl.BlockSpec(x.shape, lambda j, s: (0, 0))
    block = pl.BlockSpec((rows, wide), lambda j, s: (0, j))
    return pl.pallas_call(
        functools.partial(project_kernel, len(pieces), spans),
        grid_spec=pltpu.PrefetchScalarGridSpec(
            num_scalar_prefetch=1,
            grid=(columns // wide,),
            in_specs=[whole, whole] + [pl.BlockSpec(memory_space=pltpu.HBM)] * len(pieces + behind),
            out_specs=[block, block],
            scratch_shapes=[
                pltpu.VMEM((depth, columns), BF16),
                pltpu.SemaphoreType.DMA((columns // wide, len(spans))),
            ],
        ),
        out_shape=[pltpu.HBM((rows, columns), BF16)] * 2,
        compiler_params=pltpu.CompilerParams(vmem_limit_bytes=16 << 20),
        cost_estimate=cost(3 << 30, 1 << 16),
        name="project",
    )(at, *in_hbm([x, other] + pieces + behind))


def conv_kernel(half_ref, len_ref, projected_ref, tail_ref, conv_ref, *refs):
    act_ref, new_tail_ref = refs[-2:]
    requests, window, columns = tail_ref.shape
    length = projected_ref.shape[0] // requests
    is_vector = pl.program_id(0) < 2
    for r in range(requests):
        blank = jnp.zeros((TAIL_ROW, columns), F32)
        head_rows = jnp.concatenate([blank, tail_ref[r].astype(F32)], axis=0)
        mine = projected_ref[r * length : (r + 1) * length].astype(F32)
        extended = jnp.concatenate([head_rows, mine], axis=0)
        wanted = lax.broadcasted_iota(jnp.int32, (8, extended.shape[0]), 0) + len_ref[r]
        place = lax.broadcasted_iota(jnp.int32, (8, extended.shape[0]), 1)
        chosen = (place == wanted + TAIL_ROW).astype(F32)
        rows = jnp.dot(chosen, extended, preferred_element_type=F32)
        new_tail_ref[r] = rows[:window].astype(BF16)
        total = conv_ref[0:1] * extended[TAIL_ROW : TAIL_ROW + length]
        for tap in range(1, window + 1):
            total = total + conv_ref[tap : tap + 1] * extended[
                TAIL_ROW + tap : TAIL_ROW + tap + length
            ]
        act = total * jax.nn.sigmoid(total)
        for h in range(columns // 128):
            head = act[:, h * 128 : (h + 1) * 128]
            scale = lax.rsqrt(jnp.sum(head * head, axis=-1, keepdims=True) + 1e-06)
            scale = jnp.where(is_vector, scale, jnp.ones_like(scale))
            act_ref[r * length : (r + 1) * length, h * 128 : (h + 1) * 128] = head * scale


def conv_call(half, lengths, projected, tails, conv_weight, held):
    rows, columns = projected.shape
    requests, window = tails.shape[:2]
    wide = columns // 3
    rows_block = pl.BlockSpec((rows, wide), lambda j, s, t: (0, 2 * j + s[0]))
    tail_block = pl.BlockSpec((requests, window, wide), lambda j, s, t: (0, 0, 2 * j + s[0]))
    return pl.pallas_call(
        conv_kernel,
        grid_spec=pltpu.PrefetchScalarGridSpec(
            num_scalar_prefetch=2,
            grid=(3,),
            in_specs=[
                pl.BlockSpec((rows, wide), lambda j, s, t: (0, j)),
                tail_block,
                pl.BlockSpec((window + 1, wide), lambda j, s, t: (0, 2 * j + s[0])),
            ]
            + [pl.BlockSpec(memory_space=pl.ANY)] * len(held),
            out_specs=[rows_block, tail_block],
        ),
        out_shape=[
            pltpu.HBM((rows, 2 * columns), F32),
            pltpu.HBM(tails.shape, BF16),
        ],
        input_output_aliases={5: 0, 6: 1} if held else {},
        compiler_params=pltpu.CompilerParams(vmem_limit_bytes=16 << 20),
        cost_estimate=cost(2 << 30, 1 << 16),
        name="conv_norm",
    )(half, lengths, *in_hbm([projected, tails, conv_weight] + held))


def stats_kernel(heads, place_ref, slot_ref, k_ref, v_ref, tw_ref, fd_ref, s_ref, vs_ref, *refs):
    tail_ref, out_ref = refs
    size = 128
    row = lax.broadcasted_iota(jnp.int32, (size, size), 0)
    col = lax.broadcasted_iota(jnp.int32, (size, size), 1)
    half = heads // 2
    contract = (((0,), (0,)), ((), ()))
    keys_end = []
    for h in range(heads):
        keys = k_ref[:, h * size : (h + 1) * size]
        values = v_ref[:, h * size : (h + 1) * size]
        tail_weight = tw_ref[0, h]
        both = jnp.concatenate([keys * tail_weight, values * tail_weight], axis=1).astype(BF16)
        sums = lax.dot_general(both, keys.astype(BF16), contract, preferred_element_type=F32)
        decay = fd_ref[0, h : h + 1]
        keys_end.append(decay * s_ref[0, h] + sums[:size])
        at = half * size + h * size
        out_ref[0, at : at + size] = (decay * vs_ref[0, h] + sums[size:]).astype(BF16)
    diagonals = []
    for p in range(half):
        low, high = keys_end[p], keys_end[p + half]
        out_ref[0, p * size : (p + 1) * size] = jnp.where(row >= col, low, high).astype(BF16)
        diagonals.append(jnp.sum(jnp.where(row == col, high, 0.0), axis=0, keepdims=True))
    at = (half + heads) * size
    slot = slot_ref[pl.program_id(0)].astype(F32)
    diagonals.append(jnp.full((16 - half, size), slot, F32))
    out_ref[0, at : at + 16] = jnp.concatenate(diagonals, axis=0).astype(BF16)
    tail = tail_ref[0].astype(F32)
    strips = [tail[:, c : c + size] for c in range(0, tail.shape[1], size)]
    fill = out_ref.shape[1] - at - 16 - len(strips) * tail.shape[0]
    strips.append(jnp.zeros((fill, size), F32))
    out_ref[0, at + 16 :] = jnp.concatenate(strips, axis=0).astype(BF16)


def stats_call(places, slots, act, tail_weight, decay, keys_start, values_start, tails):
    requests, heads = keys_start.shape[:2]
    length, width = act.shape[0] // requests, heads * 128
    tail_rows = tails.shape[1] * tails.shape[2] // 128
    out_rows = (heads // 2 + heads) * 128 + 16 + tail_rows + -tail_rows % 16
    matrices = pl.BlockSpec((1, heads, 128, 128), lambda i, s, t: (i, 0, 0, 0))
    return pl.pallas_call(
        functools.partial(stats_kernel, heads),
        grid_spec=pltpu.PrefetchScalarGridSpec(
            num_scalar_prefetch=2,
            grid=(requests,),
            in_specs=[
                pl.BlockSpec((length, width), lambda i, s, t: (i, 1)),
                pl.BlockSpec((length, width), lambda i, s, t: (i, 2)),
                pl.BlockSpec((1, heads, length, 128), lambda i, s, t: (i, 0, 0, 0)),
                pl.BlockSpec((1, heads, 128), lambda i, s, t: (i, 0, 0)),
                matrices,
                matrices,
                pl.BlockSpec((1,) + tails.shape[1:], lambda i, s, t: (i, 0, 0)),
            ],
            out_specs=pl.BlockSpec((1, out_rows, 128), lambda i, s, t: (s[i], 0, 0)),
        ),
        out_shape=pltpu.HBM((requests, out_rows, 128), BF16),
        compiler_params=pltpu.CompilerParams(vmem_limit_bytes=16 << 20),
        cost_estimate=cost(3 << 30, 1 << 16),
        name="stats",
    )(
        places,
        slots,
        *in_hbm([act, act, tail_weight, decay, keys_start, values_start, tails]),
    )


def unpack_kernel(heads, part_ref, *refs):
    keys_ref, values_ref, tail_ref, keys_buf, values_buf, tail_buf, sems = refs[-7:]
    size = 128
    half = heads // 2
    window, columns = tail_ref.shape[1:]
    row = lax.broadcasted_iota(jnp.int32, (size, size), 0)
    col = lax.broadcasted_iota(jnp.int32, (size, size), 1)
    n_parts = part_ref.shape[0]
    under_way = []
    for s in range(n_parts):
        buf = s % 2
        if s >= 2:
            for copy in under_way[s - 2]:
                copy.wait()
        at = (half + heads) * size
        diagonals = part_ref[s, at : at + 16].astype(F32)
        slot = jnp.max(diagonals[half : half + 1]).astype(jnp.int32)
        for p in range(half):
            packed = part_ref[s, p * size : (p + 1) * size].astype(F32)
            turned = packed.T
            keys_buf[buf, p] = jnp.where(row >= col, packed, turned)
            keys_buf[buf, p + half] = jnp.where(
                row < col, packed, jnp.where(row == col, diagonals[p : p + 1], turned)
            )
        for h in range(heads):
            begin = (half + h) * size
            values_buf[buf, h] = part_ref[s, begin : begin + size].astype(F32)
        rows = part_ref[s, at + 16 :].astype(F32)
        strips = [rows[c * window : (c + 1) * window] for c in range(columns // size)]
        tail_buf[s] = jnp.concatenate(strips, axis=1).astype(BF16)
        copies = [
            pltpu.make_async_copy(keys_buf.at[buf], keys_ref.at[slot], sems.at[s, 0]),
            pltpu.make_async_copy(values_buf.at[buf], values_ref.at[slot], sems.at[s, 1]),
            pltpu.make_async_copy(tail_buf.at[s], tail_ref.at[slot], sems.at[s, 2]),
        ]
        for copy in copies:
            copy.start()
        under_way.append(copies)
    for copies in under_way[-2:]:
        for copy in copies:
            copy.wait()


def unpack_call(parts, heads, tail_shape, behind):
    n_parts = parts.shape[0]
    vmem = pl.BlockSpec(memory_space=pltpu.VMEM)
    hbm = pl.BlockSpec(memory_space=pltpu.HBM)
    matrices = jax.ShapeDtypeStruct((n_parts, heads, 128, 128), F32)
    return pl.pallas_call(
        functools.partial(unpack_kernel, heads),
        in_specs=[vmem] + [pl.BlockSpec(memory_space=pl.ANY)] * len(behind),
        out_specs=[hbm, hbm, hbm],
        out_shape=[matrices, matrices, jax.ShapeDtypeStruct((n_parts,) + tail_shape, BF16)],
        scratch_shapes=[
            pltpu.VMEM((2, heads, 128, 128), F32),
            pltpu.VMEM((2, heads, 128, 128), F32),
            pltpu.VMEM((n_parts,) + tail_shape, BF16),
            pltpu.SemaphoreType.DMA((n_parts, 3)),
        ],
        compiler_params=pltpu.CompilerParams(vmem_limit_bytes=16 << 20),
        cost_estimate=cost(3 << 30, 1 << 16),
        name="unpack",
    )(parts, *in_hbm(behind))


def two_terms(values):
    high = values.astype(BF16)
    low = (values - high.astype(F32)).astype(BF16)
    return high, low


def lane_sum(values):
    return jnp.sum(values, axis=-1, keepdims=True)


def cg_kernel(heads, group, ridge_ref, q_ref, k_ref, v_ref, w_ref, c_ref, s_ref, vs_ref, *refs):
    out_ref = refs[-1]
    size = 128
    part = lambda ref, h: ref[:, h * size : (h + 1) * size]
    first_half = lax.broadcasted_iota(jnp.int32, (q_ref.shape[0], size), 1) < size // 2
    transposed = (((1,), (1,)), ((), ()))
    for base in range(0, heads, group):
        hs = range(base, base + group)
        keys = [part(k_ref, h) for h in hs]
        keys2 = [jnp.concatenate([k, k], axis=0) for k in keys]
        keys2_bf = [k.astype(BF16) for k in keys2]
        keys_t = [k.T.astype(BF16) for k in keys2]
        system = []
        for i, h in enumerate(hs):
            m = jnp.concatenate([s_ref[0, h].astype(BF16), keys_t[i]], axis=1)
            system.append(jnp.concatenate([m, m], axis=0))

        def both_terms(field):
            return jnp.concatenate(two_terms(field), axis=1)

        def scored(products, i, h):
            scores = products[:, size:] * w_ref[0, h]
            high = scores.astype(BF16).astype(F32)
            return jnp.where(first_half, high, scores - high).astype(BF16)

        direction = [part(q_ref, h) for h in hs]
        residual = list(direction)
        total = [None] * group
        norm = [lane_sum(r * r) for r in residual]
        for it in range(ITERS):
            products = [
                jnp.dot(both_terms(direction[i]), system[i], preferred_element_type=F32)
                for i in range(group)
            ]
            spread = [
                jnp.dot(scored(products[i], i, h), keys2_bf[i], preferred_element_type=F32)
                for i, h in enumerate(hs)
            ]
            for i, h in enumerate(hs):
                applied = (
                    c_ref[0, h] * products[i][:, :size] + spread[i] + ridge_ref[h] * direction[i]
                )
                step = norm[i] / (lane_sum(direction[i] * applied) + 1e-20)
                moved = step * direction[i]
                total[i] = moved if total[i] is None else total[i] + moved
                if it + 1 < ITERS:
                    residual[i] = residual[i] - step * applied
                    following = lane_sum(residual[i] * residual[i])
                    direction[i] = residual[i] + following / (norm[i] + 1e-20) * direction[i]
                    norm[i] = following
        for i, h in enumerate(hs):
            start_m = jnp.concatenate([vs_ref[0, h].astype(BF16), keys2_bf[i]], axis=0)
            start_m = jnp.concatenate([start_m, start_m], axis=1)
            products = lax.dot_general(
                both_terms(total[i]), start_m, transposed, preferred_element_type=F32
            )
            values = part(v_ref, h)
            values2 = jnp.concatenate([values, values], axis=0).astype(BF16)
            read = c_ref[0, h] * products[:, :size] + jnp.dot(
                scored(products, i, h), values2, preferred_element_type=F32
            )
            out_ref[:, h * size : (h + 1) * size] = read.astype(BF16)


def cg_call(ridge, act, weight2, carried, keys_start, values_start, first, count, held, behind):
    requests, heads = keys_start.shape[:2]
    length, width = act.shape[0] // requests, heads * 128
    per_head = lambda rows: pl.BlockSpec((1, heads, rows, 128), lambda i: (i + first, 0, 0, 0))
    rows_of = lambda which: pl.BlockSpec((length, width), lambda i: (i + first, which))
    inputs = [act, act, act, weight2, carried, keys_start, values_start] + held + behind
    return pl.pallas_call(
        functools.partial(cg_kernel, heads, 8),
        grid=(count,),
        in_specs=[pl.BlockSpec(memory_space=pltpu.SMEM)]
        + [rows_of(0), rows_of(1), rows_of(2)]
        + [per_head(length), per_head(length), per_head(128), per_head(128)]
        + [pl.BlockSpec(memory_space=pl.ANY)] * len(held + behind),
        out_specs=rows_of(0),
        out_shape=jax.ShapeDtypeStruct((requests * length, width), BF16),
        input_output_aliases={8: 0} if held else {},
        compiler_params=pltpu.CompilerParams(vmem_limit_bytes=20 << 20),
        cost_estimate=cost(4 << 30, 1 << 16),
        name="cg",
    )(ridge, *in_hbm(inputs))


def release_kernel(*refs):
    del refs


def release_call(values, behind):
    hbm = pl.BlockSpec(memory_space=pltpu.HBM)
    return pl.pallas_call(
        release_kernel,
        in_specs=[hbm] * len(values) + [pl.BlockSpec(memory_space=pl.ANY)] * len(behind),
        out_specs=[hbm] * len(values),
        out_shape=[pltpu.HBM(value.shape, value.dtype) for value in values],
        input_output_aliases={i: i for i in range(len(values))},
        cost_estimate=cost(1 << 26, 1 << 10),
        name="release",
    )(*in_hbm(values + behind))


def out_kernel(x_ref, tok_ref, gain_ref, w_ref, *refs):
    after_ref, in_ref = refs[-2:]
    attended = jnp.dot(x_ref[...], w_ref[...], preferred_element_type=F32)
    after_attn = (tok_ref[...].astype(F32) + attended).astype(BF16)
    after_ref[...] = after_attn
    in_ref[...] = rms_norm(after_attn.astype(F32), gain_ref[...]).astype(BF16)


def out_call(head_rows, tokens, first, gain, weights, behind):
    rows, width = head_rows.shape[0] // 2, tokens.shape[1]
    half = lambda a: pl.BlockSpec((rows, a.shape[1]), lambda i: (first, 0))
    whole = lambda a: pl.BlockSpec(a.shape, lambda i: (0, 0))
    return pl.pallas_call(
        out_kernel,
        grid=(1,),
        in_specs=[
            half(head_rows),
            half(tokens),
            whole(gain),
            whole(weights),
        ]
        + [pl.BlockSpec(memory_space=pl.ANY)] * len(behind),
        out_specs=[pl.BlockSpec((rows, width), lambda i: (0, 0))] * 2,
        out_shape=[jax.ShapeDtypeStruct((rows, width), BF16)] * 2,
        compiler_params=pltpu.CompilerParams(vmem_limit_bytes=16 << 20),
        cost_estimate=cost(2 << 30, 1 << 16),
        name="out_proj",
    )(*in_hbm([head_rows, tokens, gain, weights] + behind))


def ffn_rows(x, matrices, ready):
    gate_w, up_w, down_w = matrices
    turned = (((1,), (1,)), ((), ()))
    total = None
    for block in range(gate_w.shape[0]):
        ready(block, 0)
        gate = lax.dot_general(x, gate_w[block], turned, preferred_element_type=F32)
        ready(block, 1)
        up = lax.dot_general(x, up_w[block], turned, preferred_element_type=F32)
        hidden = (gate * jax.nn.sigmoid(gate) * up).astype(BF16)
        ready(block, 2)
        sums = jnp.dot(hidden, down_w[block], preferred_element_type=F32)
        total = sums if total is None else total + sums
    return total


def ffn_first_kernel(spans, counts, order_ref, *refs):
    n_in, n_pieces, n_out = counts
    inputs, pieces = refs[:n_in], refs[n_in : n_in + n_pieces]
    outputs, matrices, sems = refs[-4 - n_out : -4], refs[-4:-1], refs[-1]
    size = 128

    def copies(block, which):
        for i, (piece, j) in enumerate(spans[block]):
            to = pl.ds(pl.multiple_of(order_ref[j] * size, size), size)
            yield pltpu.make_async_copy(
                pieces[piece].at[:, pl.ds(which * size, size)],
                matrices[which].at[block, :, to],
                sems.at[block, which, i],
            )

    for block in range(len(spans)):
        for which in range(3):
            for copy in copies(block, which):
                copy.start()

    def ready(block, which):
        for copy in copies(block, which):
            copy.wait()

    x = jnp.concatenate([ref[...] for ref in inputs], axis=0)
    total = ffn_rows(x, matrices, ready)
    begin = 0
    for out_ref in outputs:
        rows = out_ref.shape[0]
        out_ref[...] = total[begin : begin + rows].astype(out_ref.dtype)
        begin += rows


def ffn_first_call(order, spans, inputs, pieces, outputs):
    width = inputs[0].shape[1]
    hidden = pieces[0].shape[0]
    vmem = pl.BlockSpec(memory_space=pltpu.VMEM)
    matrix = pltpu.VMEM((len(spans), hidden, width), BF16)
    counts = (len(inputs), len(pieces), len(outputs))
    return pl.pallas_call(
        functools.partial(ffn_first_kernel, spans, counts),
        grid_spec=pltpu.PrefetchScalarGridSpec(
            num_scalar_prefetch=1,
            grid=(),
            in_specs=[vmem] * len(inputs)
            + [pl.BlockSpec(memory_space=pltpu.HBM)] * len(pieces),
            out_specs=[vmem] * (len(outputs) + 3),
            scratch_shapes=[pltpu.SemaphoreType.DMA((len(spans), 3, len(spans[0])))],
        ),
        out_shape=[jax.ShapeDtypeStruct((rows, width), kind) for rows, kind in outputs]
        + [matrix] * 3,
        compiler_params=pltpu.CompilerParams(vmem_limit_bytes=20 << 20),
        cost_estimate=cost(5 << 30, 1 << 16),
        name="ffn_first",
    )(order, *inputs, *in_hbm(pieces))


def ffn_second_kernel(counts, *refs):
    n_in, n_out = counts
    matrices, outputs = refs[n_in : n_in + 3], refs[-n_out:]
    x = jnp.concatenate([ref[...] for ref in refs[:n_in]], axis=0)
    total = ffn_rows(x, matrices, lambda block, which: None)
    begin = 0
    for out_ref in outputs:
        rows = out_ref.shape[0]
        out_ref[...] = total[begin : begin + rows].astype(out_ref.dtype)
        begin += rows


def ffn_second_call(inputs, matrices, kind, behind):
    vmem = pl.BlockSpec(memory_space=pltpu.VMEM)
    return pl.pallas_call(
        functools.partial(ffn_second_kernel, (len(inputs), len(inputs))),
        in_specs=[vmem] * (len(inputs) + 3)
        + [pl.BlockSpec(memory_space=pl.ANY)] * len(behind),
        out_specs=[vmem] * len(inputs),
        out_shape=[jax.ShapeDtypeStruct(x.shape, kind) for x in inputs],
        compiler_params=pltpu.CompilerParams(vmem_limit_bytes=16 << 20),
        cost_estimate=cost(3 << 30, 1 << 16),
        name="ffn_second",
    )(*inputs, *in_vmem(matrices), *in_hbm(behind))


def sum_kernel(*refs):
    out_ref = refs[-1]
    begin = 0
    for i in range(0, len(refs) - 1, 3):
        after_ref, mine_ref, got_ref = refs[i : i + 3]
        rows = after_ref.shape[0]
        total = after_ref[...].astype(F32) + (mine_ref[...] + got_ref[...].astype(F32))
        out_ref[begin : begin + rows] = total.astype(BF16)
        begin += rows


def sum_call(values):
    vmem = pl.BlockSpec(memory_space=pltpu.VMEM)
    rows = sum(value.shape[0] for value in values[::3])
    return pl.pallas_call(
        sum_kernel,
        in_specs=[vmem] * len(values),
        out_specs=vmem,
        out_shape=jax.ShapeDtypeStruct((rows, values[0].shape[1]), BF16),
        compiler_params=pltpu.CompilerParams(vmem_limit_bytes=8 << 20),
        cost_estimate=cost(1 << 30, 1 << 16),
        name="last_sum",
    )(*values)


def shards(
    tokens,
    lengths,
    ridge_keys,
    ridge_values,
    conv_tail,
    page_table,
    w_qkv,
    conv_weight,
    w_gates,
    decay_rate,
    ridge,
    w_out,
    attn_gain,
    ffn_gain,
    w_gate,
    w_up,
    w_down,
):
    requests, length, width = tokens.shape
    heads = decay_rate.shape[0]
    row_count = requests * length
    reqs, peers = lax.axis_size("req"), lax.axis_size("mesh")
    my_req, my_mesh = lax.axis_index("req"), lax.axis_index("mesh")
    move = lambda value, pairs: lax.ppermute(value, AXES, pairs)
    hop_one, hop_two = flip_mesh(1, reqs, peers), flip_mesh(2, reqs, peers)
    own_rows = w_qkv.shape[0]

    w_out_all = lax.all_gather(w_out, AXES, axis=0, tiled=True)
    flat_tokens = tokens.reshape(row_count, width)
    prep = functools.partial(
        prep_call,
        lengths,
        decay_rate,
        flat_tokens,
        attn_gain,
        w_gates,
        [w_gate.T, w_up.T, w_down],
    )
    ordered = (reqs, peers) == (8, 4)
    core = (my_req % 2).astype(jnp.int32).reshape(1)
    if ordered:
        shifts = {s: shift_mesh(s, reqs, peers) for s in range(1, peers)}
        flips = [flip_req(bit, reqs, peers) for bit in (1, 2, 4)]
        keep, send = split_call(core, w_qkv)
        chip_rows = jnp.concatenate([keep, move(send, flips[0])], axis=0)
        qkv_pieces, places, results, two, last = gather_rows(
            chip_rows, move, shifts, flips[1:], prep
        )
        ffn_own, *prepared = results
        spans, listed = [], []
        for piece, chips in enumerate(places):
            for i, (o, s) in enumerate(chips):
                for other in (0, 1):
                    spans.append((piece, (2 * i + other) * own_rows, own_rows))
                    listed.append((o ^ other, s))
        listed = np.array(listed, np.int32)
        owner = (my_req ^ listed[:, 0]) * peers + (my_mesh - listed[:, 1]) % peers
        qkv_at = (owner * own_rows).astype(jnp.int32)
        (ffn_own,) = release_call([ffn_own], [two])
        ffn_two = move(ffn_own, hop_two)
        (ffn_own,) = release_call([ffn_own], last)
        x_own, y_own = move(ffn_own, flips[1]), move(ffn_own, flips[2])
        normed, weight2, carried, tail_weight, decay = prepared
        mine, theirs = project_call(
            qkv_at, spans, normed, move(normed, flips[0]), qkv_pieces, [ffn_two]
        )
        got = move(theirs, flips[0])
        (ffn_two,) = release_call([ffn_two], [theirs])
        x_two, y_two = move(ffn_two, flips[1]), move(ffn_two, flips[2])
    else:
        w_qkv_all = lax.all_gather(w_qkv, AXES, axis=0, tiled=True)
        qkv_pieces = list(split_call(core, w_qkv_all))
        spans = [(0, 0, w_qkv_all.shape[0])]
        qkv_at = jnp.zeros((1,), jnp.int32)
        _, normed, weight2, carried, tail_weight, decay, _ = prep(w_out, [])
        mine, _ = project_call(qkv_at, spans, normed, normed, qkv_pieces[:1], [])
        got, _ = project_call(qkv_at, spans, normed, normed, qkv_pieces[1:], [])
        gate_all = lax.all_gather(w_gate, "req", axis=0, tiled=True)
        up_all = lax.all_gather(w_up, "req", axis=0, tiled=True)
        down_all = lax.all_gather(w_down, "req", axis=1, tiled=True)
        stripes = width // 128
        ffn_pieces = []
        for j in range(stripes):
            cut = slice(j * 128, (j + 1) * 128)
            piece = jnp.concatenate([gate_all[cut].T, up_all[cut].T, down_all[:, cut]], axis=1)
            ffn_pieces.append(piece)
        ffn_pieces = ffn_pieces + [move(piece, hop_two) for piece in ffn_pieces]
        ffn_spans = [[(i * stripes + j, j) for j in range(stripes)] for i in (0, 1)]
        ffn_order = jnp.arange(stripes)

    held = conv_call(core, lengths, mine, conv_tail, conv_weight, [])
    act, new_tail = conv_call(1 - core, lengths, got, conv_tail, conv_weight, list(held))

    packed = stats_call(
        page_table // requests,
        page_table % requests,
        act,
        tail_weight,
        decay,
        ridge_keys,
        ridge_values,
        new_tail,
    )
    if ordered:
        xy_own, xy_two = move(x_own, flips[2]), move(y_two, flips[1])
        ffn_pieces = [ffn_own, x_own, y_own, xy_own, ffn_two, x_two, y_two, xy_two]
        ffn_pieces = ffn_pieces + [move(p, flips[0]) for p in ffn_pieces]
        ffn_order = my_req ^ np.array((0, 2, 4, 6, 1, 3, 5, 7), np.int32)
        ffn_spans = [
            [(4 * i + j, j) for j in range(4)] + [(8 + 4 * i + j, 4 + j) for j in range(4)]
            for i in (0, 1)
        ]
        behind_a = [x_own, y_own]
        behind_b = [x_two, y_two, xy_own, *ffn_pieces[8:11], ffn_pieces[12]]
        behind_out = [xy_two, ffn_pieces[11], *ffn_pieces[13:15]]
    else:
        behind_a, behind_b, behind_out = [], [], []
    ffn_order = ffn_order.astype(jnp.int32)

    parts = lax.all_to_all(packed, "mesh", split_axis=0, concat_axis=0, tiled=True)

    per = requests // 2
    part_rows = per * length
    gain = ffn_gain.reshape(1, width)
    system = (ridge, act, weight2, carried, ridge_keys, ridge_values)
    heads_a = cg_call(*system, 0, per, [], [packed] + behind_a)
    after_a, in_a = out_call(heads_a, flat_tokens, 0, gain, w_out_all, [])
    theirs_a = move(in_a, hop_one)
    heads_b = cg_call(*system, per, per, [heads_a], [in_a] + behind_b)
    after_b, in_b = out_call(heads_b, flat_tokens, 1, gain, w_out_all, behind_out)
    theirs_b = move(in_b, hop_one)
    for_a, *matrices = ffn_first_call(
        ffn_order, ffn_spans, [theirs_a], ffn_pieces, [(part_rows, BF16)]
    )
    got_a = move(for_a, hop_one)
    (for_b,) = ffn_second_call([theirs_b], matrices, BF16, [for_a])
    got_b = move(for_b, hop_one)
    mine_a, mine_b = ffn_second_call([in_a, in_b], matrices, F32, [for_b])
    keys_decode, values_decode, tail_decode = unpack_call(
        parts, heads, conv_tail.shape[1:], [mine_b]
    )
    mixed = sum_call([after_a, mine_a, got_a, after_b, mine_b, got_b])
    return (
        mixed.reshape(requests, length, width),
        keys_decode,
        values_decode,
        tail_decode,
        heads_b.reshape(requests, length, -1),
    )


def solution(mesh):
    rows = P(AXES)
    in_specs = (
        rows,
        rows,
        rows,
        rows,
        rows,
        rows,
        rows,
        P(),
        P(),
        P(),
        P(),
        rows,
        P(),
        P(),
        P("req", "mesh"),
        P("req", "mesh"),
        P("mesh", "req"),
    )
    out_specs = (rows, rows, rows, rows, rows)
    return jax.shard_map(shards, mesh=mesh, in_specs=in_specs, out_specs=out_specs, check_vma=False)
```

time: 203 us -> 166 us (0.82)
  waiting for transfers between devices: 64.5 us -> 30.3 us
  local copies, waits for them, and re-layouts: 20.9 us -> 10.9 us
  Pallas kernels: 64.8 us -> 69.9 us
  starting transfers between devices: 35.3 us -> 38.8 us
    ppermute x45 -> x35, waiting for transfers between devices: 64.5 us -> 29.6 us  [shards(): move = lambda value, pairs: lax.ppermute(value, AXES, pairs)]
    unnamed x122 -> x89, local copies, waits for them, and re-layouts: 20.9 us -> 10.8 us
    ppermute x45 -> x35, starting transfers between devices: 30.6 us -> 34.9 us  [shards(): move = lambda value, pairs: lax.ppermute(value, AXES, pairs)]
    pallas_call x9 -> x18, Pallas kernels: 60.5 us -> 63.9 us  [the longest x2 21.9 us: cg_call(): pl.pallas_call(functools.partial(cg_kernel, heads, 8), grid=(count,), in_...]
  transfers between devices with their start and end apart: 47 -> 37, of which waited for: 13 -> 11; matrix products, arithmetic and copies ran while one was open for 2% -> 2% of each run, Pallas kernels for 32% -> 42%
where the time goes in v1:
time: 166 us; the launch traced here: 165 us
  Pallas kernels  69.9 us (42%)
  starting transfers between devices  38.8 us (23%)
  waiting for transfers between devices  30.3 us (18%)
  between operations  14.5 us (9%)
  local copies, waits for them, and re-layouts  10.9 us (7%)
    ppermute x35, starting transfers between devices, shards(): move = lambda value, pairs: lax.ppermute(value, AXES, pairs)  34.9 us
    ppermute x35, waiting for transfers between devices, shards(): move = lambda value, pairs: lax.ppermute(value, AXES, pairs)  29.6 us
    pallas_call x2, Pallas kernels, cg_call(): pl.pallas_call(functools.partial(cg_kernel, heads, 8), grid=(count,), in_...  21.9 us
    unnamed x89, local copies, waits for them, and re-layouts  10.8 us
    pallas_call x2, Pallas kernels, conv_call(): pl.pallas_call(conv_kernel, grid_spec=pltpu.PrefetchScalarGridSpec(num_sc...  9.14 us
    pallas_call x1, Pallas kernels, project_call(): pl.pallas_call(functools.partial(project_kernel, len(pieces), spans), gri...  6.86 us
    pallas_call x1, Pallas kernels, stats_call(): pl.pallas_call(functools.partial(stats_kernel, heads), grid_spec=pltpu.Pr...  5.94 us
    pallas_call x1, Pallas kernels, ffn_first_call(): pl.pallas_call(functools.partial(ffn_first_kernel, spans, counts), grid_s...  5.89 us
  transfers between devices with their start and end apart: 37, of which 11 were waited for; matrix products, arithmetic and copies ran while one was open for 2% of the time, Pallas kernels for 42%

profile of v1, /device:TPU:0, one launch (start us, length us, event | category | flops | bytes accessed | tf_op | source)
XLA Modules:
  0.0 165.5 jit_solution(3423456360177024102)
XLA Ops:
  7.9 1.6 split_heads.1
  11.1 3.0 %collective-permute-start.6 = (bf16[64,1536]{1,0:T(8,128)(2,1)S(1)}, bf16[64,1536]{1,0:T(8,128)(2,1)S(1)}, u32[]{:S(2)}, u32[]{:S(2)}) collective-permute-start(bf16[64,1536]{1,0:T(8,128)(2,1)S(1)} %constant_dynamic-update-slice_fusion.refs_0_), channel_id=1, source_target_pairs={{0,1},{1,2},{2,3},{3,0},{4,5},{5,6},{6,7},{7,4},{8,9},{9,10},{10,1... | collective-permute-start | bytes 589832 | tf_op jit(solution)/shard_map/ppermute | solution.py:720
  14.1 2.1 %collective-permute-start.1 = (bf16[64,1536]{1,0:T(8,128)(2,1)S(1)}, bf16[64,1536]{1,0:T(8,128)(2,1)S(1)}, u32[]{:S(2)}, u32[]{:S(2)}) collective-permute-start(bf16[64,1536]{1,0:T(8,128)(2,1)S(1)} %constant_dynamic-update-slice_fusion.refs_0_), channel_id=1, source_target_pairs={{0,3},{1,0},{2,1},{3,2},{4,7},{5,4},{6,5},{7,6},{8,11},{9,8},{10,9... | collective-permute-start | bytes 589832 | tf_op jit(solution)/shard_map/ppermute | solution.py:720
  16.2 1.6 collective-permute-start.2
  17.9 1.5 collective-permute-start.3
  19.4 2.5 %collective-permute-done.6.refs_4_ = bf16[64,1536]{1,0:T(8,128)(2,1)S(1)} collective-permute-done((bf16[64,1536]{1,0:T(8,128)(2,1)S(1)}, bf16[64,1536]{1,0:T(8,128)(2,1)S(1)}, u32[]{:S(2)}, u32[]{:S(2)}) %collective-permute-start.6) | collective-permute-done | bytes 196640 | tf_op jit(solution)/shard_map/ppermute | solution.py:720
  21.9 1.7 %collective-permute-start.7 = (bf16[64,1536]{1,0:T(8,128)(2,1)S(1)}, bf16[64,1536]{1,0:T(8,128)(2,1)S(1)}, u32[]{:S(2)}, u32[]{:S(2)}) collective-permute-start(bf16[64,1536]{1,0:T(8,128)(2,1)S(1)} %collective-permute-done.6.refs_4_), channel_id=1, source_target_pairs={{0,8},{1,9},{2,10},{3,11},{4,12},{5,13},{6,14},{7,15},{8,0},{9,1},... | collective-permute-start | bytes 589832 | tf_op jit(solution)/shard_map/ppermute | solution.py:720
  23.6 1.5 collective-permute-start.8
  28.2 5.1 %norm_gates.1 = (bf16[704,384]{1,0:T(8,128)(2,1)}, bf16[256,1024]{1,0:T(8,128)(2,1)}, f32[4,8,64,128]{3,2,1,0:T(8,128)}, f32[4,8,64,128]{3,2,1,0:T(8,128)}, f32[...) custom-call(s32[4]{0:T(128)S(1)} %copy-done.6, ...), custom_call_target="tpu_custom_call", output_to_operand_aliasing={{6}: (8, {})} | custom-call | flops 3221225472 | bytes 65536 | tf_op jit(solution)/shard_map/norm_gates/pallas_call | solution.py:142
  37.5 1.5 collective-permute-start.12
  39.0 2.8 %collective-permute-start.15 = (bf16[704,384]{1,0:T(8,128)(2,1)}, bf16[704,384]{1,0:T(8,128)(2,1)S(1)}, u32[]{:S(2)}, u32[]{:S(2)}) collective-permute-start(bf16[704,384]{1,0:T(8,128)(2,1)} %release.5.refs_0_), channel_id=1, source_target_pairs={{0,2},{1,3},{2,0},{3,1},{4,6},{5,7},{6,4},{7,5},{8,10},{9,11},{10,... | collective-permute-start | bytes 1622024 | tf_op jit(solution)/shard_map/ppermute | solution.py:720
  41.8 1.6 collective-permute-start.5
  43.4 5.3 %collective-permute-done.11.refs_9_ = bf16[128,1536]{1,0:T(8,128)(2,1)S(1)} collective-permute-done((bf16[128,1536]{1,0:T(8,128)(2,1)S(1)}, bf16[128,1536]{1,0:T(8,128)(2,1)S(1)}, u32[]{:S(2)}, u32[]{:S(2)}) %collective-permute-start.11) | collective-permute-done | bytes 393248 | tf_op jit(solution)/shard_map/ppermute | solution.py:720
  51.8 2.9 %collective-permute-done.5.refs_3_ = bf16[64,1536]{1,0:T(8,128)(2,1)S(1)} collective-permute-done((bf16[64,1536]{1,0:T(8,128)(2,1)S(1)}, bf16[64,1536]{1,0:T(8,128)(2,1)S(1)}, u32[]{:S(2)}, u32[]{:S(2)}) %collective-permute-start.5) | collective-permute-done | bytes 196640 | tf_op jit(solution)/shard_map/ppermute | solution.py:720
  55.5 12.1 %collective-permute-done.15.refs_13_.refs_0_ = bf16[704,384]{1,0:T(8,128)(2,1)S(1)} collective-permute-done((bf16[704,384]{1,0:T(8,128)(2,1)}, bf16[704,384]{1,0:T(8,128)(2,1)S(1)}, u32[]{:S(2)}, u32[]{:S(2)}) %collective-permute-start.15) | collective-permute-done | bytes 540704 | tf_op jit(solution)/shard_map/ppermute | solution.py:720
  69.3 6.9 %project.1 = (bf16[256,1536]{1,0:T(8,128)(2,1)}, bf16[256,1536]{1,0:T(8,128)(2,1)}) custom-call(s32[32]{0:T(128)S(1)} %fusion.2.at_ref, bf16[256,1024]{1,0:T(8,128)(2,1)} %get-tuple-element.35.x_ref, bf16[256,1024]{1,0:T(8,128)(2,1)} %copy-done.34, bf16[64,1536]{1,0:T(8,128)(2,1)} %copy-done.27, bf16[64,1536]{1,0:T(8,128)(2,1)} %copy-done.36, ...), custom_call_target="tpu_custom_call" | custom-call | flops 3221225472 | bytes 65536 | tf_op jit(solution)/shard_map/project/pallas_call | solution.py:220
  79.6 1.6 collective-permute-start.20
  81.2 4.6 %conv_norm.2 = (f32[256,3072]{1,0:T(8,128)}, bf16[4,3,3072]{2,1,0:T(4,128)(2,1)}) custom-call(s32[1]{0:T(128)} %bitcast.core_ref.half_ref, s32[4]{0:T(128)S(1)} %copy-done.7, bf16[256,1536]{1,0:T(8,128)(2,1)} %get-tuple-element.39.projected_ref, bf16[4,3,3072]{2,1,0:T(4,128)(2,1)} %copy.34.tail_ref, f32[4,3072]{1,0:T(4,128)} %conv_ref.3), custom_call_target="tpu_custom_call" | custom-call | flops 2147483648 | bytes 65536 | tf_op jit(solution)/shard_map/conv_norm/pallas_call | solution.py:273
  86.6 4.6 %conv_norm.3 = (f32[256,3072]{1,0:T(8,128)}, bf16[4,3,3072]{2,1,0:T(4,128)(2,1)}) custom-call(s32[1]{0:T(128)S(6)} %sub.13.half_ref, s32[4]{0:T(128)S(1)} %copy-done.7, bf16[256,1536]{1,0:T(8,128)(2,1)} %copy-done.30, bf16[4,3,3072]{2,1,0:T(4,128)(2,1)} %copy.34.tail_ref, f32[4,3072]{1,0:T(4,128)} %conv_ref.3, ...), custom_call_target="tpu_custom_call", output_to_operand_aliasing={{0}: (5, {}), {1}: (6, {})} | custom-call | flops 2147483648 | bytes 65536 | tf_op jit(solution)/shard_map/conv_norm/pallas_call | solution.py:273
  91.2 5.9 %stats.1.refs_0_ = bf16[4,1632,128]{2,1,0:T(8,128)(2,1)} custom-call(s32[4]{0:T(128)S(1)} %get-tuple-element.67.place_ref, s32[4]{0:T(128)S(1)} %get-tuple-element.66.slot_ref, f32[256,3072]{1,0:T(8,128)} %get-tuple-element.42.k_ref.v_ref.q_ref, f32[256,3072]{1,0:T(8,128)} %get-tuple-element.42.k_ref.v_ref.q_ref, ...), custom_call_target="tpu_custom_call" | custom-call | flops 3221225472 | bytes 65536 | tf_op jit(solution)/shard_map/stats/pallas_call | solution.py:337
  97.1 3.9 %all-to-all-start = ((bf16[4,1632,128]{2,1,0:T(8,128)(2,1)}), bf16[4,1632,128]{2,1,0:T(8,128)(2,1)S(1)}, u32[]{:S(2)}, u32[]{:S(2)}) async-start(bf16[4,1632,128]{2,1,0:T(8,128)(2,1)} %stats.1.refs_0_), calls=%async_computation | async-start | bytes 3342336 | tf_op jit(solution)/shard_map/all_to_all | solution.py:816
  101.6 1.9 %collective-permute-done.19.refs_2_.refs_6_ = bf16[704,384]{1,0:T(8,128)(2,1)S(1)} collective-permute-done((bf16[704,384]{1,0:T(8,128)(2,1)}, bf16[704,384]{1,0:T(8,128)(2,1)S(1)}, u32[]{:S(2)}, u32[]{:S(2)}) %collective-permute-start.19) | collective-permute-done | bytes 540704 | tf_op jit(solution)/shard_map/ppermute | solution.py:720
  104.1 1.5 collective-permute-start.26
  105.6 11.0 %cg.2.x_ref.refs_0_ = bf16[256,1024]{1,0:T(8,128)(2,1)} custom-call(f32[8]{0:T(128)S(1)} %copy-done.2, f32[256,3072]{1,0:T(8,128)} %get-tuple-element.42.k_ref.v_ref.q_ref, f32[256,3072]{1,0:T(8,128)} %get-tuple-element.42.k_ref.v_ref.q_ref, f32[256,3072]{1,0:T(8,128)} %get-tuple-element.42.k_ref.v_ref.q_ref, f32[4,8,64,128]{3,2,1,0:T(8,128)} %get-tuple-element.43.w_ref, ...), custom_call_target="tpu_custom_call" | custom-call | flops 4294967296 | bytes 65536 | tf_op jit(solution)/shard_map/cg/pallas_call | solution.py:509
  118.5 2.4 %out_proj.2 = (bf16[128,1024]{1,0:T(8,128)(2,1)S(1)}, bf16[128,1024]{1,0:T(8,128)(2,1)S(1)}) custom-call(bf16[256,1024]{1,0:T(8,128)(2,1)} %cg.2.x_ref.refs_0_, bf16[256,1024]{1,0:T(8,128)(2,1)} %bitcast.11, f32[1,1024]{1,0:T(1,128)} %bitcast.17, bf16[1024,1024]{1,0:T(8,128)(2,1)} %all-gather.2.cloned.1.call-done.w_ref), custom_call_target="tpu_custom_call" | custom-call | flops 2147483648 | bytes 65536 | tf_op jit(solution)/shard_map/out_proj/pallas_call | solution.py:554
  121.8 11.0 %cg.3.x_ref = bf16[256,1024]{1,0:T(8,128)(2,1)} custom-call(f32[8]{0:T(128)S(1)} %copy-done.2, f32[256,3072]{1,0:T(8,128)} %get-tuple-element.42.k_ref.v_ref.q_ref, f32[256,3072]{1,0:T(8,128)} %get-tuple-element.42.k_ref.v_ref.q_ref, f32[256,3072]{1,0:T(8,128)} %get-tuple-element.42.k_ref.v_ref.q_ref, ...), custom_call_target="tpu_custom_call", output_to_operand_aliasing={{}: (8, {})} | custom-call | flops 4294967296 | bytes 65536 | tf_op jit(solution)/shard_map/cg/pallas_call | solution.py:509
  132.8 2.4 %out_proj.3 = (bf16[128,1024]{1,0:T(8,128)(2,1)S(1)}, bf16[128,1024]{1,0:T(8,128)(2,1)S(1)}) custom-call(bf16[256,1024]{1,0:T(8,128)(2,1)} %cg.3.x_ref, bf16[256,1024]{1,0:T(8,128)(2,1)} %bitcast.12, f32[1,1024]{1,0:T(1,128)} %bitcast.18, bf16[1024,1024]{1,0:T(8,128)(2,1)} %all-gather.2.cloned.1.call-done.w_ref, bf16[704,384]{1,0:T(8,128)(2,1)} %copy-done.31, ...), custom_call_target="tpu_custom_call" | custom-call | flops 2147483648 | bytes 65536 | tf_op jit(solution)/shard_map/out_proj/pallas_call | solution.py:554
  138.2 5.9 %ffn_first.1 = (bf16[128,1024]{1,0:T(8,128)(2,1)S(1)}, bf16[2,704,1024]{2,1,0:T(8,128)(2,1)S(1)}, bf16[2,704,1024]{2,1,0:T(8,128)(2,1)S(1)}, bf16[2,704,1024]{2,1,0:T(8,128)(2,1)S(1)}) custom-call(s32[8]{0:T(128)S(1)} %broadcast_xor_fusion.order_ref, bf16[128,1024]{1,0:T(8,128)(2,1)S(1)} %collective-permute-done.30.refs_0_, ...), custom_call_target="tpu_custom_call" | custom-call | flops 5368709120 | bytes 65536 | tf_op jit(solution)/shard_map/ffn_first/pallas_call | solution.py:627
  145.6 2.4 %ffn_second.2.refs_5_ = bf16[128,1024]{1,0:T(8,128)(2,1)S(1)} custom-call(bf16[128,1024]{1,0:T(8,128)(2,1)S(1)} %collective-permute-done.32.refs_0_, bf16[2,704,1024]{2,1,0:T(8,128)(2,1)S(1)} %get-tuple-element.51.refs_1_.refs_2_, bf16[2,704,1024]{2,1,0:T(8,128)(2,1)S(1)} %get-tuple-element.52.refs_2_.refs_3_, ...), custom_call_target="tpu_custom_call" | custom-call | flops 3221225472 | bytes 65536 | tf_op jit(solution)/shard_map/ffn_second/pallas_call | solution.py:659
  148.7 2.6 %ffn_second.3 = (f32[128,1024]{1,0:T(8,128)S(1)}, f32[128,1024]{1,0:T(8,128)S(1)}) custom-call(bf16[128,1024]{1,0:T(8,128)(2,1)S(1)} %copy-done.1, bf16[128,1024]{1,0:T(8,128)(2,1)S(1)} %get-tuple-element.50.refs_1_, bf16[2,704,1024]{2,1,0:T(8,128)(2,1)S(1)} %get-tuple-element.51.refs_1_.refs_2_, ...), custom_call_target="tpu_custom_call" | custom-call | flops 3221225472 | bytes 65536 | tf_op jit(solution)/shard_map/ffn_second/pallas_call | solution.py:659
  152.1 2.7 %unpack.1 = (f32[4,8,128,128]{3,2,1,0:T(8,128)}, f32[4,8,128,128]{3,2,1,0:T(8,128)}, bf16[4,3,3072]{2,1,0:T(4,128)(2,1)S(1)}) custom-call(bf16[4,1632,128]{2,1,0:T(8,128)(2,1)S(1)} %all-to-all-done.part_ref, f32[128,1024]{1,0:T(8,128)} %copy-done.8), custom_call_target="tpu_custom_call" | custom-call | flops 3221225472 | bytes 65536 | tf_op jit(solution)/shard_map/unpack/pallas_call | solution.py:412
  155.5 2.1 %collective-permute-done.34.refs_5_ = bf16[128,1024]{1,0:T(8,128)(2,1)S(1)} collective-permute-done((bf16[128,1024]{1,0:T(8,128)(2,1)S(1)}, bf16[128,1024]{1,0:T(8,128)(2,1)S(1)}, u32[]{:S(2)}, u32[]{:S(2)}) %collective-permute-start.34) | collective-permute-done | bytes 262176 | tf_op jit(solution)/shard_map/ppermute | solution.py:720
  (158 shorter events, 30.8 us)
Async XLA Ops:
  7.2 111.3 %all-gather.2.cloned.1.call-start = ((), (), s32[]{:S(2)}) async-start(), calls=%async_computation.1 | async-start | bytes 2162688 | tf_op jit(solution)/shard_map/all_gather | solution.py:724
  11.1 10.7 %collective-permute-start.6 = (bf16[64,1536]{1,0:T(8,128)(2,1)S(1)}, bf16[64,1536]{1,0:T(8,128)(2,1)S(1)}, u32[]{:S(2)}, u32[]{:S(2)}) collective-permute-start(bf16[64,1536]{1,0:T(8,128)(2,1)S(1)} %constant_dynamic-update-slice_fusion.refs_0_), channel_id=1, source_target_pairs={{0,1},{1,2},{2,3},{3,0},{4,5},{5,6},{6,7},{7,4},{8,9},{9,10},{10,1... | collective-permute-start | bytes 589832 | tf_op jit(solution)/shard_map/ppermute | solution.py:720
  14.1 11.0 %collective-permute-start.1 = (bf16[64,1536]{1,0:T(8,128)(2,1)S(1)}, bf16[64,1536]{1,0:T(8,128)(2,1)S(1)}, u32[]{:S(2)}, u32[]{:S(2)}) collective-permute-start(bf16[64,1536]{1,0:T(8,128)(2,1)S(1)} %constant_dynamic-update-slice_fusion.refs_0_), channel_id=1, source_target_pairs={{0,3},{1,0},{2,1},{3,2},{4,7},{5,4},{6,5},{7,6},{8,11},{9,8},{10,9... | collective-permute-start | bytes 589832 | tf_op jit(solution)/shard_map/ppermute | solution.py:720
  16.2 9.9 %collective-permute-start.2 = (bf16[64,1536]{1,0:T(8,128)(2,1)S(1)}, bf16[64,1536]{1,0:T(8,128)(2,1)S(1)}, u32[]{:S(2)}, u32[]{:S(2)}) collective-permute-start(bf16[64,1536]{1,0:T(8,128)(2,1)S(1)} %constant_dynamic-update-slice_fusion.refs_0_), channel_id=1, source_target_pairs={{0,8},{1,9},{2,10},{3,11},{4,12},{5,13},{6,14},{7,15},{8,0},{9,1},... | collective-permute-start | bytes 589832 | tf_op jit(solution)/shard_map/ppermute | solution.py:720
  21.9 11.5 %collective-permute-start.7 = (bf16[64,1536]{1,0:T(8,128)(2,1)S(1)}, bf16[64,1536]{1,0:T(8,128)(2,1)S(1)}, u32[]{:S(2)}, u32[]{:S(2)}) collective-permute-start(bf16[64,1536]{1,0:T(8,128)(2,1)S(1)} %collective-permute-done.6.refs_4_), channel_id=1, source_target_pairs={{0,8},{1,9},{2,10},{3,11},{4,12},{5,13},{6,14},{7,15},{8,0},{9,1},... | collective-permute-start | bytes 589832 | tf_op jit(solution)/shard_map/ppermute | solution.py:720
  23.6 9.8 %collective-permute-start.8 = (bf16[64,1536]{1,0:T(8,128)(2,1)S(1)}, bf16[64,1536]{1,0:T(8,128)(2,1)S(1)}, u32[]{:S(2)}, u32[]{:S(2)}) collective-permute-start(bf16[64,1536]{1,0:T(8,128)(2,1)S(1)} %collective-permute-done.6.refs_4_), channel_id=1, source_target_pairs={{0,16},{1,17},{2,18},{3,19},{4,20},{5,21},{6,22},{7,23},{8,24},{9,... | collective-permute-start | bytes 589832 | tf_op jit(solution)/shard_map/ppermute | solution.py:720
  36.1 12.5 %collective-permute-start.11 = (bf16[128,1536]{1,0:T(8,128)(2,1)S(1)}, bf16[128,1536]{1,0:T(8,128)(2,1)S(1)}, u32[]{:S(2)}, u32[]{:S(2)}) collective-permute-start(bf16[128,1536]{1,0:T(8,128)(2,1)S(1)} %pad_maximum_fusion.refs_8_), channel_id=1, source_target_pairs={{0,8},{1,9},{2,10},{3,11},{4,12},{5,13},{6,14},{7,15},{8,0},{9,1},... | collective-permute-start | bytes 1179656 | tf_op jit(solution)/shard_map/ppermute | solution.py:720
  37.5 13.0 %collective-permute-start.12 = (bf16[128,1536]{1,0:T(8,128)(2,1)S(1)}, bf16[128,1536]{1,0:T(8,128)(2,1)S(1)}, u32[]{:S(2)}, u32[]{:S(2)}) collective-permute-start(bf16[128,1536]{1,0:T(8,128)(2,1)S(1)} %pad_maximum_fusion.refs_8_), channel_id=1, source_target_pairs={{0,16},{1,17},{2,18},{3,19},{4,20},{5,21},{6,22},{7,23},{8,24},{9,... | collective-permute-start | bytes 1179656 | tf_op jit(solution)/shard_map/ppermute | solution.py:720
  39.0 28.7 %collective-permute-start.15 = (bf16[704,384]{1,0:T(8,128)(2,1)}, bf16[704,384]{1,0:T(8,128)(2,1)S(1)}, u32[]{:S(2)}, u32[]{:S(2)}) collective-permute-start(bf16[704,384]{1,0:T(8,128)(2,1)} %release.5.refs_0_), channel_id=1, source_target_pairs={{0,2},{1,3},{2,0},{3,1},{4,6},{5,7},{6,4},{7,5},{8,10},{9,11},{10,... | collective-permute-start | bytes 1622024 | tf_op jit(solution)/shard_map/ppermute | solution.py:720
  41.8 13.8 %collective-permute-start.4 = (bf16[256,1024]{1,0:T(8,128)(2,1)S(1)}, bf16[256,1024]{1,0:T(8,128)(2,1)S(1)}, u32[]{:S(2)}, u32[]{:S(2)}) collective-permute-start(bf16[256,1024]{1,0:T(8,128)(2,1)S(1)} %copy-done.33), channel_id=1, source_target_pairs={{0,4},{1,5},{2,6},{3,7},{4,0},{5,1},{6,2},{7,3},{8,12},{9,13},{10,... | collective-permute-start | bytes 1572872 | tf_op jit(solution)/shard_map/ppermute | solution.py:720
  41.8 12.9 %collective-permute-start.5 = (bf16[64,1536]{1,0:T(8,128)(2,1)S(1)}, bf16[64,1536]{1,0:T(8,128)(2,1)S(1)}, u32[]{:S(2)}, u32[]{:S(2)}) collective-permute-start(bf16[64,1536]{1,0:T(8,128)(2,1)S(1)} %copy-done.37), channel_id=1, source_target_pairs={{0,16},{1,17},{2,18},{3,19},{4,20},{5,21},{6,22},{7,23},{8,24},{9,... | collective-permute-start | bytes 589832 | tf_op jit(solution)/shard_map/ppermute | solution.py:720
  50.5 17.2 %collective-permute-start.13 = (bf16[64,1536]{1,0:T(8,128)(2,1)S(1)}, bf16[64,1536]{1,0:T(8,128)(2,1)S(1)}, u32[]{:S(2)}, u32[]{:S(2)}) collective-permute-start(bf16[64,1536]{1,0:T(8,128)(2,1)S(1)} %slice.8), channel_id=1, source_target_pairs={{0,16},{1,17},{2,18},{3,19},{4,20},{5,21},{6,22},{7,23},{8,24},{9,... | collective-permute-start | bytes 589832 | tf_op jit(solution)/shard_map/ppermute | solution.py:720
  54.7 13.0 %collective-permute-start.14 = (bf16[64,1536]{1,0:T(8,128)(2,1)S(1)}, bf16[64,1536]{1,0:T(8,128)(2,1)S(1)}, u32[]{:S(2)}, u32[]{:S(2)}) collective-permute-start(bf16[64,1536]{1,0:T(8,128)(2,1)S(1)} %slice.9), channel_id=1, source_target_pairs={{0,8},{1,9},{2,10},{3,11},{4,12},{5,13},{6,14},{7,15},{8,0},{9,1},... | collective-permute-start | bytes 589832 | tf_op jit(solution)/shard_map/ppermute | solution.py:720
  77.0 24.0 %collective-permute-start.17 = (bf16[704,384]{1,0:T(8,128)(2,1)}, bf16[704,384]{1,0:T(8,128)(2,1)}, u32[]{:S(2)}, u32[]{:S(2)}) collective-permute-start(bf16[704,384]{1,0:T(8,128)(2,1)} %release.6.refs_1_), channel_id=1, source_target_pairs={{0,8},{1,9},{2,10},{3,11},{4,12},{5,13},{6,14},{7,15},{8,0},{9,1},... | collective-permute-start | bytes 1622024 | tf_op jit(solution)/shard_map/ppermute | solution.py:720
  77.6 23.5 %collective-permute-start.18 = (bf16[704,384]{1,0:T(8,128)(2,1)}, bf16[704,384]{1,0:T(8,128)(2,1)}, u32[]{:S(2)}, u32[]{:S(2)}) collective-permute-start(bf16[704,384]{1,0:T(8,128)(2,1)} %release.6.refs_1_), channel_id=1, source_target_pairs={{0,16},{1,17},{2,18},{3,19},{4,20},{5,21},{6,22},{7,23},{8,24},{9,... | collective-permute-start | bytes 1622024 | tf_op jit(solution)/shard_map/ppermute | solution.py:720
  78.1 25.4 %collective-permute-start.19 = (bf16[704,384]{1,0:T(8,128)(2,1)}, bf16[704,384]{1,0:T(8,128)(2,1)S(1)}, u32[]{:S(2)}, u32[]{:S(2)}) collective-permute-start(bf16[704,384]{1,0:T(8,128)(2,1)} %release.7.refs_5_), channel_id=1, source_target_pairs={{0,8},{1,9},{2,10},{3,11},{4,12},{5,13},{6,14},{7,15},{8,0},{9,1},... | collective-permute-start | bytes 1622024 | tf_op jit(solution)/shard_map/ppermute | solution.py:720
  79.6 24.3 %collective-permute-start.20 = (bf16[704,384]{1,0:T(8,128)(2,1)}, bf16[704,384]{1,0:T(8,128)(2,1)}, u32[]{:S(2)}, u32[]{:S(2)}) collective-permute-start(bf16[704,384]{1,0:T(8,128)(2,1)} %release.7.refs_5_), channel_id=1, source_target_pairs={{0,16},{1,17},{2,18},{3,19},{4,20},{5,21},{6,22},{7,23},{8,24},{9,... | collective-permute-start | bytes 1622024 | tf_op jit(solution)/shard_map/ppermute | solution.py:720
  85.7 18.4 %collective-permute-start.22 = (bf16[704,384]{1,0:T(8,128)(2,1)S(1)}, bf16[704,384]{1,0:T(8,128)(2,1)}, u32[]{:S(2)}, u32[]{:S(2)}) collective-permute-start(bf16[704,384]{1,0:T(8,128)(2,1)S(1)} %copy-done.12), channel_id=1, source_target_pairs={{0,4},{1,5},{2,6},{3,7},{4,0},{5,1},{6,2},{7,3},{8,12},{9,13},{10,... | collective-permute-start | bytes 1622024 | tf_op jit(solution)/shard_map/ppermute | solution.py:720
  97.1 55.0 %all-to-all-start = ((bf16[4,1632,128]{2,1,0:T(8,128)(2,1)}), bf16[4,1632,128]{2,1,0:T(8,128)(2,1)S(1)}, u32[]{:S(2)}, u32[]{:S(2)}) async-start(bf16[4,1632,128]{2,1,0:T(8,128)(2,1)} %stats.1.refs_0_), calls=%async_computation | async-start | bytes 3342336 | tf_op jit(solution)/shard_map/all_to_all | solution.py:816
  101.0 15.5 %collective-permute-start.25 = (bf16[704,384]{1,0:T(8,128)(2,1)}, bf16[704,384]{1,0:T(8,128)(2,1)S(1)}, u32[]{:S(2)}, u32[]{:S(2)}) collective-permute-start(bf16[704,384]{1,0:T(8,128)(2,1)} %release.7.refs_5_), channel_id=1, source_target_pairs={{0,4},{1,5},{2,6},{3,7},{4,0},{5,1},{6,2},{7,3},{8,12},{9,13},{10,... | collective-permute-start | bytes 1622024 | tf_op jit(solution)/shard_map/ppermute | solution.py:720
  101.1 15.8 %collective-permute-start.21 = (bf16[704,384]{1,0:T(8,128)(2,1)}, bf16[704,384]{1,0:T(8,128)(2,1)}, u32[]{:S(2)}, u32[]{:S(2)}) collective-permute-start(bf16[704,384]{1,0:T(8,128)(2,1)} %collective-permute-done.17.refs_1_.refs_2_), channel_id=1, source_target_pairs={{0,16},{1,17},{2,18},{3,19},{4,20},{5,21},{6,22},{7,23},{8,24},{9,... | collective-permute-start | bytes 1622024 | tf_op jit(solution)/shard_map/ppermute | solution.py:720
  103.5 13.9 %collective-permute-start.23 = (bf16[704,384]{1,0:T(8,128)(2,1)}, bf16[704,384]{1,0:T(8,128)(2,1)S(1)}, u32[]{:S(2)}, u32[]{:S(2)}) collective-permute-start(bf16[704,384]{1,0:T(8,128)(2,1)} %collective-permute-done.17.refs_1_.refs_2_), channel_id=1, source_target_pairs={{0,4},{1,5},{2,6},{3,7},{4,0},{5,1},{6,2},{7,3},{8,12},{9,13},{10,... | collective-permute-start | bytes 1622024 | tf_op jit(solution)/shard_map/ppermute | solution.py:720
  103.9 17.3 %collective-permute-start.24 = (bf16[704,384]{1,0:T(8,128)(2,1)}, bf16[704,384]{1,0:T(8,128)(2,1)}, u32[]{:S(2)}, u32[]{:S(2)}) collective-permute-start(bf16[704,384]{1,0:T(8,128)(2,1)} %collective-permute-done.18.refs_2_.refs_3_), channel_id=1, source_target_pairs={{0,4},{1,5},{2,6},{3,7},{4,0},{5,1},{6,2},{7,3},{8,12},{9,13},{10,... | collective-permute-start | bytes 1622024 | tf_op jit(solution)/shard_map/ppermute | solution.py:720
  104.1 16.8 %collective-permute-start.26 = (bf16[704,384]{1,0:T(8,128)(2,1)}, bf16[704,384]{1,0:T(8,128)(2,1)S(1)}, u32[]{:S(2)}, u32[]{:S(2)}) collective-permute-start(bf16[704,384]{1,0:T(8,128)(2,1)} %collective-permute-done.20.refs_3_.refs_7_), channel_id=1, source_target_pairs={{0,8},{1,9},{2,10},{3,11},{4,12},{5,13},{6,14},{7,15},{8,0},{9,1},... | collective-permute-start | bytes 1622024 | tf_op jit(solution)/shard_map/ppermute | solution.py:720
  116.6 16.1 %collective-permute-start.29 = (bf16[704,384]{1,0:T(8,128)(2,1)}, bf16[704,384]{1,0:T(8,128)(2,1)}, u32[]{:S(2)}, u32[]{:S(2)}) collective-permute-start(bf16[704,384]{1,0:T(8,128)(2,1)} %collective-permute-done.20.refs_3_.refs_7_), channel_id=1, source_target_pairs={{0,4},{1,5},{2,6},{3,7},{4,0},{5,1},{6,2},{7,3},{8,12},{9,13},{10,... | collective-permute-start | bytes 1622024 | tf_op jit(solution)/shard_map/ppermute | solution.py:720
  116.9 15.8 %collective-permute-start.28 = (bf16[704,384]{1,0:T(8,128)(2,1)S(1)}, bf16[704,384]{1,0:T(8,128)(2,1)}, u32[]{:S(2)}, u32[]{:S(2)}) collective-permute-start(bf16[704,384]{1,0:T(8,128)(2,1)S(1)} %collective-permute-done.19.refs_2_.refs_6_), channel_id=1, source_target_pairs={{0,4},{1,5},{2,6},{3,7},{4,0},{5,1},{6,2},{7,3},{8,12},{9,13},{10,... | collective-permute-start | bytes 1622024 | tf_op jit(solution)/shard_map/ppermute | solution.py:720
  118.2 14.5 %collective-permute-start.27 = (bf16[704,384]{1,0:T(8,128)(2,1)}, bf16[704,384]{1,0:T(8,128)(2,1)}, u32[]{:S(2)}, u32[]{:S(2)}) collective-permute-start(bf16[704,384]{1,0:T(8,128)(2,1)} %collective-permute-done.21.refs_4_), channel_id=1, source_target_pairs={{0,4},{1,5},{2,6},{3,7},{4,0},{5,1},{6,2},{7,3},{8,12},{9,13},{10,... | collective-permute-start | bytes 1622024 | tf_op jit(solution)/shard_map/ppermute | solution.py:720
  120.9 16.5 %collective-permute-start.31 = (bf16[704,384]{1,0:T(8,128)(2,1)S(1)}, bf16[704,384]{1,0:T(8,128)(2,1)S(1)}, u32[]{:S(2)}, u32[]{:S(2)}) collective-permute-start(bf16[704,384]{1,0:T(8,128)(2,1)S(1)} %collective-permute-done.26.refs_0_.refs_8_), channel_id=1, source_target_pairs={{0,4},{1,5},{2,6},{3,7},{4,0},{5,1},{6,2},{7,3},{8,12},{9,13},{10,... | collective-permute-start | bytes 1622024 | tf_op jit(solution)/shard_map/ppermute | solution.py:720
  121.2 16.2 %collective-permute-start.30 = (bf16[128,1024]{1,0:T(8,128)(2,1)S(1)}, bf16[128,1024]{1,0:T(8,128)(2,1)S(1)}, u32[]{:S(2)}, u32[]{:S(2)}) collective-permute-start(bf16[128,1024]{1,0:T(8,128)(2,1)S(1)} %get-tuple-element.49.refs_1_.refs_0_), channel_id=1, source_target_pairs={{0,1},{1,0},{2,3},{3,2},{4,5},{5,4},{6,7},{7,6},{8,9},{9,8},{10,11... | collective-permute-start | bytes 786440 | tf_op jit(solution)/shard_map/ppermute | solution.py:720
  135.9 9.7 %collective-permute-start.32 = (bf16[128,1024]{1,0:T(8,128)(2,1)S(1)}, bf16[128,1024]{1,0:T(8,128)(2,1)S(1)}, u32[]{:S(2)}, u32[]{:S(2)}) collective-permute-start(bf16[128,1024]{1,0:T(8,128)(2,1)S(1)} %get-tuple-element.50.refs_1_), channel_id=1, source_target_pairs={{0,1},{1,0},{2,3},{3,2},{4,5},{5,4},{6,7},{7,6},{8,9},{9,8},{10,11... | collective-permute-start | bytes 786440 | tf_op jit(solution)/shard_map/ppermute | solution.py:720
  144.1 11.4 %collective-permute-start.33 = (bf16[128,1024]{1,0:T(8,128)(2,1)S(1)}, bf16[128,1024]{1,0:T(8,128)(2,1)S(1)}, u32[]{:S(2)}, u32[]{:S(2)}) collective-permute-start(bf16[128,1024]{1,0:T(8,128)(2,1)S(1)} %get-tuple-element.54.refs_4_), channel_id=1, source_target_pairs={{0,1},{1,0},{2,3},{3,2},{4,5},{5,4},{6,7},{7,6},{8,9},{9,8},{10,11... | collective-permute-start | bytes 786440 | tf_op jit(solution)/shard_map/ppermute | solution.py:720
  148.0 9.7 %collective-permute-start.34 = (bf16[128,1024]{1,0:T(8,128)(2,1)S(1)}, bf16[128,1024]{1,0:T(8,128)(2,1)S(1)}, u32[]{:S(2)}, u32[]{:S(2)}) collective-permute-start(bf16[128,1024]{1,0:T(8,128)(2,1)S(1)} %ffn_second.2.refs_5_), channel_id=1, source_target_pairs={{0,1},{1,0},{2,3},{3,2},{4,5},{5,4},{6,7},{7,6},{8,9},{9,8},{10,11... | collective-permute-start | bytes 786440 | tf_op jit(solution)/shard_map/ppermute | solution.py:720
  (48 other events, 362.0 us)
Sparse Core Ops, SparseCore 0:
  10.9 75.3 all-gather.1

commit v2 on v1

--- a/solution.py
+++ b/solution.py
@@ -451,10 +451,14 @@
         system = []
         for i, h in enumerate(hs):
             m = jnp.concatenate([s_ref[0, h].astype(BF16), keys_t[i]], axis=1)
-            system.append(jnp.concatenate([m, m], axis=0))
+            system.append(m)
 
         def both_terms(field):
-            return jnp.concatenate(two_terms(field), axis=1)
+            return jnp.concatenate(two_terms(field), axis=0)
+
+        def joined(products):
+            rows = products.shape[0] // 2
+            return products[:rows] + products[rows:]
 
         def scored(products, i, h):
             scores = products[:, size:] * w_ref[0, h]
@@ -467,7 +471,7 @@
         norm = [lane_sum(r * r) for r in residual]
         for it in range(ITERS):
             products = [
-                jnp.dot(both_terms(direction[i]), system[i], preferred_element_type=F32)
+                joined(jnp.dot(both_terms(direction[i]), system[i], preferred_element_type=F32))
                 for i in range(group)
             ]
             spread = [
@@ -488,9 +492,10 @@
                     norm[i] = following
         for i, h in enumerate(hs):
             start_m = jnp.concatenate([vs_ref[0, h].astype(BF16), keys2_bf[i]], axis=0)
-            start_m = jnp.concatenate([start_m, start_m], axis=1)
-            products = lax.dot_general(
-                both_terms(total[i]), start_m, transposed, preferred_element_type=F32
+            products = joined(
+                lax.dot_general(
+                    both_terms(total[i]), start_m, transposed, preferred_element_type=F32
+                )
             )
             values = part(v_ref, h)
             values2 = jnp.concatenate([values, values], axis=0).astype(BF16)

time: 166 us -> 165 us (level)
  Pallas kernels: 69.9 us -> 67.8 us
    pallas_call x2, Pallas kernels: 21.9 us -> 19.9 us  [cg_call(): pl.pallas_call(functools.partial(cg_kernel, heads, 8), grid=(count,), in_...]
  transfers between devices with their start and end apart: 37 -> 37, of which waited for: 11 -> 12; matrix products, arithmetic and copies ran while one was open for 2% -> 2% of each run, Pallas kernels for 42% -> 41%
where the time goes in v2:
time: 165 us
  Pallas kernels  67.8 us (41%)
  starting transfers between devices  39 us (24%)
  waiting for transfers between devices  30.8 us (19%)
  between operations  14.5 us (9%)
  local copies, waits for them, and re-layouts  11.4 us (7%)
    ppermute x35, starting transfers between devices, shards(): move = lambda value, pairs: lax.ppermute(value, AXES, pairs)  35.1 us
    ppermute x35, waiting for transfers between devices, shards(): move = lambda value, pairs: lax.ppermute(value, AXES, pairs)  30.1 us
    pallas_call x2, Pallas kernels, cg_call(): pl.pallas_call(functools.partial(cg_kernel, heads, 8), grid=(count,), in_...  19.9 us
    unnamed x89, local copies, waits for them, and re-layouts  11.4 us
    pallas_call x2, Pallas kernels, conv_call(): pl.pallas_call(conv_kernel, grid_spec=pltpu.PrefetchScalarGridSpec(num_sc...  9.14 us
    pallas_call x1, Pallas kernels, project_call(): pl.pallas_call(functools.partial(project_kernel, len(pieces), spans), gri...  6.86 us
    pallas_call x1, Pallas kernels, stats_call(): pl.pallas_call(functools.partial(stats_kernel, heads), grid_spec=pltpu.Pr...  5.94 us
    pallas_call x1, Pallas kernels, ffn_first_call(): pl.pallas_call(functools.partial(ffn_first_kernel, spans, counts), grid_s...  5.89 us
  transfers between devices with their start and end apart: 37, of which 12 were waited for; matrix products, arithmetic and copies ran while one was open for 2% of the time, Pallas kernels for 41%

profile of v2, /device:TPU:0, one launch (start us, length us, event | category | flops | bytes accessed | tf_op | source)
XLA Modules:
  0.0 164.7 jit_solution(5137564007000110272)
XLA Ops:
  7.9 1.6 split_heads.1
  11.1 3.0 %collective-permute-start.6 = (bf16[64,1536]{1,0:T(8,128)(2,1)S(1)}, bf16[64,1536]{1,0:T(8,128)(2,1)S(1)}, u32[]{:S(2)}, u32[]{:S(2)}) collective-permute-start(bf16[64,1536]{1,0:T(8,128)(2,1)S(1)} %constant_dynamic-update-slice_fusion.refs_0_), channel_id=1, source_target_pairs={{0,1},{1,2},{2,3},{3,0},{4,5},{5,6},{6,7},{7,4},{8,9},{9,10},{10,1... | collective-permute-start | bytes 589832 | tf_op jit(solution)/shard_map/ppermute | solution.py:725
  14.1 2.1 %collective-permute-start.1 = (bf16[64,1536]{1,0:T(8,128)(2,1)S(1)}, bf16[64,1536]{1,0:T(8,128)(2,1)S(1)}, u32[]{:S(2)}, u32[]{:S(2)}) collective-permute-start(bf16[64,1536]{1,0:T(8,128)(2,1)S(1)} %constant_dynamic-update-slice_fusion.refs_0_), channel_id=1, source_target_pairs={{0,3},{1,0},{2,1},{3,2},{4,7},{5,4},{6,5},{7,6},{8,11},{9,8},{10,9... | collective-permute-start | bytes 589832 | tf_op jit(solution)/shard_map/ppermute | solution.py:725
  16.2 1.6 %collective-permute-start.2 = (bf16[64,1536]{1,0:T(8,128)(2,1)S(1)}, bf16[64,1536]{1,0:T(8,128)(2,1)S(1)}, u32[]{:S(2)}, u32[]{:S(2)}) collective-permute-start(bf16[64,1536]{1,0:T(8,128)(2,1)S(1)} %constant_dynamic-update-slice_fusion.refs_0_), channel_id=1, source_target_pairs={{0,8},{1,9},{2,10},{3,11},{4,12},{5,13},{6,14},{7,15},{8,0},{9,1},... | collective-permute-start | bytes 589832 | tf_op jit(solution)/shard_map/ppermute | solution.py:725
  17.9 1.5 collective-permute-start.3
  19.4 2.5 %collective-permute-done.6.refs_4_ = bf16[64,1536]{1,0:T(8,128)(2,1)S(1)} collective-permute-done((bf16[64,1536]{1,0:T(8,128)(2,1)S(1)}, bf16[64,1536]{1,0:T(8,128)(2,1)S(1)}, u32[]{:S(2)}, u32[]{:S(2)}) %collective-permute-start.6) | collective-permute-done | bytes 196640 | tf_op jit(solution)/shard_map/ppermute | solution.py:725
  21.9 1.7 %collective-permute-start.7 = (bf16[64,1536]{1,0:T(8,128)(2,1)S(1)}, bf16[64,1536]{1,0:T(8,128)(2,1)S(1)}, u32[]{:S(2)}, u32[]{:S(2)}) collective-permute-start(bf16[64,1536]{1,0:T(8,128)(2,1)S(1)} %collective-permute-done.6.refs_4_), channel_id=1, source_target_pairs={{0,8},{1,9},{2,10},{3,11},{4,12},{5,13},{6,14},{7,15},{8,0},{9,1},... | collective-permute-start | bytes 589832 | tf_op jit(solution)/shard_map/ppermute | solution.py:725
  23.6 1.5 collective-permute-start.8
  28.2 5.1 %norm_gates.1 = (bf16[704,384]{1,0:T(8,128)(2,1)}, bf16[256,1024]{1,0:T(8,128)(2,1)}, f32[4,8,64,128]{3,2,1,0:T(8,128)}, f32[4,8,64,128]{3,2,1,0:T(8,128)}, f32[...) custom-call(s32[4]{0:T(128)S(1)} %copy-done.6, ...), custom_call_target="tpu_custom_call", output_to_operand_aliasing={{6}: (8, {})} | custom-call | flops 3221225472 | bytes 65536 | tf_op jit(solution)/shard_map/norm_gates/pallas_call | solution.py:142
  39.0 2.8 %collective-permute-start.15 = (bf16[704,384]{1,0:T(8,128)(2,1)}, bf16[704,384]{1,0:T(8,128)(2,1)S(1)}, u32[]{:S(2)}, u32[]{:S(2)}) collective-permute-start(bf16[704,384]{1,0:T(8,128)(2,1)} %release.5.refs_0_), channel_id=1, source_target_pairs={{0,2},{1,3},{2,0},{3,1},{4,6},{5,7},{6,4},{7,5},{8,10},{9,11},{10,... | collective-permute-start | bytes 1622024 | tf_op jit(solution)/shard_map/ppermute | solution.py:725
  41.8 1.6 collective-permute-start.5
  43.4 5.3 %collective-permute-done.11.refs_9_ = bf16[128,1536]{1,0:T(8,128)(2,1)S(1)} collective-permute-done((bf16[128,1536]{1,0:T(8,128)(2,1)S(1)}, bf16[128,1536]{1,0:T(8,128)(2,1)S(1)}, u32[]{:S(2)}, u32[]{:S(2)}) %collective-permute-start.11) | collective-permute-done | bytes 393248 | tf_op jit(solution)/shard_map/ppermute | solution.py:725
  51.8 2.9 %collective-permute-done.5.refs_3_ = bf16[64,1536]{1,0:T(8,128)(2,1)S(1)} collective-permute-done((bf16[64,1536]{1,0:T(8,128)(2,1)S(1)}, bf16[64,1536]{1,0:T(8,128)(2,1)S(1)}, u32[]{:S(2)}, u32[]{:S(2)}) %collective-permute-start.5) | collective-permute-done | bytes 196640 | tf_op jit(solution)/shard_map/ppermute | solution.py:725
  55.5 12.1 %collective-permute-done.15.refs_13_.refs_0_ = bf16[704,384]{1,0:T(8,128)(2,1)S(1)} collective-permute-done((bf16[704,384]{1,0:T(8,128)(2,1)}, bf16[704,384]{1,0:T(8,128)(2,1)S(1)}, u32[]{:S(2)}, u32[]{:S(2)}) %collective-permute-start.15) | collective-permute-done | bytes 540704 | tf_op jit(solution)/shard_map/ppermute | solution.py:725
  69.3 6.9 %project.1 = (bf16[256,1536]{1,0:T(8,128)(2,1)}, bf16[256,1536]{1,0:T(8,128)(2,1)}) custom-call(s32[32]{0:T(128)S(1)} %fusion.2.at_ref, bf16[256,1024]{1,0:T(8,128)(2,1)} %get-tuple-element.35.x_ref, bf16[256,1024]{1,0:T(8,128)(2,1)} %copy-done.34, bf16[64,1536]{1,0:T(8,128)(2,1)} %copy-done.27, bf16[64,1536]{1,0:T(8,128)(2,1)} %copy-done.36, ...), custom_call_target="tpu_custom_call" | custom-call | flops 3221225472 | bytes 65536 | tf_op jit(solution)/shard_map/project/pallas_call | solution.py:220
  79.6 1.6 collective-permute-start.20
  81.2 4.6 %conv_norm.2 = (f32[256,3072]{1,0:T(8,128)}, bf16[4,3,3072]{2,1,0:T(4,128)(2,1)}) custom-call(s32[1]{0:T(128)} %bitcast.core_ref.half_ref, s32[4]{0:T(128)S(1)} %copy-done.7, bf16[256,1536]{1,0:T(8,128)(2,1)} %get-tuple-element.39.projected_ref, bf16[4,3,3072]{2,1,0:T(4,128)(2,1)} %copy.34.tail_ref, f32[4,3072]{1,0:T(4,128)} %conv_ref.3), custom_call_target="tpu_custom_call" | custom-call | flops 2147483648 | bytes 65536 | tf_op jit(solution)/shard_map/conv_norm/pallas_call | solution.py:273
  86.6 4.6 %conv_norm.3 = (f32[256,3072]{1,0:T(8,128)}, bf16[4,3,3072]{2,1,0:T(4,128)(2,1)}) custom-call(s32[1]{0:T(128)S(6)} %sub.13.half_ref, s32[4]{0:T(128)S(1)} %copy-done.7, bf16[256,1536]{1,0:T(8,128)(2,1)} %copy-done.30, bf16[4,3,3072]{2,1,0:T(4,128)(2,1)} %copy.34.tail_ref, f32[4,3072]{1,0:T(4,128)} %conv_ref.3, ...), custom_call_target="tpu_custom_call", output_to_operand_aliasing={{0}: (5, {}), {1}: (6, {})} | custom-call | flops 2147483648 | bytes 65536 | tf_op jit(solution)/shard_map/conv_norm/pallas_call | solution.py:273
  91.2 5.9 %stats.1.refs_0_ = bf16[4,1632,128]{2,1,0:T(8,128)(2,1)} custom-call(s32[4]{0:T(128)S(1)} %get-tuple-element.67.place_ref, s32[4]{0:T(128)S(1)} %get-tuple-element.66.slot_ref, f32[256,3072]{1,0:T(8,128)} %get-tuple-element.42.k_ref.v_ref.q_ref, f32[256,3072]{1,0:T(8,128)} %get-tuple-element.42.k_ref.v_ref.q_ref, ...), custom_call_target="tpu_custom_call" | custom-call | flops 3221225472 | bytes 65536 | tf_op jit(solution)/shard_map/stats/pallas_call | solution.py:337
  97.1 3.9 %all-to-all-start = ((bf16[4,1632,128]{2,1,0:T(8,128)(2,1)}), bf16[4,1632,128]{2,1,0:T(8,128)(2,1)S(1)}, u32[]{:S(2)}, u32[]{:S(2)}) async-start(bf16[4,1632,128]{2,1,0:T(8,128)(2,1)} %stats.1.refs_0_), calls=%async_computation | async-start | bytes 3342336 | tf_op jit(solution)/shard_map/all_to_all | solution.py:821
  101.6 1.9 %collective-permute-done.19.refs_2_.refs_6_ = bf16[704,384]{1,0:T(8,128)(2,1)S(1)} collective-permute-done((bf16[704,384]{1,0:T(8,128)(2,1)}, bf16[704,384]{1,0:T(8,128)(2,1)S(1)}, u32[]{:S(2)}, u32[]{:S(2)}) %collective-permute-start.19) | collective-permute-done | bytes 540704 | tf_op jit(solution)/shard_map/ppermute | solution.py:725
  105.6 10.0 %cg.2.x_ref.refs_0_ = bf16[256,1024]{1,0:T(8,128)(2,1)} custom-call(f32[8]{0:T(128)S(1)} %copy-done.2, f32[256,3072]{1,0:T(8,128)} %get-tuple-element.42.k_ref.v_ref.q_ref, f32[256,3072]{1,0:T(8,128)} %get-tuple-element.42.k_ref.v_ref.q_ref, f32[256,3072]{1,0:T(8,128)} %get-tuple-element.42.k_ref.v_ref.q_ref, f32[4,8,64,128]{3,2,1,0:T(8,128)} %get-tuple-element.43.w_ref, ...), custom_call_target="tpu_custom_call" | custom-call | flops 4294967296 | bytes 65536 | tf_op jit(solution)/shard_map/cg/pallas_call | solution.py:514
  117.5 2.4 %out_proj.2 = (bf16[128,1024]{1,0:T(8,128)(2,1)S(1)}, bf16[128,1024]{1,0:T(8,128)(2,1)S(1)}) custom-call(bf16[256,1024]{1,0:T(8,128)(2,1)} %cg.2.x_ref.refs_0_, bf16[256,1024]{1,0:T(8,128)(2,1)} %bitcast.11, f32[1,1024]{1,0:T(1,128)} %bitcast.17, bf16[1024,1024]{1,0:T(8,128)(2,1)} %all-gather.2.cloned.1.call-done.w_ref), custom_call_target="tpu_custom_call" | custom-call | flops 2147483648 | bytes 65536 | tf_op jit(solution)/shard_map/out_proj/pallas_call | solution.py:559
  120.2 1.5 collective-permute-start.30
  121.8 10.0 %cg.3.x_ref = bf16[256,1024]{1,0:T(8,128)(2,1)} custom-call(f32[8]{0:T(128)S(1)} %copy-done.2, f32[256,3072]{1,0:T(8,128)} %get-tuple-element.42.k_ref.v_ref.q_ref, f32[256,3072]{1,0:T(8,128)} %get-tuple-element.42.k_ref.v_ref.q_ref, f32[256,3072]{1,0:T(8,128)} %get-tuple-element.42.k_ref.v_ref.q_ref, ...), custom_call_target="tpu_custom_call", output_to_operand_aliasing={{}: (8, {})} | custom-call | flops 4294967296 | bytes 65536 | tf_op jit(solution)/shard_map/cg/pallas_call | solution.py:514
  131.8 2.4 %out_proj.3 = (bf16[128,1024]{1,0:T(8,128)(2,1)S(1)}, bf16[128,1024]{1,0:T(8,128)(2,1)S(1)}) custom-call(bf16[256,1024]{1,0:T(8,128)(2,1)} %cg.3.x_ref, bf16[256,1024]{1,0:T(8,128)(2,1)} %bitcast.12, f32[1,1024]{1,0:T(1,128)} %bitcast.18, bf16[1024,1024]{1,0:T(8,128)(2,1)} %all-gather.2.cloned.1.call-done.w_ref, bf16[704,384]{1,0:T(8,128)(2,1)} %copy-done.31, ...), custom_call_target="tpu_custom_call" | custom-call | flops 2147483648 | bytes 65536 | tf_op jit(solution)/shard_map/out_proj/pallas_call | solution.py:559
  136.2 5.9 %ffn_first.1 = (bf16[128,1024]{1,0:T(8,128)(2,1)S(1)}, bf16[2,704,1024]{2,1,0:T(8,128)(2,1)S(1)}, bf16[2,704,1024]{2,1,0:T(8,128)(2,1)S(1)}, bf16[2,704,1024]{2,1,0:T(8,128)(2,1)S(1)}) custom-call(s32[8]{0:T(128)S(1)} %broadcast_xor_fusion.order_ref, bf16[128,1024]{1,0:T(8,128)(2,1)S(1)} %collective-permute-done.30.refs_0_, ...), custom_call_target="tpu_custom_call" | custom-call | flops 5368709120 | bytes 65536 | tf_op jit(solution)/shard_map/ffn_first/pallas_call | solution.py:632
  142.1 1.6 collective-permute-start.33
  143.7 2.0 %collective-permute-done.32.refs_0_ = bf16[128,1024]{1,0:T(8,128)(2,1)S(1)} collective-permute-done((bf16[128,1024]{1,0:T(8,128)(2,1)S(1)}, bf16[128,1024]{1,0:T(8,128)(2,1)S(1)}, u32[]{:S(2)}, u32[]{:S(2)}) %collective-permute-start.32) | collective-permute-done | bytes 262176 | tf_op jit(solution)/shard_map/ppermute | solution.py:725
  145.7 2.3 %ffn_second.2.refs_5_ = bf16[128,1024]{1,0:T(8,128)(2,1)S(1)} custom-call(bf16[128,1024]{1,0:T(8,128)(2,1)S(1)} %collective-permute-done.32.refs_0_, bf16[2,704,1024]{2,1,0:T(8,128)(2,1)S(1)} %get-tuple-element.51.refs_1_.refs_2_, bf16[2,704,1024]{2,1,0:T(8,128)(2,1)S(1)} %get-tuple-element.52.refs_2_.refs_3_, ...), custom_call_target="tpu_custom_call" | custom-call | flops 3221225472 | bytes 65536 | tf_op jit(solution)/shard_map/ffn_second/pallas_call | solution.py:664
  148.8 2.6 %ffn_second.3 = (f32[128,1024]{1,0:T(8,128)S(1)}, f32[128,1024]{1,0:T(8,128)S(1)}) custom-call(bf16[128,1024]{1,0:T(8,128)(2,1)S(1)} %copy-done.1, bf16[128,1024]{1,0:T(8,128)(2,1)S(1)} %get-tuple-element.50.refs_1_, bf16[2,704,1024]{2,1,0:T(8,128)(2,1)S(1)} %get-tuple-element.51.refs_1_.refs_2_, ...), custom_call_target="tpu_custom_call" | custom-call | flops 3221225472 | bytes 65536 | tf_op jit(solution)/shard_map/ffn_second/pallas_call | solution.py:664
  152.2 2.7 %unpack.1 = (f32[4,8,128,128]{3,2,1,0:T(8,128)}, f32[4,8,128,128]{3,2,1,0:T(8,128)}, bf16[4,3,3072]{2,1,0:T(4,128)(2,1)S(1)}) custom-call(bf16[4,1632,128]{2,1,0:T(8,128)(2,1)S(1)} %all-to-all-done.part_ref, f32[128,1024]{1,0:T(8,128)} %copy-done.8), custom_call_target="tpu_custom_call" | custom-call | flops 3221225472 | bytes 65536 | tf_op jit(solution)/shard_map/unpack/pallas_call | solution.py:412
  (158 shorter events, 32.1 us)
Async XLA Ops:
  7.2 110.3 %all-gather.2.cloned.1.call-start = ((), (), s32[]{:S(2)}) async-start(), calls=%async_computation.1 | async-start | bytes 2162688 | tf_op jit(solution)/shard_map/all_gather | solution.py:729
  11.1 10.7 %collective-permute-start.6 = (bf16[64,1536]{1,0:T(8,128)(2,1)S(1)}, bf16[64,1536]{1,0:T(8,128)(2,1)S(1)}, u32[]{:S(2)}, u32[]{:S(2)}) collective-permute-start(bf16[64,1536]{1,0:T(8,128)(2,1)S(1)} %constant_dynamic-update-slice_fusion.refs_0_), channel_id=1, source_target_pairs={{0,1},{1,2},{2,3},{3,0},{4,5},{5,6},{6,7},{7,4},{8,9},{9,10},{10,1... | collective-permute-start | bytes 589832 | tf_op jit(solution)/shard_map/ppermute | solution.py:725
  14.1 11.0 %collective-permute-start.1 = (bf16[64,1536]{1,0:T(8,128)(2,1)S(1)}, bf16[64,1536]{1,0:T(8,128)(2,1)S(1)}, u32[]{:S(2)}, u32[]{:S(2)}) collective-permute-start(bf16[64,1536]{1,0:T(8,128)(2,1)S(1)} %constant_dynamic-update-slice_fusion.refs_0_), channel_id=1, source_target_pairs={{0,3},{1,0},{2,1},{3,2},{4,7},{5,4},{6,5},{7,6},{8,11},{9,8},{10,9... | collective-permute-start | bytes 589832 | tf_op jit(solution)/shard_map/ppermute | solution.py:725
  16.2 9.9 %collective-permute-start.2 = (bf16[64,1536]{1,0:T(8,128)(2,1)S(1)}, bf16[64,1536]{1,0:T(8,128)(2,1)S(1)}, u32[]{:S(2)}, u32[]{:S(2)}) collective-permute-start(bf16[64,1536]{1,0:T(8,128)(2,1)S(1)} %constant_dynamic-update-slice_fusion.refs_0_), channel_id=1, source_target_pairs={{0,8},{1,9},{2,10},{3,11},{4,12},{5,13},{6,14},{7,15},{8,0},{9,1},... | collective-permute-start | bytes 589832 | tf_op jit(solution)/shard_map/ppermute | solution.py:725
  21.9 11.5 %collective-permute-start.7 = (bf16[64,1536]{1,0:T(8,128)(2,1)S(1)}, bf16[64,1536]{1,0:T(8,128)(2,1)S(1)}, u32[]{:S(2)}, u32[]{:S(2)}) collective-permute-start(bf16[64,1536]{1,0:T(8,128)(2,1)S(1)} %collective-permute-done.6.refs_4_), channel_id=1, source_target_pairs={{0,8},{1,9},{2,10},{3,11},{4,12},{5,13},{6,14},{7,15},{8,0},{9,1},... | collective-permute-start | bytes 589832 | tf_op jit(solution)/shard_map/ppermute | solution.py:725
  23.6 9.8 %collective-permute-start.8 = (bf16[64,1536]{1,0:T(8,128)(2,1)S(1)}, bf16[64,1536]{1,0:T(8,128)(2,1)S(1)}, u32[]{:S(2)}, u32[]{:S(2)}) collective-permute-start(bf16[64,1536]{1,0:T(8,128)(2,1)S(1)} %collective-permute-done.6.refs_4_), channel_id=1, source_target_pairs={{0,16},{1,17},{2,18},{3,19},{4,20},{5,21},{6,22},{7,23},{8,24},{9,... | collective-permute-start | bytes 589832 | tf_op jit(solution)/shard_map/ppermute | solution.py:725
  36.1 12.5 %collective-permute-start.11 = (bf16[128,1536]{1,0:T(8,128)(2,1)S(1)}, bf16[128,1536]{1,0:T(8,128)(2,1)S(1)}, u32[]{:S(2)}, u32[]{:S(2)}) collective-permute-start(bf16[128,1536]{1,0:T(8,128)(2,1)S(1)} %pad_maximum_fusion.refs_8_), channel_id=1, source_target_pairs={{0,8},{1,9},{2,10},{3,11},{4,12},{5,13},{6,14},{7,15},{8,0},{9,1},... | collective-permute-start | bytes 1179656 | tf_op jit(solution)/shard_map/ppermute | solution.py:725
  37.5 13.0 %collective-permute-start.12 = (bf16[128,1536]{1,0:T(8,128)(2,1)S(1)}, bf16[128,1536]{1,0:T(8,128)(2,1)S(1)}, u32[]{:S(2)}, u32[]{:S(2)}) collective-permute-start(bf16[128,1536]{1,0:T(8,128)(2,1)S(1)} %pad_maximum_fusion.refs_8_), channel_id=1, source_target_pairs={{0,16},{1,17},{2,18},{3,19},{4,20},{5,21},{6,22},{7,23},{8,24},{9,... | collective-permute-start | bytes 1179656 | tf_op jit(solution)/shard_map/ppermute | solution.py:725
  39.0 28.7 %collective-permute-start.15 = (bf16[704,384]{1,0:T(8,128)(2,1)}, bf16[704,384]{1,0:T(8,128)(2,1)S(1)}, u32[]{:S(2)}, u32[]{:S(2)}) collective-permute-start(bf16[704,384]{1,0:T(8,128)(2,1)} %release.5.refs_0_), channel_id=1, source_target_pairs={{0,2},{1,3},{2,0},{3,1},{4,6},{5,7},{6,4},{7,5},{8,10},{9,11},{10,... | collective-permute-start | bytes 1622024 | tf_op jit(solution)/shard_map/ppermute | solution.py:725
  41.8 13.8 %collective-permute-start.4 = (bf16[256,1024]{1,0:T(8,128)(2,1)S(1)}, bf16[256,1024]{1,0:T(8,128)(2,1)S(1)}, u32[]{:S(2)}, u32[]{:S(2)}) collective-permute-start(bf16[256,1024]{1,0:T(8,128)(2,1)S(1)} %copy-done.33), channel_id=1, source_target_pairs={{0,4},{1,5},{2,6},{3,7},{4,0},{5,1},{6,2},{7,3},{8,12},{9,13},{10,... | collective-permute-start | bytes 1572872 | tf_op jit(solution)/shard_map/ppermute | solution.py:725
  41.8 12.9 %collective-permute-start.5 = (bf16[64,1536]{1,0:T(8,128)(2,1)S(1)}, bf16[64,1536]{1,0:T(8,128)(2,1)S(1)}, u32[]{:S(2)}, u32[]{:S(2)}) collective-permute-start(bf16[64,1536]{1,0:T(8,128)(2,1)S(1)} %copy-done.37), channel_id=1, source_target_pairs={{0,16},{1,17},{2,18},{3,19},{4,20},{5,21},{6,22},{7,23},{8,24},{9,... | collective-permute-start | bytes 589832 | tf_op jit(solution)/shard_map/ppermute | solution.py:725
  50.5 17.2 %collective-permute-start.13 = (bf16[64,1536]{1,0:T(8,128)(2,1)S(1)}, bf16[64,1536]{1,0:T(8,128)(2,1)S(1)}, u32[]{:S(2)}, u32[]{:S(2)}) collective-permute-start(bf16[64,1536]{1,0:T(8,128)(2,1)S(1)} %slice.8), channel_id=1, source_target_pairs={{0,16},{1,17},{2,18},{3,19},{4,20},{5,21},{6,22},{7,23},{8,24},{9,... | collective-permute-start | bytes 589832 | tf_op jit(solution)/shard_map/ppermute | solution.py:725
  54.7 13.0 %collective-permute-start.14 = (bf16[64,1536]{1,0:T(8,128)(2,1)S(1)}, bf16[64,1536]{1,0:T(8,128)(2,1)S(1)}, u32[]{:S(2)}, u32[]{:S(2)}) collective-permute-start(bf16[64,1536]{1,0:T(8,128)(2,1)S(1)} %slice.9), channel_id=1, source_target_pairs={{0,8},{1,9},{2,10},{3,11},{4,12},{5,13},{6,14},{7,15},{8,0},{9,1},... | collective-permute-start | bytes 589832 | tf_op jit(solution)/shard_map/ppermute | solution.py:725
  76.1 9.6 %collective-permute-start.16 = (bf16[256,1536]{1,0:T(8,128)(2,1)}, bf16[256,1536]{1,0:T(8,128)(2,1)S(1)}, u32[]{:S(2)}, u32[]{:S(2)}) collective-permute-start(bf16[256,1536]{1,0:T(8,128)(2,1)} %get-tuple-element.38.refs_1_), channel_id=1, source_target_pairs={{0,4},{1,5},{2,6},{3,7},{4,0},{5,1},{6,2},{7,3},{8,12},{9,13},{10,... | collective-permute-start | bytes 2359304 | tf_op jit(solution)/shard_map/ppermute | solution.py:725
  77.0 24.0 %collective-permute-start.17 = (bf16[704,384]{1,0:T(8,128)(2,1)}, bf16[704,384]{1,0:T(8,128)(2,1)}, u32[]{:S(2)}, u32[]{:S(2)}) collective-permute-start(bf16[704,384]{1,0:T(8,128)(2,1)} %release.6.refs_1_), channel_id=1, source_target_pairs={{0,8},{1,9},{2,10},{3,11},{4,12},{5,13},{6,14},{7,15},{8,0},{9,1},... | collective-permute-start | bytes 1622024 | tf_op jit(solution)/shard_map/ppermute | solution.py:725
  77.6 23.5 %collective-permute-start.18 = (bf16[704,384]{1,0:T(8,128)(2,1)}, bf16[704,384]{1,0:T(8,128)(2,1)}, u32[]{:S(2)}, u32[]{:S(2)}) collective-permute-start(bf16[704,384]{1,0:T(8,128)(2,1)} %release.6.refs_1_), channel_id=1, source_target_pairs={{0,16},{1,17},{2,18},{3,19},{4,20},{5,21},{6,22},{7,23},{8,24},{9,... | collective-permute-start | bytes 1622024 | tf_op jit(solution)/shard_map/ppermute | solution.py:725
  78.1 25.4 %collective-permute-start.19 = (bf16[704,384]{1,0:T(8,128)(2,1)}, bf16[704,384]{1,0:T(8,128)(2,1)S(1)}, u32[]{:S(2)}, u32[]{:S(2)}) collective-permute-start(bf16[704,384]{1,0:T(8,128)(2,1)} %release.7.refs_5_), channel_id=1, source_target_pairs={{0,8},{1,9},{2,10},{3,11},{4,12},{5,13},{6,14},{7,15},{8,0},{9,1},... | collective-permute-start | bytes 1622024 | tf_op jit(solution)/shard_map/ppermute | solution.py:725
  79.6 24.3 %collective-permute-start.20 = (bf16[704,384]{1,0:T(8,128)(2,1)}, bf16[704,384]{1,0:T(8,128)(2,1)}, u32[]{:S(2)}, u32[]{:S(2)}) collective-permute-start(bf16[704,384]{1,0:T(8,128)(2,1)} %release.7.refs_5_), channel_id=1, source_target_pairs={{0,16},{1,17},{2,18},{3,19},{4,20},{5,21},{6,22},{7,23},{8,24},{9,... | collective-permute-start | bytes 1622024 | tf_op jit(solution)/shard_map/ppermute | solution.py:725
  85.7 18.4 %collective-permute-start.22 = (bf16[704,384]{1,0:T(8,128)(2,1)S(1)}, bf16[704,384]{1,0:T(8,128)(2,1)}, u32[]{:S(2)}, u32[]{:S(2)}) collective-permute-start(bf16[704,384]{1,0:T(8,128)(2,1)S(1)} %copy-done.12), channel_id=1, source_target_pairs={{0,4},{1,5},{2,6},{3,7},{4,0},{5,1},{6,2},{7,3},{8,12},{9,13},{10,... | collective-permute-start | bytes 1622024 | tf_op jit(solution)/shard_map/ppermute | solution.py:725
  97.1 55.1 %all-to-all-start = ((bf16[4,1632,128]{2,1,0:T(8,128)(2,1)}), bf16[4,1632,128]{2,1,0:T(8,128)(2,1)S(1)}, u32[]{:S(2)}, u32[]{:S(2)}) async-start(bf16[4,1632,128]{2,1,0:T(8,128)(2,1)} %stats.1.refs_0_), calls=%async_computation | async-start | bytes 3342336 | tf_op jit(solution)/shard_map/all_to_all | solution.py:821
  101.0 14.5 %collective-permute-start.25 = (bf16[704,384]{1,0:T(8,128)(2,1)}, bf16[704,384]{1,0:T(8,128)(2,1)S(1)}, u32[]{:S(2)}, u32[]{:S(2)}) collective-permute-start(bf16[704,384]{1,0:T(8,128)(2,1)} %release.7.refs_5_), channel_id=1, source_target_pairs={{0,4},{1,5},{2,6},{3,7},{4,0},{5,1},{6,2},{7,3},{8,12},{9,13},{10,... | collective-permute-start | bytes 1622024 | tf_op jit(solution)/shard_map/ppermute | solution.py:725
  101.1 15.0 %collective-permute-start.21 = (bf16[704,384]{1,0:T(8,128)(2,1)}, bf16[704,384]{1,0:T(8,128)(2,1)}, u32[]{:S(2)}, u32[]{:S(2)}) collective-permute-start(bf16[704,384]{1,0:T(8,128)(2,1)} %collective-permute-done.17.refs_1_.refs_2_), channel_id=1, source_target_pairs={{0,16},{1,17},{2,18},{3,19},{4,20},{5,21},{6,22},{7,23},{8,24},{9,... | collective-permute-start | bytes 1622024 | tf_op jit(solution)/shard_map/ppermute | solution.py:725
  103.5 12.9 %collective-permute-start.23 = (bf16[704,384]{1,0:T(8,128)(2,1)}, bf16[704,384]{1,0:T(8,128)(2,1)S(1)}, u32[]{:S(2)}, u32[]{:S(2)}) collective-permute-start(bf16[704,384]{1,0:T(8,128)(2,1)} %collective-permute-done.17.refs_1_.refs_2_), channel_id=1, source_target_pairs={{0,4},{1,5},{2,6},{3,7},{4,0},{5,1},{6,2},{7,3},{8,12},{9,13},{10,... | collective-permute-start | bytes 1622024 | tf_op jit(solution)/shard_map/ppermute | solution.py:725
  103.9 16.3 %collective-permute-start.24 = (bf16[704,384]{1,0:T(8,128)(2,1)}, bf16[704,384]{1,0:T(8,128)(2,1)}, u32[]{:S(2)}, u32[]{:S(2)}) collective-permute-start(bf16[704,384]{1,0:T(8,128)(2,1)} %collective-permute-done.18.refs_2_.refs_3_), channel_id=1, source_target_pairs={{0,4},{1,5},{2,6},{3,7},{4,0},{5,1},{6,2},{7,3},{8,12},{9,13},{10,... | collective-permute-start | bytes 1622024 | tf_op jit(solution)/shard_map/ppermute | solution.py:725
  104.1 15.8 %collective-permute-start.26 = (bf16[704,384]{1,0:T(8,128)(2,1)}, bf16[704,384]{1,0:T(8,128)(2,1)S(1)}, u32[]{:S(2)}, u32[]{:S(2)}) collective-permute-start(bf16[704,384]{1,0:T(8,128)(2,1)} %collective-permute-done.20.refs_3_.refs_7_), channel_id=1, source_target_pairs={{0,8},{1,9},{2,10},{3,11},{4,12},{5,13},{6,14},{7,15},{8,0},{9,1},... | collective-permute-start | bytes 1622024 | tf_op jit(solution)/shard_map/ppermute | solution.py:725
  115.6 16.1 %collective-permute-start.29 = (bf16[704,384]{1,0:T(8,128)(2,1)}, bf16[704,384]{1,0:T(8,128)(2,1)}, u32[]{:S(2)}, u32[]{:S(2)}) collective-permute-start(bf16[704,384]{1,0:T(8,128)(2,1)} %collective-permute-done.20.refs_3_.refs_7_), channel_id=1, source_target_pairs={{0,4},{1,5},{2,6},{3,7},{4,0},{5,1},{6,2},{7,3},{8,12},{9,13},{10,... | collective-permute-start | bytes 1622024 | tf_op jit(solution)/shard_map/ppermute | solution.py:725
  116.1 15.6 %collective-permute-start.28 = (bf16[704,384]{1,0:T(8,128)(2,1)S(1)}, bf16[704,384]{1,0:T(8,128)(2,1)}, u32[]{:S(2)}, u32[]{:S(2)}) collective-permute-start(bf16[704,384]{1,0:T(8,128)(2,1)S(1)} %collective-permute-done.19.refs_2_.refs_6_), channel_id=1, source_target_pairs={{0,4},{1,5},{2,6},{3,7},{4,0},{5,1},{6,2},{7,3},{8,12},{9,13},{10,... | collective-permute-start | bytes 1622024 | tf_op jit(solution)/shard_map/ppermute | solution.py:725
  117.2 14.5 %collective-permute-start.27 = (bf16[704,384]{1,0:T(8,128)(2,1)}, bf16[704,384]{1,0:T(8,128)(2,1)}, u32[]{:S(2)}, u32[]{:S(2)}) collective-permute-start(bf16[704,384]{1,0:T(8,128)(2,1)} %collective-permute-done.21.refs_4_), channel_id=1, source_target_pairs={{0,4},{1,5},{2,6},{3,7},{4,0},{5,1},{6,2},{7,3},{8,12},{9,13},{10,... | collective-permute-start | bytes 1622024 | tf_op jit(solution)/shard_map/ppermute | solution.py:725
  119.9 15.5 %collective-permute-start.31 = (bf16[704,384]{1,0:T(8,128)(2,1)S(1)}, bf16[704,384]{1,0:T(8,128)(2,1)S(1)}, u32[]{:S(2)}, u32[]{:S(2)}) collective-permute-start(bf16[704,384]{1,0:T(8,128)(2,1)S(1)} %collective-permute-done.26.refs_0_.refs_8_), channel_id=1, source_target_pairs={{0,4},{1,5},{2,6},{3,7},{4,0},{5,1},{6,2},{7,3},{8,12},{9,13},{10,... | collective-permute-start | bytes 1622024 | tf_op jit(solution)/shard_map/ppermute | solution.py:725
  120.2 15.2 %collective-permute-start.30 = (bf16[128,1024]{1,0:T(8,128)(2,1)S(1)}, bf16[128,1024]{1,0:T(8,128)(2,1)S(1)}, u32[]{:S(2)}, u32[]{:S(2)}) collective-permute-start(bf16[128,1024]{1,0:T(8,128)(2,1)S(1)} %get-tuple-element.49.refs_1_.refs_0_), channel_id=1, source_target_pairs={{0,1},{1,0},{2,3},{3,2},{4,5},{5,4},{6,7},{7,6},{8,9},{9,8},{10,11... | collective-permute-start | bytes 786440 | tf_op jit(solution)/shard_map/ppermute | solution.py:725
  134.9 10.8 %collective-permute-start.32 = (bf16[128,1024]{1,0:T(8,128)(2,1)S(1)}, bf16[128,1024]{1,0:T(8,128)(2,1)S(1)}, u32[]{:S(2)}, u32[]{:S(2)}) collective-permute-start(bf16[128,1024]{1,0:T(8,128)(2,1)S(1)} %get-tuple-element.50.refs_1_), channel_id=1, source_target_pairs={{0,1},{1,0},{2,3},{3,2},{4,5},{5,4},{6,7},{7,6},{8,9},{9,8},{10,11... | collective-permute-start | bytes 786440 | tf_op jit(solution)/shard_map/ppermute | solution.py:725
  142.1 13.5 %collective-permute-start.33 = (bf16[128,1024]{1,0:T(8,128)(2,1)S(1)}, bf16[128,1024]{1,0:T(8,128)(2,1)S(1)}, u32[]{:S(2)}, u32[]{:S(2)}) collective-permute-start(bf16[128,1024]{1,0:T(8,128)(2,1)S(1)} %get-tuple-element.54.refs_4_), channel_id=1, source_target_pairs={{0,1},{1,0},{2,3},{3,2},{4,5},{5,4},{6,7},{7,6},{8,9},{9,8},{10,11... | collective-permute-start | bytes 786440 | tf_op jit(solution)/shard_map/ppermute | solution.py:725
  (48 other events, 361.8 us)
Sparse Core Ops, SparseCore 0:
  10.9 75.3 all-gather.1

commit v3 on v2

--- a/solution.py
+++ b/solution.py
@@ -757,7 +757,6 @@
         listed = np.array(listed, np.int32)
         owner = (my_req ^ listed[:, 0]) * peers + (my_mesh - listed[:, 1]) % peers
         qkv_at = (owner * own_rows).astype(jnp.int32)
-        (ffn_own,) = release_call([ffn_own], [two])
         ffn_two = move(ffn_own, hop_two)
         (ffn_own,) = release_call([ffn_own], last)
         x_own, y_own = move(ffn_own, flips[1]), move(ffn_own, flips[2])

time: 165 us -> 165 us (level)
    unnamed x89 -> x81, local copies, waits for them, and re-layouts: 11.4 us -> 11 us
where the time goes in v3:
time: 165 us
  Pallas kernels  67.8 us (41%)
  starting transfers between devices  39 us (24%)
  waiting for transfers between devices  31.2 us (19%)
  between operations  14.5 us (9%)
  local copies, waits for them, and re-layouts  11 us (7%)
    ppermute x35, starting transfers between devices, shards(): move = lambda value, pairs: lax.ppermute(value, AXES, pairs)  35.1 us
    ppermute x35, waiting for transfers between devices, shards(): move = lambda value, pairs: lax.ppermute(value, AXES, pairs)  30.5 us
    pallas_call x2, Pallas kernels, cg_call(): pl.pallas_call(functools.partial(cg_kernel, heads, 8), grid=(count,), in_...  19.9 us
    unnamed x81, local copies, waits for them, and re-layouts  11 us
    pallas_call x2, Pallas kernels, conv_call(): pl.pallas_call(conv_kernel, grid_spec=pltpu.PrefetchScalarGridSpec(num_sc...  9.12 us
    pallas_call x1, Pallas kernels, project_call(): pl.pallas_call(functools.partial(project_kernel, len(pieces), spans), gri...  6.86 us
    pallas_call x1, Pallas kernels, stats_call(): pl.pallas_call(functools.partial(stats_kernel, heads), grid_spec=pltpu.Pr...  5.94 us
    pallas_call x1, Pallas kernels, ffn_first_call(): pl.pallas_call(functools.partial(ffn_first_kernel, spans, counts), grid_s...  5.89 us
  transfers between devices with their start and end apart: 37, of which 12 were waited for; matrix products, arithmetic and copies ran while one was open for 2% of the time, Pallas kernels for 41%

profile of v3, /device:TPU:0, one launch (start us, length us, event | category | flops | bytes accessed | tf_op | source)
XLA Modules:
  0.0 164.6 jit_solution(12438730263579334191)
XLA Ops:
  7.9 1.6 split_heads.1
  11.1 3.0 %collective-permute-start.6 = (bf16[64,1536]{1,0:T(8,128)(2,1)S(1)}, bf16[64,1536]{1,0:T(8,128)(2,1)S(1)}, u32[]{:S(2)}, u32[]{:S(2)}) collective-permute-start(bf16[64,1536]{1,0:T(8,128)(2,1)S(1)} %constant_dynamic-update-slice_fusion.refs_0_), channel_id=1, source_target_pairs={{0,1},{1,2},{2,3},{3,0},{4,5},{5,6},{6,7},{7,4},{8,9},{9,10},{10,1... | collective-permute-start | bytes 589832 | tf_op jit(solution)/shard_map/ppermute | solution.py:725
  14.1 2.1 %collective-permute-start.1 = (bf16[64,1536]{1,0:T(8,128)(2,1)S(1)}, bf16[64,1536]{1,0:T(8,128)(2,1)S(1)}, u32[]{:S(2)}, u32[]{:S(2)}) collective-permute-start(bf16[64,1536]{1,0:T(8,128)(2,1)S(1)} %constant_dynamic-update-slice_fusion.refs_0_), channel_id=1, source_target_pairs={{0,3},{1,0},{2,1},{3,2},{4,7},{5,4},{6,5},{7,6},{8,11},{9,8},{10,9... | collective-permute-start | bytes 589832 | tf_op jit(solution)/shard_map/ppermute | solution.py:725
  16.2 1.6 %collective-permute-start.2 = (bf16[64,1536]{1,0:T(8,128)(2,1)S(1)}, bf16[64,1536]{1,0:T(8,128)(2,1)S(1)}, u32[]{:S(2)}, u32[]{:S(2)}) collective-permute-start(bf16[64,1536]{1,0:T(8,128)(2,1)S(1)} %constant_dynamic-update-slice_fusion.refs_0_), channel_id=1, source_target_pairs={{0,8},{1,9},{2,10},{3,11},{4,12},{5,13},{6,14},{7,15},{8,0},{9,1},... | collective-permute-start | bytes 589832 | tf_op jit(solution)/shard_map/ppermute | solution.py:725
  17.9 1.5 collective-permute-start.3
  19.4 2.5 %collective-permute-done.6.refs_4_ = bf16[64,1536]{1,0:T(8,128)(2,1)S(1)} collective-permute-done((bf16[64,1536]{1,0:T(8,128)(2,1)S(1)}, bf16[64,1536]{1,0:T(8,128)(2,1)S(1)}, u32[]{:S(2)}, u32[]{:S(2)}) %collective-permute-start.6) | collective-permute-done | bytes 196640 | tf_op jit(solution)/shard_map/ppermute | solution.py:725
  21.9 1.7 %collective-permute-start.7 = (bf16[64,1536]{1,0:T(8,128)(2,1)S(1)}, bf16[64,1536]{1,0:T(8,128)(2,1)S(1)}, u32[]{:S(2)}, u32[]{:S(2)}) collective-permute-start(bf16[64,1536]{1,0:T(8,128)(2,1)S(1)} %collective-permute-done.6.refs_4_), channel_id=1, source_target_pairs={{0,8},{1,9},{2,10},{3,11},{4,12},{5,13},{6,14},{7,15},{8,0},{9,1},... | collective-permute-start | bytes 589832 | tf_op jit(solution)/shard_map/ppermute | solution.py:725
  23.6 1.5 collective-permute-start.8
  28.2 5.1 %norm_gates.1 = (bf16[704,384]{1,0:T(8,128)(2,1)}, bf16[256,1024]{1,0:T(8,128)(2,1)}, f32[4,8,64,128]{3,2,1,0:T(8,128)}, f32[4,8,64,128]{3,2,1,0:T(8,128)}, f32[...) custom-call(s32[4]{0:T(128)S(1)} %copy-done.6, ...), custom_call_target="tpu_custom_call", output_to_operand_aliasing={{6}: (8, {})} | custom-call | flops 3221225472 | bytes 65536 | tf_op jit(solution)/shard_map/norm_gates/pallas_call | solution.py:142
  38.9 2.8 %collective-permute-start.15 = (bf16[704,384]{1,0:T(8,128)(2,1)}, bf16[704,384]{1,0:T(8,128)(2,1)}, u32[]{:S(2)}, u32[]{:S(2)}) collective-permute-start(bf16[704,384]{1,0:T(8,128)(2,1)} %get-tuple-element.37.refs_0_), channel_id=1, source_target_pairs={{0,2},{1,3},{2,0},{3,1},{4,6},{5,7},{6,4},{7,5},{8,10},{9,11},{10,... | collective-permute-start | bytes 1622024 | tf_op jit(solution)/shard_map/ppermute | solution.py:725
  41.7 1.6 collective-permute-start.5
  43.3 5.3 %collective-permute-done.11.refs_9_ = bf16[128,1536]{1,0:T(8,128)(2,1)S(1)} collective-permute-done((bf16[128,1536]{1,0:T(8,128)(2,1)S(1)}, bf16[128,1536]{1,0:T(8,128)(2,1)S(1)}, u32[]{:S(2)}, u32[]{:S(2)}) %collective-permute-start.11) | collective-permute-done | bytes 393248 | tf_op jit(solution)/shard_map/ppermute | solution.py:725
  51.7 2.9 %collective-permute-done.5.refs_3_ = bf16[64,1536]{1,0:T(8,128)(2,1)S(1)} collective-permute-done((bf16[64,1536]{1,0:T(8,128)(2,1)}, bf16[64,1536]{1,0:T(8,128)(2,1)S(1)}, u32[]{:S(2)}, u32[]{:S(2)}) %collective-permute-start.5) | collective-permute-done | bytes 196640 | tf_op jit(solution)/shard_map/ppermute | solution.py:725
  55.5 12.2 %collective-permute-done.15.refs_13_.refs_0_ = bf16[704,384]{1,0:T(8,128)(2,1)} collective-permute-done((bf16[704,384]{1,0:T(8,128)(2,1)}, bf16[704,384]{1,0:T(8,128)(2,1)}, u32[]{:S(2)}, u32[]{:S(2)}) %collective-permute-start.15) | collective-permute-done | bytes 540704 | tf_op jit(solution)/shard_map/ppermute | solution.py:725
  69.1 6.9 %project.1 = (bf16[256,1536]{1,0:T(8,128)(2,1)}, bf16[256,1536]{1,0:T(8,128)(2,1)}) custom-call(s32[32]{0:T(128)S(1)} %fusion.2.at_ref, bf16[256,1024]{1,0:T(8,128)(2,1)} %get-tuple-element.35.x_ref, bf16[256,1024]{1,0:T(8,128)(2,1)} %copy-done.31, bf16[64,1536]{1,0:T(8,128)(2,1)} %copy-done.26, bf16[64,1536]{1,0:T(8,128)(2,1)} %copy-done.33, ...), custom_call_target="tpu_custom_call" | custom-call | flops 3221225472 | bytes 65536 | tf_op jit(solution)/shard_map/project/pallas_call | solution.py:220
  79.5 1.6 collective-permute-start.20
  81.1 4.6 %conv_norm.2 = (f32[256,3072]{1,0:T(8,128)}, bf16[4,3,3072]{2,1,0:T(4,128)(2,1)}) custom-call(s32[1]{0:T(128)} %bitcast.core_ref.half_ref, s32[4]{0:T(128)S(1)} %copy-done.7, bf16[256,1536]{1,0:T(8,128)(2,1)} %get-tuple-element.39.projected_ref, bf16[4,3,3072]{2,1,0:T(4,128)(2,1)} %copy.33.tail_ref, f32[4,3072]{1,0:T(4,128)} %conv_ref.3), custom_call_target="tpu_custom_call" | custom-call | flops 2147483648 | bytes 65536 | tf_op jit(solution)/shard_map/conv_norm/pallas_call | solution.py:273
  86.5 4.6 %conv_norm.3 = (f32[256,3072]{1,0:T(8,128)}, bf16[4,3,3072]{2,1,0:T(4,128)(2,1)}) custom-call(s32[1]{0:T(128)S(6)} %sub.13.half_ref, s32[4]{0:T(128)S(1)} %copy-done.7, bf16[256,1536]{1,0:T(8,128)(2,1)} %copy-done.29, bf16[4,3,3072]{2,1,0:T(4,128)(2,1)} %copy.33.tail_ref, f32[4,3072]{1,0:T(4,128)} %conv_ref.3, ...), custom_call_target="tpu_custom_call", output_to_operand_aliasing={{0}: (5, {}), {1}: (6, {})} | custom-call | flops 2147483648 | bytes 65536 | tf_op jit(solution)/shard_map/conv_norm/pallas_call | solution.py:273
  91.1 5.9 %stats.1.refs_0_ = bf16[4,1632,128]{2,1,0:T(8,128)(2,1)} custom-call(s32[4]{0:T(128)S(1)} %get-tuple-element.67.place_ref, s32[4]{0:T(128)S(1)} %get-tuple-element.66.slot_ref, f32[256,3072]{1,0:T(8,128)} %get-tuple-element.42.k_ref.v_ref.q_ref, f32[256,3072]{1,0:T(8,128)} %get-tuple-element.42.k_ref.v_ref.q_ref, ...), custom_call_target="tpu_custom_call" | custom-call | flops 3221225472 | bytes 65536 | tf_op jit(solution)/shard_map/stats/pallas_call | solution.py:337
  97.1 3.9 %all-to-all-start = ((bf16[4,1632,128]{2,1,0:T(8,128)(2,1)}), bf16[4,1632,128]{2,1,0:T(8,128)(2,1)S(1)}, u32[]{:S(2)}, u32[]{:S(2)}) async-start(bf16[4,1632,128]{2,1,0:T(8,128)(2,1)} %stats.1.refs_0_), calls=%async_computation | async-start | bytes 3342336 | tf_op jit(solution)/shard_map/all_to_all | solution.py:820
  101.5 1.8 %collective-permute-done.19.refs_2_.refs_6_ = bf16[704,384]{1,0:T(8,128)(2,1)S(1)} collective-permute-done((bf16[704,384]{1,0:T(8,128)(2,1)}, bf16[704,384]{1,0:T(8,128)(2,1)S(1)}, u32[]{:S(2)}, u32[]{:S(2)}) %collective-permute-start.19) | collective-permute-done | bytes 540704 | tf_op jit(solution)/shard_map/ppermute | solution.py:725
  105.4 10.0 %cg.2.x_ref.refs_0_ = bf16[256,1024]{1,0:T(8,128)(2,1)} custom-call(f32[8]{0:T(128)S(1)} %copy-done.2, f32[256,3072]{1,0:T(8,128)} %get-tuple-element.42.k_ref.v_ref.q_ref, f32[256,3072]{1,0:T(8,128)} %get-tuple-element.42.k_ref.v_ref.q_ref, f32[256,3072]{1,0:T(8,128)} %get-tuple-element.42.k_ref.v_ref.q_ref, f32[4,8,64,128]{3,2,1,0:T(8,128)} %get-tuple-element.43.w_ref, ...), custom_call_target="tpu_custom_call" | custom-call | flops 4294967296 | bytes 65536 | tf_op jit(solution)/shard_map/cg/pallas_call | solution.py:514
  117.4 2.4 %out_proj.2 = (bf16[128,1024]{1,0:T(8,128)(2,1)S(1)}, bf16[128,1024]{1,0:T(8,128)(2,1)S(1)}) custom-call(bf16[256,1024]{1,0:T(8,128)(2,1)} %cg.2.x_ref.refs_0_, bf16[256,1024]{1,0:T(8,128)(2,1)} %bitcast.11, f32[1,1024]{1,0:T(1,128)} %bitcast.17, bf16[1024,1024]{1,0:T(8,128)(2,1)} %all-gather.2.cloned.1.call-done.w_ref), custom_call_target="tpu_custom_call" | custom-call | flops 2147483648 | bytes 65536 | tf_op jit(solution)/shard_map/out_proj/pallas_call | solution.py:559
  120.0 1.7 %collective-permute-start.30 = (bf16[128,1024]{1,0:T(8,128)(2,1)S(1)}, bf16[128,1024]{1,0:T(8,128)(2,1)S(1)}, u32[]{:S(2)}, u32[]{:S(2)}) collective-permute-start(bf16[128,1024]{1,0:T(8,128)(2,1)S(1)} %get-tuple-element.49.refs_1_.refs_0_), channel_id=1, source_target_pairs={{0,1},{1,0},{2,3},{3,2},{4,5},{5,4},{6,7},{7,6},{8,9},{9,8},{10,11... | collective-permute-start | bytes 786440 | tf_op jit(solution)/shard_map/ppermute | solution.py:725
  121.7 10.0 %cg.3.x_ref = bf16[256,1024]{1,0:T(8,128)(2,1)} custom-call(f32[8]{0:T(128)S(1)} %copy-done.2, f32[256,3072]{1,0:T(8,128)} %get-tuple-element.42.k_ref.v_ref.q_ref, f32[256,3072]{1,0:T(8,128)} %get-tuple-element.42.k_ref.v_ref.q_ref, f32[256,3072]{1,0:T(8,128)} %get-tuple-element.42.k_ref.v_ref.q_ref, ...), custom_call_target="tpu_custom_call", output_to_operand_aliasing={{}: (8, {})} | custom-call | flops 4294967296 | bytes 65536 | tf_op jit(solution)/shard_map/cg/pallas_call | solution.py:514
  131.7 2.4 %out_proj.3 = (bf16[128,1024]{1,0:T(8,128)(2,1)S(1)}, bf16[128,1024]{1,0:T(8,128)(2,1)S(1)}) custom-call(bf16[256,1024]{1,0:T(8,128)(2,1)} %cg.3.x_ref, bf16[256,1024]{1,0:T(8,128)(2,1)} %bitcast.12, f32[1,1024]{1,0:T(1,128)} %bitcast.18, bf16[1024,1024]{1,0:T(8,128)(2,1)} %all-gather.2.cloned.1.call-done.w_ref, ...), custom_call_target="tpu_custom_call" | custom-call | flops 2147483648 | bytes 65536 | tf_op jit(solution)/shard_map/out_proj/pallas_call | solution.py:559
  136.1 5.9 %ffn_first.1 = (bf16[128,1024]{1,0:T(8,128)(2,1)S(1)}, bf16[2,704,1024]{2,1,0:T(8,128)(2,1)S(1)}, bf16[2,704,1024]{2,1,0:T(8,128)(2,1)S(1)}, bf16[2,704,1024]{2,1,0:T(8,128)(2,1)S(1)}) custom-call(s32[8]{0:T(128)S(1)} %broadcast_xor_fusion.order_ref, bf16[128,1024]{1,0:T(8,128)(2,1)S(1)} %collective-permute-done.30.refs_0_, ...), custom_call_target="tpu_custom_call" | custom-call | flops 5368709120 | bytes 65536 | tf_op jit(solution)/shard_map/ffn_first/pallas_call | solution.py:632
  142.0 1.6 collective-permute-start.33
  143.5 2.1 %collective-permute-done.32.refs_0_ = bf16[128,1024]{1,0:T(8,128)(2,1)S(1)} collective-permute-done((bf16[128,1024]{1,0:T(8,128)(2,1)S(1)}, bf16[128,1024]{1,0:T(8,128)(2,1)S(1)}, u32[]{:S(2)}, u32[]{:S(2)}) %collective-permute-start.32) | collective-permute-done | bytes 262176 | tf_op jit(solution)/shard_map/ppermute | solution.py:725
  145.6 2.4 %ffn_second.2.refs_5_ = bf16[128,1024]{1,0:T(8,128)(2,1)S(1)} custom-call(bf16[128,1024]{1,0:T(8,128)(2,1)S(1)} %collective-permute-done.32.refs_0_, bf16[2,704,1024]{2,1,0:T(8,128)(2,1)S(1)} %get-tuple-element.51.refs_1_.refs_2_, bf16[2,704,1024]{2,1,0:T(8,128)(2,1)S(1)} %get-tuple-element.52.refs_2_.refs_3_, ...), custom_call_target="tpu_custom_call" | custom-call | flops 3221225472 | bytes 65536 | tf_op jit(solution)/shard_map/ffn_second/pallas_call | solution.py:664
  148.7 2.6 %ffn_second.3 = (f32[128,1024]{1,0:T(8,128)S(1)}, f32[128,1024]{1,0:T(8,128)S(1)}) custom-call(bf16[128,1024]{1,0:T(8,128)(2,1)S(1)} %copy-done.1, bf16[128,1024]{1,0:T(8,128)(2,1)S(1)} %get-tuple-element.50.refs_1_, bf16[2,704,1024]{2,1,0:T(8,128)(2,1)S(1)} %get-tuple-element.51.refs_1_.refs_2_, ...), custom_call_target="tpu_custom_call" | custom-call | flops 3221225472 | bytes 65536 | tf_op jit(solution)/shard_map/ffn_second/pallas_call | solution.py:664
  152.2 2.7 %unpack.1 = (f32[4,8,128,128]{3,2,1,0:T(8,128)}, f32[4,8,128,128]{3,2,1,0:T(8,128)}, bf16[4,3,3072]{2,1,0:T(4,128)(2,1)S(1)}) custom-call(bf16[4,1632,128]{2,1,0:T(8,128)(2,1)S(1)} %all-to-all-done.part_ref, f32[128,1024]{1,0:T(8,128)} %copy-done.8), custom_call_target="tpu_custom_call" | custom-call | flops 3221225472 | bytes 65536 | tf_op jit(solution)/shard_map/unpack/pallas_call | solution.py:412
  (149 shorter events, 31.7 us)
Async XLA Ops:
  7.2 110.2 %all-gather.2.cloned.1.call-start = ((), (), s32[]{:S(2)}) async-start(), calls=%async_computation.1 | async-start | bytes 2162688 | tf_op jit(solution)/shard_map/all_gather | solution.py:729
  11.1 10.7 %collective-permute-start.6 = (bf16[64,1536]{1,0:T(8,128)(2,1)S(1)}, bf16[64,1536]{1,0:T(8,128)(2,1)S(1)}, u32[]{:S(2)}, u32[]{:S(2)}) collective-permute-start(bf16[64,1536]{1,0:T(8,128)(2,1)S(1)} %constant_dynamic-update-slice_fusion.refs_0_), channel_id=1, source_target_pairs={{0,1},{1,2},{2,3},{3,0},{4,5},{5,6},{6,7},{7,4},{8,9},{9,10},{10,1... | collective-permute-start | bytes 589832 | tf_op jit(solution)/shard_map/ppermute | solution.py:725
  14.1 11.0 %collective-permute-start.1 = (bf16[64,1536]{1,0:T(8,128)(2,1)S(1)}, bf16[64,1536]{1,0:T(8,128)(2,1)S(1)}, u32[]{:S(2)}, u32[]{:S(2)}) collective-permute-start(bf16[64,1536]{1,0:T(8,128)(2,1)S(1)} %constant_dynamic-update-slice_fusion.refs_0_), channel_id=1, source_target_pairs={{0,3},{1,0},{2,1},{3,2},{4,7},{5,4},{6,5},{7,6},{8,11},{9,8},{10,9... | collective-permute-start | bytes 589832 | tf_op jit(solution)/shard_map/ppermute | solution.py:725
  16.2 9.9 %collective-permute-start.2 = (bf16[64,1536]{1,0:T(8,128)(2,1)S(1)}, bf16[64,1536]{1,0:T(8,128)(2,1)S(1)}, u32[]{:S(2)}, u32[]{:S(2)}) collective-permute-start(bf16[64,1536]{1,0:T(8,128)(2,1)S(1)} %constant_dynamic-update-slice_fusion.refs_0_), channel_id=1, source_target_pairs={{0,8},{1,9},{2,10},{3,11},{4,12},{5,13},{6,14},{7,15},{8,0},{9,1},... | collective-permute-start | bytes 589832 | tf_op jit(solution)/shard_map/ppermute | solution.py:725
  21.9 11.4 %collective-permute-start.7 = (bf16[64,1536]{1,0:T(8,128)(2,1)S(1)}, bf16[64,1536]{1,0:T(8,128)(2,1)S(1)}, u32[]{:S(2)}, u32[]{:S(2)}) collective-permute-start(bf16[64,1536]{1,0:T(8,128)(2,1)S(1)} %collective-permute-done.6.refs_4_), channel_id=1, source_target_pairs={{0,8},{1,9},{2,10},{3,11},{4,12},{5,13},{6,14},{7,15},{8,0},{9,1},... | collective-permute-start | bytes 589832 | tf_op jit(solution)/shard_map/ppermute | solution.py:725
  23.6 9.7 %collective-permute-start.8 = (bf16[64,1536]{1,0:T(8,128)(2,1)S(1)}, bf16[64,1536]{1,0:T(8,128)(2,1)S(1)}, u32[]{:S(2)}, u32[]{:S(2)}) collective-permute-start(bf16[64,1536]{1,0:T(8,128)(2,1)S(1)} %collective-permute-done.6.refs_4_), channel_id=1, source_target_pairs={{0,16},{1,17},{2,18},{3,19},{4,20},{5,21},{6,22},{7,23},{8,24},{9,... | collective-permute-start | bytes 589832 | tf_op jit(solution)/shard_map/ppermute | solution.py:725
  36.1 12.5 %collective-permute-start.11 = (bf16[128,1536]{1,0:T(8,128)(2,1)S(1)}, bf16[128,1536]{1,0:T(8,128)(2,1)S(1)}, u32[]{:S(2)}, u32[]{:S(2)}) collective-permute-start(bf16[128,1536]{1,0:T(8,128)(2,1)S(1)} %pad_maximum_fusion.refs_8_), channel_id=1, source_target_pairs={{0,8},{1,9},{2,10},{3,11},{4,12},{5,13},{6,14},{7,15},{8,0},{9,1},... | collective-permute-start | bytes 1179656 | tf_op jit(solution)/shard_map/ppermute | solution.py:725
  37.4 13.0 %collective-permute-start.12 = (bf16[128,1536]{1,0:T(8,128)(2,1)S(1)}, bf16[128,1536]{1,0:T(8,128)(2,1)S(1)}, u32[]{:S(2)}, u32[]{:S(2)}) collective-permute-start(bf16[128,1536]{1,0:T(8,128)(2,1)S(1)} %pad_maximum_fusion.refs_8_), channel_id=1, source_target_pairs={{0,16},{1,17},{2,18},{3,19},{4,20},{5,21},{6,22},{7,23},{8,24},{9,... | collective-permute-start | bytes 1179656 | tf_op jit(solution)/shard_map/ppermute | solution.py:725
  38.9 28.8 %collective-permute-start.15 = (bf16[704,384]{1,0:T(8,128)(2,1)}, bf16[704,384]{1,0:T(8,128)(2,1)}, u32[]{:S(2)}, u32[]{:S(2)}) collective-permute-start(bf16[704,384]{1,0:T(8,128)(2,1)} %get-tuple-element.37.refs_0_), channel_id=1, source_target_pairs={{0,2},{1,3},{2,0},{3,1},{4,6},{5,7},{6,4},{7,5},{8,10},{9,11},{10,... | collective-permute-start | bytes 1622024 | tf_op jit(solution)/shard_map/ppermute | solution.py:725
  41.7 13.8 %collective-permute-start.4 = (bf16[256,1024]{1,0:T(8,128)(2,1)}, bf16[256,1024]{1,0:T(8,128)(2,1)S(1)}, u32[]{:S(2)}, u32[]{:S(2)}) collective-permute-start(bf16[256,1024]{1,0:T(8,128)(2,1)} %get-tuple-element.35.x_ref), channel_id=1, source_target_pairs={{0,4},{1,5},{2,6},{3,7},{4,0},{5,1},{6,2},{7,3},{8,12},{9,13},{10,... | collective-permute-start | bytes 1572872 | tf_op jit(solution)/shard_map/ppermute | solution.py:725
  41.7 12.9 %collective-permute-start.5 = (bf16[64,1536]{1,0:T(8,128)(2,1)}, bf16[64,1536]{1,0:T(8,128)(2,1)S(1)}, u32[]{:S(2)}, u32[]{:S(2)}) collective-permute-start(bf16[64,1536]{1,0:T(8,128)(2,1)} %copy-done.33), channel_id=1, source_target_pairs={{0,16},{1,17},{2,18},{3,19},{4,20},{5,21},{6,22},{7,23},{8,24},{9,... | collective-permute-start | bytes 589832 | tf_op jit(solution)/shard_map/ppermute | solution.py:725
  50.4 17.3 %collective-permute-start.13 = (bf16[64,1536]{1,0:T(8,128)(2,1)S(1)}, bf16[64,1536]{1,0:T(8,128)(2,1)S(1)}, u32[]{:S(2)}, u32[]{:S(2)}) collective-permute-start(bf16[64,1536]{1,0:T(8,128)(2,1)S(1)} %slice.8), channel_id=1, source_target_pairs={{0,16},{1,17},{2,18},{3,19},{4,20},{5,21},{6,22},{7,23},{8,24},{9,... | collective-permute-start | bytes 589832 | tf_op jit(solution)/shard_map/ppermute | solution.py:725
  54.6 13.1 %collective-permute-start.14 = (bf16[64,1536]{1,0:T(8,128)(2,1)S(1)}, bf16[64,1536]{1,0:T(8,128)(2,1)S(1)}, u32[]{:S(2)}, u32[]{:S(2)}) collective-permute-start(bf16[64,1536]{1,0:T(8,128)(2,1)S(1)} %slice.9), channel_id=1, source_target_pairs={{0,8},{1,9},{2,10},{3,11},{4,12},{5,13},{6,14},{7,15},{8,0},{9,1},... | collective-permute-start | bytes 589832 | tf_op jit(solution)/shard_map/ppermute | solution.py:725
  76.0 9.7 %collective-permute-start.16 = (bf16[256,1536]{1,0:T(8,128)(2,1)}, bf16[256,1536]{1,0:T(8,128)(2,1)S(1)}, u32[]{:S(2)}, u32[]{:S(2)}) collective-permute-start(bf16[256,1536]{1,0:T(8,128)(2,1)} %get-tuple-element.38.refs_1_), channel_id=1, source_target_pairs={{0,4},{1,5},{2,6},{3,7},{4,0},{5,1},{6,2},{7,3},{8,12},{9,13},{10,... | collective-permute-start | bytes 2359304 | tf_op jit(solution)/shard_map/ppermute | solution.py:725
  77.0 24.0 %collective-permute-start.17 = (bf16[704,384]{1,0:T(8,128)(2,1)}, bf16[704,384]{1,0:T(8,128)(2,1)}, u32[]{:S(2)}, u32[]{:S(2)}) collective-permute-start(bf16[704,384]{1,0:T(8,128)(2,1)} %release.4.refs_1_), channel_id=1, source_target_pairs={{0,8},{1,9},{2,10},{3,11},{4,12},{5,13},{6,14},{7,15},{8,0},{9,1},... | collective-permute-start | bytes 1622024 | tf_op jit(solution)/shard_map/ppermute | solution.py:725
  77.5 23.6 %collective-permute-start.18 = (bf16[704,384]{1,0:T(8,128)(2,1)}, bf16[704,384]{1,0:T(8,128)(2,1)}, u32[]{:S(2)}, u32[]{:S(2)}) collective-permute-start(bf16[704,384]{1,0:T(8,128)(2,1)} %release.4.refs_1_), channel_id=1, source_target_pairs={{0,16},{1,17},{2,18},{3,19},{4,20},{5,21},{6,22},{7,23},{8,24},{9,... | collective-permute-start | bytes 1622024 | tf_op jit(solution)/shard_map/ppermute | solution.py:725
  78.0 25.4 %collective-permute-start.19 = (bf16[704,384]{1,0:T(8,128)(2,1)}, bf16[704,384]{1,0:T(8,128)(2,1)S(1)}, u32[]{:S(2)}, u32[]{:S(2)}) collective-permute-start(bf16[704,384]{1,0:T(8,128)(2,1)} %release.5.refs_5_), channel_id=1, source_target_pairs={{0,8},{1,9},{2,10},{3,11},{4,12},{5,13},{6,14},{7,15},{8,0},{9,1},... | collective-permute-start | bytes 1622024 | tf_op jit(solution)/shard_map/ppermute | solution.py:725
  79.5 24.2 %collective-permute-start.20 = (bf16[704,384]{1,0:T(8,128)(2,1)}, bf16[704,384]{1,0:T(8,128)(2,1)S(1)}, u32[]{:S(2)}, u32[]{:S(2)}) collective-permute-start(bf16[704,384]{1,0:T(8,128)(2,1)} %release.5.refs_5_), channel_id=1, source_target_pairs={{0,16},{1,17},{2,18},{3,19},{4,20},{5,21},{6,22},{7,23},{8,24},{9,... | collective-permute-start | bytes 1622024 | tf_op jit(solution)/shard_map/ppermute | solution.py:725
  85.7 18.3 %collective-permute-start.22 = (bf16[704,384]{1,0:T(8,128)(2,1)}, bf16[704,384]{1,0:T(8,128)(2,1)}, u32[]{:S(2)}, u32[]{:S(2)}) collective-permute-start(bf16[704,384]{1,0:T(8,128)(2,1)} %release.4.refs_1_), channel_id=1, source_target_pairs={{0,4},{1,5},{2,6},{3,7},{4,0},{5,1},{6,2},{7,3},{8,12},{9,13},{10,... | collective-permute-start | bytes 1622024 | tf_op jit(solution)/shard_map/ppermute | solution.py:725
  97.1 55.1 %all-to-all-start = ((bf16[4,1632,128]{2,1,0:T(8,128)(2,1)}), bf16[4,1632,128]{2,1,0:T(8,128)(2,1)S(1)}, u32[]{:S(2)}, u32[]{:S(2)}) async-start(bf16[4,1632,128]{2,1,0:T(8,128)(2,1)} %stats.1.refs_0_), calls=%async_computation | async-start | bytes 3342336 | tf_op jit(solution)/shard_map/all_to_all | solution.py:820
  101.0 14.4 %collective-permute-start.25 = (bf16[704,384]{1,0:T(8,128)(2,1)}, bf16[704,384]{1,0:T(8,128)(2,1)S(1)}, u32[]{:S(2)}, u32[]{:S(2)}) collective-permute-start(bf16[704,384]{1,0:T(8,128)(2,1)} %release.5.refs_5_), channel_id=1, source_target_pairs={{0,4},{1,5},{2,6},{3,7},{4,0},{5,1},{6,2},{7,3},{8,12},{9,13},{10,... | collective-permute-start | bytes 1622024 | tf_op jit(solution)/shard_map/ppermute | solution.py:725
  101.1 15.0 %collective-permute-start.21 = (bf16[704,384]{1,0:T(8,128)(2,1)}, bf16[704,384]{1,0:T(8,128)(2,1)}, u32[]{:S(2)}, u32[]{:S(2)}) collective-permute-start(bf16[704,384]{1,0:T(8,128)(2,1)} %collective-permute-done.17.refs_1_.refs_2_), channel_id=1, source_target_pairs={{0,16},{1,17},{2,18},{3,19},{4,20},{5,21},{6,22},{7,23},{8,24},{9,... | collective-permute-start | bytes 1622024 | tf_op jit(solution)/shard_map/ppermute | solution.py:725
  103.3 12.8 %collective-permute-start.23 = (bf16[704,384]{1,0:T(8,128)(2,1)}, bf16[704,384]{1,0:T(8,128)(2,1)S(1)}, u32[]{:S(2)}, u32[]{:S(2)}) collective-permute-start(bf16[704,384]{1,0:T(8,128)(2,1)} %collective-permute-done.17.refs_1_.refs_2_), channel_id=1, source_target_pairs={{0,4},{1,5},{2,6},{3,7},{4,0},{5,1},{6,2},{7,3},{8,12},{9,13},{10,... | collective-permute-start | bytes 1622024 | tf_op jit(solution)/shard_map/ppermute | solution.py:725
  103.6 16.3 %collective-permute-start.24 = (bf16[704,384]{1,0:T(8,128)(2,1)}, bf16[704,384]{1,0:T(8,128)(2,1)}, u32[]{:S(2)}, u32[]{:S(2)}) collective-permute-start(bf16[704,384]{1,0:T(8,128)(2,1)} %collective-permute-done.18.refs_2_.refs_3_), channel_id=1, source_target_pairs={{0,4},{1,5},{2,6},{3,7},{4,0},{5,1},{6,2},{7,3},{8,12},{9,13},{10,... | collective-permute-start | bytes 1622024 | tf_op jit(solution)/shard_map/ppermute | solution.py:725
  103.9 15.8 %collective-permute-start.26 = (bf16[704,384]{1,0:T(8,128)(2,1)S(1)}, bf16[704,384]{1,0:T(8,128)(2,1)}, u32[]{:S(2)}, u32[]{:S(2)}) collective-permute-start(bf16[704,384]{1,0:T(8,128)(2,1)S(1)} %collective-permute-done.20.refs_3_.refs_7_), channel_id=1, source_target_pairs={{0,8},{1,9},{2,10},{3,11},{4,12},{5,13},{6,14},{7,15},{8,0},{9,1},... | collective-permute-start | bytes 1622024 | tf_op jit(solution)/shard_map/ppermute | solution.py:725
  115.4 16.3 %collective-permute-start.29 = (bf16[704,384]{1,0:T(8,128)(2,1)S(1)}, bf16[704,384]{1,0:T(8,128)(2,1)}, u32[]{:S(2)}, u32[]{:S(2)}) collective-permute-start(bf16[704,384]{1,0:T(8,128)(2,1)S(1)} %collective-permute-done.20.refs_3_.refs_7_), channel_id=1, source_target_pairs={{0,4},{1,5},{2,6},{3,7},{4,0},{5,1},{6,2},{7,3},{8,12},{9,13},{10,... | collective-permute-start | bytes 1622024 | tf_op jit(solution)/shard_map/ppermute | solution.py:725
  116.1 15.6 %collective-permute-start.28 = (bf16[704,384]{1,0:T(8,128)(2,1)S(1)}, bf16[704,384]{1,0:T(8,128)(2,1)}, u32[]{:S(2)}, u32[]{:S(2)}) collective-permute-start(bf16[704,384]{1,0:T(8,128)(2,1)S(1)} %collective-permute-done.19.refs_2_.refs_6_), channel_id=1, source_target_pairs={{0,4},{1,5},{2,6},{3,7},{4,0},{5,1},{6,2},{7,3},{8,12},{9,13},{10,... | collective-permute-start | bytes 1622024 | tf_op jit(solution)/shard_map/ppermute | solution.py:725
  117.0 14.7 %collective-permute-start.27 = (bf16[704,384]{1,0:T(8,128)(2,1)}, bf16[704,384]{1,0:T(8,128)(2,1)}, u32[]{:S(2)}, u32[]{:S(2)}) collective-permute-start(bf16[704,384]{1,0:T(8,128)(2,1)} %collective-permute-done.21.refs_4_), channel_id=1, source_target_pairs={{0,4},{1,5},{2,6},{3,7},{4,0},{5,1},{6,2},{7,3},{8,12},{9,13},{10,... | collective-permute-start | bytes 1622024 | tf_op jit(solution)/shard_map/ppermute | solution.py:725
  119.8 15.5 %collective-permute-start.31 = (bf16[704,384]{1,0:T(8,128)(2,1)}, bf16[704,384]{1,0:T(8,128)(2,1)S(1)}, u32[]{:S(2)}, u32[]{:S(2)}) collective-permute-start(bf16[704,384]{1,0:T(8,128)(2,1)} %collective-permute-done.26.refs_0_.refs_8_), channel_id=1, source_target_pairs={{0,4},{1,5},{2,6},{3,7},{4,0},{5,1},{6,2},{7,3},{8,12},{9,13},{10,... | collective-permute-start | bytes 1622024 | tf_op jit(solution)/shard_map/ppermute | solution.py:725
  120.0 15.3 %collective-permute-start.30 = (bf16[128,1024]{1,0:T(8,128)(2,1)S(1)}, bf16[128,1024]{1,0:T(8,128)(2,1)S(1)}, u32[]{:S(2)}, u32[]{:S(2)}) collective-permute-start(bf16[128,1024]{1,0:T(8,128)(2,1)S(1)} %get-tuple-element.49.refs_1_.refs_0_), channel_id=1, source_target_pairs={{0,1},{1,0},{2,3},{3,2},{4,5},{5,4},{6,7},{7,6},{8,9},{9,8},{10,11... | collective-permute-start | bytes 786440 | tf_op jit(solution)/shard_map/ppermute | solution.py:725
  134.7 10.9 %collective-permute-start.32 = (bf16[128,1024]{1,0:T(8,128)(2,1)S(1)}, bf16[128,1024]{1,0:T(8,128)(2,1)S(1)}, u32[]{:S(2)}, u32[]{:S(2)}) collective-permute-start(bf16[128,1024]{1,0:T(8,128)(2,1)S(1)} %get-tuple-element.50.refs_1_), channel_id=1, source_target_pairs={{0,1},{1,0},{2,3},{3,2},{4,5},{5,4},{6,7},{7,6},{8,9},{9,8},{10,11... | collective-permute-start | bytes 786440 | tf_op jit(solution)/shard_map/ppermute | solution.py:725
  142.0 13.6 %collective-permute-start.33 = (bf16[128,1024]{1,0:T(8,128)(2,1)S(1)}, bf16[128,1024]{1,0:T(8,128)(2,1)S(1)}, u32[]{:S(2)}, u32[]{:S(2)}) collective-permute-start(bf16[128,1024]{1,0:T(8,128)(2,1)S(1)} %get-tuple-element.54.refs_4_), channel_id=1, source_target_pairs={{0,1},{1,0},{2,3},{3,2},{4,5},{5,4},{6,7},{7,6},{8,9},{9,8},{10,11... | collective-permute-start | bytes 786440 | tf_op jit(solution)/shard_map/ppermute | solution.py:725
  (44 other events, 339.7 us)
Sparse Core Ops, SparseCore 0:
  10.9 75.3 all-gather.1
